TPU v7x, 512 devices: a whole 4x4x16 slice. The times are simulated.
512 devices in a mesh: tx: 16 (over y, x_hi, core), mp: 16 (over z), rep: 2 (over x_lo).
Axes of the slice: x: 4 (x_hi: 2, x_lo: 2; x = x_hi * 2 + x_lo), y: 4, z: 16, core: 2. Of those that a mesh axis runs over, the one named last changes fastest.
Arguments:
- jacobian: bfloat16 [16, 8192, 2048], P('tx', ('mp', 'rep')), may hold values from -0.44921875 to 0.44921875
- coupling: float32 [4, 16, 8192], P(None, 'tx', ('mp', 'rep')), may hold values from 0.2 to 2
- brick_left: int32 [16, 32, 24], P('tx', ('mp', 'rep')), may hold values from 0 to 7
- brick_right: int32 [16, 32, 24], P('tx', ('mp', 'rep')), may hold values from 0 to 7
- tile_target: int32 [16, 32, 24], P('tx', ('mp', 'rep')), may hold values from 0 to 127, as said below
Outputs:
- normal_tiles: float32 [128, 256, 256], P('mp', ('tx', 'rep'))
Inputs may be any that keep to these rules, and one draw needn't show every extreme that they name: Among the 24 entries of one row tile_target[t, b, :], no owner (entry // 8) occurs more than 2 times; in every row some owner occurs exactly 2 times, the same owner for all rows b of one t with the same remainder of b divided by the number of rep devices.
All inputs are finite; a program needn't handle non-finite values.
Results may differ from a plain program's by a relative error of at most 0.0039.
Values may be sent and summed in bfloat16 or wider, within the bound.
No kernel may reach another device: no remote copies, remote signals or barrier semaphores. Data moves between devices by JAX's collectives and lax.ppermute only.
A program may use at most 64 MiB of HBM per device.

v0:
```python
import jax
import jax.numpy as jnp
from jax import lax
from jax.sharding import PartitionSpec as P

BRICK = 256
FOOT_BRICKS = 8
STEPS = 4
LISTED = 6
TILES_DEV = 8


def shifted(block, axis, distance):
    devices = range(lax.axis_size(axis))
    route = [((i - distance) % len(devices), i) for i in devices]
    return lax.ppermute(block, axis, route)


def body(jacobian, coupling, brick_left, brick_right, tile_target):
    rows = jacobian.shape[1]
    own_bricks = jacobian[0].reshape(rows, FOOT_BRICKS, BRICK)
    left_ids = brick_left[0, 0].reshape(STEPS, LISTED)
    right_ids = brick_right[0, 0].reshape(STEPS, LISTED)
    rights = [jnp.take(own_bricks, right_ids[0], axis=1)]
    travelling = own_bricks
    for step in range(1, STEPS):
        travelling = shifted(travelling, "tx", -1)
        rights.append(jnp.take(travelling, right_ids[step], axis=1))
    partials = []
    for step in range(STEPS):
        weight = coupling[step, 0]
        left = (
            jnp.take(own_bricks, left_ids[step], axis=1).astype(jnp.float32) * weight[:, None, None]
        ).astype(jnp.bfloat16)
        product = jnp.einsum("rla,rlb->lab", left, rights[step], preferred_element_type=jnp.float32)
        partials.append(product.astype(jnp.bfloat16))
    partials = jnp.concatenate(partials, axis=0)
    targets = tile_target[0, 0]
    owners = lax.axis_size("mp")
    pairs = targets.shape[0]
    capacity = max(2, (4 * pairs + 3 * owners - 1) // (3 * owners))
    owner = targets // TILES_DEV
    local = targets % TILES_DEV
    order = jnp.arange(pairs)
    earlier = (owner[None, :] == owner[:, None]) & (order[None, :] < order[:, None])
    rank = jnp.sum(earlier.astype(jnp.int32), axis=1)
    dest = owner * capacity + rank
    slots = jnp.zeros((owners * capacity, BRICK, BRICK), jnp.bfloat16).at[dest].set(partials)
    labels = (
        jnp.full((owners * capacity,), -1.0, jnp.bfloat16).at[dest].set(local.astype(jnp.bfloat16))
    )
    got_tiles, got_labels = (
        lax.all_to_all(slots, "mp", split_axis=0, concat_axis=0, tiled=True),
        lax.all_to_all(labels, "mp", split_axis=0, concat_axis=0, tiled=True),
    )
    selector = (
        got_labels.astype(jnp.float32)[None, :] == jnp.arange(TILES_DEV, dtype=jnp.float32)[:, None]
    ).astype(jnp.bfloat16)
    owned = jnp.dot(
        selector,
        got_tiles.reshape(owners * capacity, BRICK * BRICK),
        preferred_element_type=jnp.float32,
    )
    owned = owned.reshape(TILES_DEV, BRICK, BRICK)
    return lax.psum_scatter(owned, ("tx", "rep"), scatter_dimension=1, tiled=True)


def solution(mesh):
    in_specs = (
        P("tx", ("mp", "rep"), None),
        P(None, "tx", ("mp", "rep")),
        P("tx", ("mp", "rep"), None),
        P("tx", ("mp", "rep"), None),
        P("tx", ("mp", "rep"), None),
    )
    out_specs = P("mp", ("tx", "rep"), None)
    return jax.shard_map(body, mesh=mesh, in_specs=in_specs, out_specs=out_specs, check_vma=False)
```

profile of v0, /device:TPU:32, one launch (start us, length us, event | category | flops | bytes accessed | tf_op | source)
XLA Modules:
  0.0 430.6 jit_solution(5908291566138440152)
XLA Ops:
  6.5 0.0 copy-start.6
  6.5 0.0 copy-start.3
  6.5 0.0 copy-start.4
  6.5 1.5 copy.41
  8.1 0.5 copy.42
  8.6 6.8 %collective-permute-start = (bf16[256,8,256]{2,0,1:T(8,128)(2,1)S(1)}, bf16[256,8,256]{2,0,1:T(8,128)(2,1)}, u32[]{:S(2)}, u32[]{:S(2)}) collective-permute-start(bf16[256,8,256]{2,0,1:T(8,128)(2,1)S(1)} %copy.42), channel_id=1, source_target_pairs={{32,0},{64,32},{96,64},{128,96},{160,128},{192,160},{224,192},{256... | collective-permute-start | bytes 3145736 | tf_op jit(solution)/shard_map/ppermute | solution.py:16
  15.4 0.0 copy-done.6
  15.5 0.2 convert_reduce_fusion
  15.7 0.7 scatter_custom_fusion
  16.4 0.7 all_to_all.12
  17.1 15.2 %all-to-all-start = ((bf16[16,2,1]{1,2,0:T(2,128)(2,1)}), bf16[16,2,1]{1,2,0:T(2,128)(2,1)S(1)}, u32[]{:S(2)}, u32[]{:S(2)}) async-start(bf16[16,2,1]{1,2,0:T(2,128)(2,1)} %all_to_all.12), calls=%async_computation | async-start | bytes 16384 | tf_op jit(solution)/shard_map/all_to_all | solution.py:54
  32.3 0.0 collective-permute-done
  32.3 3.0 collective-permute-start.1
  35.3 0.0 copy-done.3
  35.3 0.0 copy-done.4
  35.3 0.1 compare_and_fusion.6
  35.4 0.6 gather_fusion.6
  36.0 0.6 gather_fusion.4
  36.6 0.0 copy-start.5
  36.6 0.6 gather_fusion.2
  37.2 1.5 gather_fusion.1
  38.8 1.5 gather_fusion
  40.3 7.5 %collective-permute-done.1 = bf16[256,8,256]{2,0,1:T(8,128)(2,1)} collective-permute-done((bf16[256,8,256]{2,0,1:T(8,128)(2,1)}, bf16[256,8,256]{2,0,1:T(8,128)(2,1)}, u32[]{:S(2)}, u32[]{:S(2)}) %collective-permute-start.1) | collective-permute-done | bytes 1048608 | tf_op jit(solution)/shard_map/ppermute | solution.py:16
  47.9 7.4 %collective-permute-start.2 = (bf16[256,8,256]{2,0,1:T(8,128)(2,1)}, bf16[256,8,256]{2,0,1:T(8,128)(2,1)}, u32[]{:S(2)}, u32[]{:S(2)}) collective-permute-start(bf16[256,8,256]{2,0,1:T(8,128)(2,1)} %collective-permute-done.1), channel_id=1, source_target_pairs={{32,0},{64,32},{96,64},{128,96},{160,128},{192,160},{224,192},{256... | collective-permute-start | bytes 3145736 | tf_op jit(solution)/shard_map/ppermute | solution.py:16
  55.3 0.0 copy-done.5
  55.3 2.9 convolution_convert_fusion.3
  58.2 1.8 gather_fusion.3
  60.0 1.5 convolution_convert_fusion.2
  61.5 1.8 gather_fusion.5
  63.4 1.6 convolution_convert_fusion.1
  64.9 0.0 copy-start
  64.9 0.0 copy-start.1
  64.9 3.0 collective-permute-done.2
  67.9 1.8 gather_fusion.7
  69.7 0.0 copy-start.2
  69.7 0.6 convolution_convert_fusion
  70.4 0.0 copy-done
  70.4 0.0 copy-done.1
  70.4 0.5 copy-done.2
  70.9 1.9 pad_maximum_fusion
  72.7 2.5 broadcast_in_dim.14
  75.2 8.7 %scatter_fusion = bf16[32,256,256]{2,1,0:T(8,128)(2,1)} fusion(bf16[32,256,256]{2,1,0:T(8,128)(2,1)} %broadcast_in_dim.14, s32[24]{0:T(128)S(1)} %fusion.40, bf16[24,256,256]{2,1,0:T(8,128)(2,1)} %pad_maximum_fusion), kind=kCustom, calls=%fused_computation.9 | custom fusion | bytes 9437280 | tf_op jit(solution)/shard_map/scatter | solution.py:48
  83.9 0.0 all-to-all-done
  83.9 15.1 %all-to-all-start.1 = ((bf16[32,256,256]{2,1,0:T(8,128)(2,1)}), bf16[32,256,256]{2,1,0:T(8,128)(2,1)}, u32[]{:S(2)}, u32[]{:S(2)}) async-start(bf16[32,256,256]{2,1,0:T(8,128)(2,1)} %scatter_fusion), calls=%async_computation.1 | async-start | bytes 8388608 | tf_op jit(solution)/shard_map/all_to_all | solution.py:53
  99.0 0.0 reduce-scatter.2.cloned.1.call-start
  99.1 0.1 reshape.166
  99.2 177.1 %all-to-all-done.1 = bf16[32,256,256]{2,1,0:T(8,128)(2,1)} async-done(((bf16[32,256,256]{2,1,0:T(8,128)(2,1)}), bf16[32,256,256]{2,1,0:T(8,128)(2,1)}, u32[]{:S(2)}, u32[]{:S(2)}) %all-to-all-start.1) | async-done | bytes 4194336 | tf_op jit(solution)/shard_map/all_to_all | solution.py:53
  276.3 5.9 %fusion = f32[8,256,256]{2,0,1:T(8,128)} fusion(f32[32]{0:T(128)S(1)} %reshape.166, bf16[4,8,256,256]{3,2,1,0:T(8,128)(2,1)} %bitcast.29), kind=kOutput, calls=%fused_computation.10 | convolution fusion | flops 33554688 | bytes 6291584 | tf_op jit(solution)/shard_map/dot_general | solution.py:59
  282.2 0.0 reduce-scatter.2.cloned.1.call-update
  282.2 140.0 %reduce-scatter.2.cloned.1.call-done = f32[8,8,256]{2,0,1:T(8,128)} async-done(((f32[8,256,256]{2,0,1:T(8,128)}), f32[8,8,256]{2,0,1:T(8,128)}) %reduce-scatter.2.cloned.1.call-update) | async-done | bytes 65552 | tf_op jit(solution)/shard_map/reduce_scatter | solution.py:65
  422.2 1.5 copy.53
  (12 shorter events, 0.1 us)
Async XLA Ops:
  6.5 8.9 %copy-start.6 = (s32[1,1,24]{2,1,0:T(1,128)S(1)}, s32[1,1,24]{2,1,0:T(1,128)}, u32[]{:S(2)}) copy-start(s32[1,1,24]{2,1,0:T(1,128)} %param.11) | copy-start | bytes 292
  6.5 28.7 %copy-start.3 = (s32[1,1,24]{2,1,0:T(1,128)S(1)}, s32[1,1,24]{2,1,0:T(1,128)}, u32[]{:S(2)}) copy-start(s32[1,1,24]{2,1,0:T(1,128)} %param.10) | copy-start | bytes 292
  6.5 28.7 %copy-start.4 = (s32[1,1,24]{2,1,0:T(1,128)S(1)}, s32[1,1,24]{2,1,0:T(1,128)}, u32[]{:S(2)}) copy-start(s32[1,1,24]{2,1,0:T(1,128)} %param.9) | copy-start | bytes 292
  8.6 23.7 %collective-permute-start = (bf16[256,8,256]{2,0,1:T(8,128)(2,1)S(1)}, bf16[256,8,256]{2,0,1:T(8,128)(2,1)}, u32[]{:S(2)}, u32[]{:S(2)}) collective-permute-start(bf16[256,8,256]{2,0,1:T(8,128)(2,1)S(1)} %copy.42), channel_id=1, source_target_pairs={{32,0},{64,32},{96,64},{128,96},{160,128},{192,160},{224,192},{256... | collective-permute-start | bytes 3145736 | tf_op jit(solution)/shard_map/ppermute | solution.py:16
  17.1 66.8 %all-to-all-start = ((bf16[16,2,1]{1,2,0:T(2,128)(2,1)}), bf16[16,2,1]{1,2,0:T(2,128)(2,1)S(1)}, u32[]{:S(2)}, u32[]{:S(2)}) async-start(bf16[16,2,1]{1,2,0:T(2,128)(2,1)} %all_to_all.12), calls=%async_computation | async-start | bytes 16384 | tf_op jit(solution)/shard_map/all_to_all | solution.py:54
  32.3 15.6 %collective-permute-start.1 = (bf16[256,8,256]{2,0,1:T(8,128)(2,1)}, bf16[256,8,256]{2,0,1:T(8,128)(2,1)}, u32[]{:S(2)}, u32[]{:S(2)}) collective-permute-start(bf16[256,8,256]{2,0,1:T(8,128)(2,1)} %collective-permute-done), channel_id=1, source_target_pairs={{32,0},{64,32},{96,64},{128,96},{160,128},{192,160},{224,192},{256... | collective-permute-start | bytes 3145736 | tf_op jit(solution)/shard_map/ppermute | solution.py:16
  36.6 18.7 %copy-start.5 = (f32[4,1,256]{2,1,0:T(1,128)S(1)}, f32[4,1,256]{2,1,0:T(1,128)}, u32[]{:S(2)}) copy-start(f32[4,1,256]{2,1,0:T(1,128)} %param.8) | copy-start | bytes 12292
  47.9 20.0 %collective-permute-start.2 = (bf16[256,8,256]{2,0,1:T(8,128)(2,1)}, bf16[256,8,256]{2,0,1:T(8,128)(2,1)}, u32[]{:S(2)}, u32[]{:S(2)}) collective-permute-start(bf16[256,8,256]{2,0,1:T(8,128)(2,1)} %collective-permute-done.1), channel_id=1, source_target_pairs={{32,0},{64,32},{96,64},{128,96},{160,128},{192,160},{224,192},{256... | collective-permute-start | bytes 3145736 | tf_op jit(solution)/shard_map/ppermute | solution.py:16
  64.9 5.4 %copy-start = (bf16[6,256,256]{2,1,0:T(8,128)(2,1)S(1)}, bf16[6,256,256]{2,1,0:T(8,128)(2,1)}, u32[]{:S(2)}) copy-start(bf16[6,256,256]{2,1,0:T(8,128)(2,1)} %convolution_convert_fusion.3) | copy-start | bytes 2359300
  64.9 5.4 %copy-start.1 = (bf16[6,256,256]{2,1,0:T(8,128)(2,1)S(1)}, bf16[6,256,256]{2,1,0:T(8,128)(2,1)}, u32[]{:S(2)}) copy-start(bf16[6,256,256]{2,1,0:T(8,128)(2,1)} %convolution_convert_fusion.2) | copy-start | bytes 2359300
  69.7 1.1 copy-start.2
  83.9 192.4 %all-to-all-start.1 = ((bf16[32,256,256]{2,1,0:T(8,128)(2,1)}), bf16[32,256,256]{2,1,0:T(8,128)(2,1)}, u32[]{:S(2)}, u32[]{:S(2)}) async-start(bf16[32,256,256]{2,1,0:T(8,128)(2,1)} %scatter_fusion), calls=%async_computation.1 | async-start | bytes 8388608 | tf_op jit(solution)/shard_map/all_to_all | solution.py:53
  99.0 323.2 %reduce-scatter.2.cloned.1.call-start = ((), (), s32[]{:S(2)}) async-start(), calls=%async_computation.3 | async-start | bytes 2162688 | tf_op jit(solution)/shard_map/reduce_scatter | solution.py:65
Sparse Core Ops, SparseCore 0:
  282.3 139.8 reduce-scatter.1
where the time goes:
time: 431 us
  waiting for transfers between devices  328 us (76%)
  starting transfers between devices  47.5 us (11%)
  local copies, waits for them, and re-layouts  27 us (6%)
  between operations  13.6 us (3%)
  matrix products  12.4 us (3%)
    all_to_all x1, waiting for transfers between devices, body(): lax.all_to_all(slots, 'mp', split_axis=0, concat_axis=0, tiled=True)  177 us
    reduce_scatter x1, waiting for transfers between devices, body(): lax.psum_scatter(owned, ('tx', 'rep'), scatter_dimension=1, tiled=True)  140 us
    ppermute x3, starting transfers between devices, shifted(): return lax.ppermute(block, axis, route)  17.2 us
    all_to_all x1, starting transfers between devices, body(): lax.all_to_all(labels, 'mp', split_axis=0, concat_axis=0, tiled=True)  15.2 us
    all_to_all x1, starting transfers between devices, body(): lax.all_to_all(slots, 'mp', split_axis=0, concat_axis=0, tiled=True)  15.1 us
    ppermute x3, waiting for transfers between devices, shifted(): return lax.ppermute(block, axis, route)  10.5 us
    scatter x1, local copies, waits for them, and re-layouts, body(): jnp.zeros((owners * capacity, BRICK, BRICK), jnp.bfloat16).at[dest]  8.71 us
  transfers between devices with their start and end apart: 6, of which 4 were waited for; matrix products, arithmetic and copies ran while one was open for 7% of the time, Pallas kernels for 0%

commit v1 on v0

v1 whole, which is shorter than its diff:
```python
import jax
import jax.numpy as jnp
from jax import lax
from jax.experimental import pallas as pl
from jax.experimental.pallas import tpu as pltpu
from jax.sharding import PartitionSpec as P

BRICK = 256
STEPS = 4
LISTED = 6
PAIRS = STEPS * LISTED
TILES_DEV = 8
PLANE = ("tx", "rep")
HELD = ((0, 0), (0, 1), (1, 2), (0, 2))


def fetched(block, distance):
    devices = lax.axis_size("tx")
    route = [((i + distance) % devices, i) for i in range(devices)]
    return lax.ppermute(block, "tx", route)


def exchanged(block, axis):
    return lax.all_to_all(block, axis, split_axis=0, concat_axis=0, tiled=True)


def product_kernel(left_ids, right_ids, weight, own, second, fourth, out):
    blocks = (own, second, fourth)
    parts, rows, _ = out.shape
    slab = rows // PAIRS

    def brick(block, index):
        return block[:, pl.ds(pl.multiple_of(index * BRICK, BRICK), BRICK)]

    for first in range(0, PAIRS, 2):
        step = first // LISTED
        left_block, right_block = (blocks[i] for i in HELD[step])
        pair = []
        for entry in (first, first + 1):
            left = brick(left_block, left_ids[entry]).astype(jnp.float32) * weight[:, step : step + 1]
            tile = lax.dot_general(
                left.astype(jnp.bfloat16),
                brick(right_block, right_ids[entry]),
                (((0,), (0,)), ((), ())),
                preferred_element_type=jnp.float32,
            )
            pair.append(tile.reshape(parts, slab, BRICK))
        out[:, first * slab : (first + 2) * slab, :] = jnp.concatenate(pair, axis=1).astype(jnp.bfloat16)


def sum_kernel(labels, got, out, total):
    parts, rows, _ = got.shape
    slab = rows // PAIRS
    total[...] = jnp.zeros_like(total)

    def one_part(part, carry):
        for first in range(0, PAIRS, 2):
            both = got[part, first * slab : (first + 2) * slab, :].astype(jnp.float32)
            for half in range(2):
                tile = labels[part * PAIRS + first + half]
                total[tile] += both[half * slab : (half + 1) * slab]
        return carry

    lax.fori_loop(0, parts, one_part, 0)
    out[...] = total[...].reshape(out.shape).astype(out.dtype)


def body(jacobian, coupling, brick_left, brick_right, tile_target):
    own = jacobian[0]
    rows = own.shape[0]
    weight = coupling[:, 0]
    left_ids, right_ids = brick_left[0, 0], brick_right[0, 0]
    parts = lax.axis_size("tx") * lax.axis_size("rep")
    owners = lax.axis_size("mp")
    slab = BRICK // parts
    tiles = owners * TILES_DEV

    second = fetched(own, 1)
    fourth = fetched(own, 3)
    middle = slice(2 * LISTED, 3 * LISTED)
    small = jnp.concatenate(
        [weight[2], left_ids[middle].astype(jnp.float32), right_ids[middle].astype(jnp.float32)]
    )
    small = fetched(small, 1)
    weight = weight.at[2].set(small[:rows])
    left_ids = left_ids.at[middle].set(small[rows : rows + LISTED].astype(jnp.int32))
    right_ids = right_ids.at[middle].set(small[rows + LISTED :].astype(jnp.int32))

    labels = exchanged(jnp.broadcast_to(tile_target[0], (parts, PAIRS)), PLANE)
    labels = labels.reshape(lax.axis_size("tx"), lax.axis_size("rep"), STEPS, LISTED)
    labels = labels.at[:, :, 2].set(jnp.roll(labels[:, :, 2], -1, axis=0)).reshape(-1)

    smem = pl.BlockSpec(memory_space=pltpu.SMEM)
    vmem = pl.BlockSpec(memory_space=pltpu.VMEM)
    partials = pl.pallas_call(
        product_kernel,
        out_shape=jax.ShapeDtypeStruct((parts, PAIRS * slab, BRICK), jnp.bfloat16),
        in_specs=[smem, smem, vmem, vmem, vmem, vmem],
        out_specs=vmem,
        compiler_params=pltpu.CompilerParams(vmem_limit_bytes=32 * 2**20),
        name="products",
    )(left_ids, right_ids, weight.T, own, second, fourth)
    got = exchanged(partials, PLANE)
    sums = pl.pallas_call(
        sum_kernel,
        out_shape=jax.ShapeDtypeStruct((tiles * slab, BRICK), jnp.bfloat16),
        in_specs=[smem, vmem],
        out_specs=vmem,
        scratch_shapes=[pltpu.VMEM((tiles, slab, BRICK), jnp.float32)],
        compiler_params=pltpu.CompilerParams(vmem_limit_bytes=32 * 2**20),
        name="sums",
    )(labels, got)
    sums = exchanged(sums, "mp").reshape(owners, TILES_DEV, slab, BRICK)
    return jnp.sum(sums.astype(jnp.float32), axis=0)


def solution(mesh):
    in_specs = (
        P("tx", ("mp", "rep"), None),
        P(None, "tx", ("mp", "rep")),
        P("tx", ("mp", "rep"), None),
        P("tx", ("mp", "rep"), None),
        P("tx", ("mp", "rep"), None),
    )
    out_specs = P("mp", ("tx", "rep"), None)
    return jax.shard_map(body, mesh=mesh, in_specs=in_specs, out_specs=out_specs, check_vma=False)
```

time: 431 us -> 144 us (0.33)
  the two profiles are of different devices: /device:TPU:32 before, /device:TPU:3 now
where the time goes in v1:
time: 144 us; the launch traced here: 143 us
  waiting for transfers between devices  46.9 us (33%)
  blocking collectives  42.8 us (30%)
  starting transfers between devices  38.1 us (26%)
  local copies, waits for them, and re-layouts  8.56 us (6%)
  Pallas kernels  5.3 us (4%)
  other arithmetic  1.7 us (1%)
    all_to_all x1, blocking collectives, exchanged(): return lax.all_to_all(block, axis, split_axis=0, concat_axis=0, tiled=True)  42.8 us
    all_to_all x2, waiting for transfers between devices, exchanged(): return lax.all_to_all(block, axis, split_axis=0, concat_axis=0, tiled=True)  38.9 us
    all_to_all x2, starting transfers between devices, exchanged(): return lax.all_to_all(block, axis, split_axis=0, concat_axis=0, tiled=True)  26.6 us
    ppermute x3, starting transfers between devices, fetched(): return lax.ppermute(block, 'tx', route)  11.4 us
    ppermute x3, waiting for transfers between devices, fetched(): return lax.ppermute(block, 'tx', route)  8.01 us
    unnamed x7, local copies, waits for them, and re-layouts  5 us
  transfers between devices with their start and end apart: 5, of which 3 were waited for; matrix products, arithmetic and copies ran while one was open for 4% of the time, Pallas kernels for 2%

profile of v1, /device:TPU:3, one launch (start us, length us, event | category | flops | bytes accessed | tf_op | source)
XLA Modules:
  0.0 143.5 jit_solution(1853274153035668678)
XLA Ops:
  0.0 0.7 copy.26
  0.7 0.7 copy.27
  1.3 2.6 %collective-permute-start.1 = (bf16[256,2048]{1,0:T(8,128)(2,1)}, bf16[256,2048]{1,0:T(8,128)(2,1)S(1)}, u32[]{:S(2)}, u32[]{:S(2)}) collective-permute-start(bf16[256,2048]{1,0:T(8,128)(2,1)} %bitcast.20), channel_id=1, source_target_pairs={{32,0},{64,32},{96,64},{128,96},{160,128},{192,160},{224,192},{256... | collective-permute-start | bytes 3145736 | tf_op jit(solution)/shard_map/ppermute | solution.py:20
  3.9 6.9 %collective-permute-start.2 = (bf16[256,2048]{1,0:T(8,128)(2,1)}, bf16[256,2048]{1,0:T(8,128)(2,1)S(1)}, u32[]{:S(2)}, u32[]{:S(2)}) collective-permute-start(bf16[256,2048]{1,0:T(8,128)(2,1)} %bitcast.21), channel_id=1, source_target_pairs={{96,0},{128,32},{160,64},{192,96},{224,128},{256,160},{288,192},{3... | collective-permute-start | bytes 3145736 | tf_op jit(solution)/shard_map/ppermute | solution.py:20
  10.8 0.7 slice.106
  11.5 0.1 convert_bitcast_fusion
  11.6 0.1 pad_maximum_fusion
  11.7 1.9 %collective-permute-start = (f32[268]{0:T(512)S(1)}, f32[268]{0:T(512)S(1)}, u32[]{:S(2)}, u32[]{:S(2)}) collective-permute-start(f32[268]{0:T(512)S(1)} %pad_maximum_fusion), channel_id=1, source_target_pairs={{32,0},{64,32},{96,64},{128,96},{160,128},{192,160},{224,192},{256... | collective-permute-start | bytes 3224 | tf_op jit(solution)/shard_map/ppermute | solution.py:20
  13.6 1.3 broadcast_in_dim.2
  14.9 7.0 %all-to-all-start = ((s32[32,1,24]{2,1,0:T(1,128)}), s32[32,1,24]{2,1,0:T(1,128)S(1)}, u32[]{:S(2)}, u32[]{:S(2)}) async-start(s32[32,1,24]{2,1,0:T(1,128)} %broadcast_in_dim.2), calls=%async_computation | async-start | bytes 32768 | tf_op jit(solution)/shard_map/all_to_all | solution.py:24
  21.8 0.8 copy.17
  22.7 2.1 %collective-permute-done = f32[268]{0:T(512)S(1)} collective-permute-done((f32[268]{0:T(512)S(1)}, f32[268]{0:T(512)S(1)}, u32[]{:S(2)}, u32[]{:S(2)}) %collective-permute-start) | collective-permute-done | bytes 1104 | tf_op jit(solution)/shard_map/ppermute | solution.py:20
  24.7 0.1 constant_dynamic-update-slice_fusion
  24.9 0.1 copy.18
  25.0 0.6 scatter.19
  25.6 0.0 collective-permute-done.1.second
  25.6 5.9 %collective-permute-done.2.fourth = bf16[256,2048]{1,0:T(8,128)(2,1)S(1)} collective-permute-done((bf16[256,2048]{1,0:T(8,128)(2,1)}, bf16[256,2048]{1,0:T(8,128)(2,1)S(1)}, u32[]{:S(2)}, u32[]{:S(2)}) %collective-permute-start.2) | collective-permute-done | bytes 1048608 | tf_op jit(solution)/shard_map/ppermute | solution.py:20
  31.6 0.0 copy-start.1
  31.6 1.2 copy-done.1
  32.8 2.6 %products.1 = bf16[32,192,256]{2,1,0:T(8,128)(2,1)S(1)} custom-call(s32[24]{0:T(128)S(1)} %get-tuple-element.54.left_ids, s32[24]{0:T(128)S(1)} %get-tuple-element.53.right_ids, f32[256,4]{1,0:T(8,128)S(1)} %bitcast.24, bf16[256,2048]{1,0:T(8,128)(2,1)S(1)} %bitcast.22, bf16[256,2048]{1,0:T(8,128)(2,1)S(1)} %collective-permute-done.1.second, ...), custom_call_target="tpu_custom_call" | custom-call | tf_op jit(solution)/shard_map/products/pallas_call | solution.py:95
  35.4 0.0 copy-start
  35.4 1.6 %copy-done = bf16[32,192,256]{2,1,0:T(8,128)(2,1)} copy-done((bf16[32,192,256]{2,1,0:T(8,128)(2,1)}, bf16[32,192,256]{2,1,0:T(8,128)(2,1)S(1)}, u32[]{:S(2)}) %copy-start) | copy-done | bytes 3145752
  37.1 0.0 all-to-all-done
  37.1 19.7 %all-to-all-start.1 = ((bf16[32,192,256]{2,1,0:T(8,128)(2,1)}), bf16[32,192,256]{2,1,0:T(8,128)(2,1)S(1)}, u32[]{:S(2)}, u32[]{:S(2)}) async-start(bf16[32,192,256]{2,1,0:T(8,128)(2,1)} %copy-done), calls=%async_computation.1 | async-start | bytes 6291456 | tf_op jit(solution)/shard_map/all_to_all | solution.py:24
  56.8 0.5 broadcast.59
  57.3 0.7 reduce.12
  58.0 0.1 reshape.129
  58.1 0.1 scatter.14
  58.2 0.1 reshape.131.labels
  58.4 38.9 %all-to-all-done.1.got = bf16[32,192,256]{2,1,0:T(8,128)(2,1)S(1)} async-done(((bf16[32,192,256]{2,1,0:T(8,128)(2,1)}), bf16[32,192,256]{2,1,0:T(8,128)(2,1)S(1)}, u32[]{:S(2)}, u32[]{:S(2)}) %all-to-all-start.1) | async-done | bytes 3145760 | tf_op jit(solution)/shard_map/all_to_all | solution.py:24
  97.3 2.7 %sums.1 = bf16[1024,256]{1,0:T(8,128)(2,1)S(1)} custom-call(s32[768]{0:T(1024)S(1)} %reshape.131.labels, bf16[32,192,256]{2,1,0:T(8,128)(2,1)S(1)} %all-to-all-done.1.got), custom_call_target="tpu_custom_call" | custom-call | tf_op jit(solution)/shard_map/sums/pallas_call | solution.py:104
  100.0 42.8 %all_to_all.20 = bf16[16,64,256]{2,1,0:T(8,128)(2,1)S(1)} all-to-all(bf16[16,64,256]{2,1,0:T(8,128)(2,1)S(1)} %bitcast.19), channel_id=1, replica_groups=mesh['tx'=16,'mp'=16,'rep'=2] {'mp'}, dimensions={0} | all-to-all | bytes 1048576 | tf_op jit(solution)/shard_map/all_to_all | solution.py:24
  142.8 0.7 convert_reduce_fusion
  (4 shorter events, 0.0 us)
Async XLA Ops:
  1.3 24.3 %collective-permute-start.1 = (bf16[256,2048]{1,0:T(8,128)(2,1)}, bf16[256,2048]{1,0:T(8,128)(2,1)S(1)}, u32[]{:S(2)}, u32[]{:S(2)}) collective-permute-start(bf16[256,2048]{1,0:T(8,128)(2,1)} %bitcast.20), channel_id=1, source_target_pairs={{32,0},{64,32},{96,64},{128,96},{160,128},{192,160},{224,192},{256... | collective-permute-start | bytes 3145736 | tf_op jit(solution)/shard_map/ppermute | solution.py:20
  3.9 27.7 %collective-permute-start.2 = (bf16[256,2048]{1,0:T(8,128)(2,1)}, bf16[256,2048]{1,0:T(8,128)(2,1)S(1)}, u32[]{:S(2)}, u32[]{:S(2)}) collective-permute-start(bf16[256,2048]{1,0:T(8,128)(2,1)} %bitcast.21), channel_id=1, source_target_pairs={{96,0},{128,32},{160,64},{192,96},{224,128},{256,160},{288,192},{3... | collective-permute-start | bytes 3145736 | tf_op jit(solution)/shard_map/ppermute | solution.py:20
  11.7 13.1 %collective-permute-start = (f32[268]{0:T(512)S(1)}, f32[268]{0:T(512)S(1)}, u32[]{:S(2)}, u32[]{:S(2)}) collective-permute-start(f32[268]{0:T(512)S(1)} %pad_maximum_fusion), channel_id=1, source_target_pairs={{32,0},{64,32},{96,64},{128,96},{160,128},{192,160},{224,192},{256... | collective-permute-start | bytes 3224 | tf_op jit(solution)/shard_map/ppermute | solution.py:20
  14.9 22.2 %all-to-all-start = ((s32[32,1,24]{2,1,0:T(1,128)}), s32[32,1,24]{2,1,0:T(1,128)S(1)}, u32[]{:S(2)}, u32[]{:S(2)}) async-start(s32[32,1,24]{2,1,0:T(1,128)} %broadcast_in_dim.2), calls=%async_computation | async-start | bytes 32768 | tf_op jit(solution)/shard_map/all_to_all | solution.py:24
  31.6 1.2 copy-start.1
  35.4 1.7 %copy-start = (bf16[32,192,256]{2,1,0:T(8,128)(2,1)}, bf16[32,192,256]{2,1,0:T(8,128)(2,1)S(1)}, u32[]{:S(2)}) copy-start(bf16[32,192,256]{2,1,0:T(8,128)(2,1)S(1)} %products.1) | copy-start | bytes 9437188
  37.1 60.2 %all-to-all-start.1 = ((bf16[32,192,256]{2,1,0:T(8,128)(2,1)}), bf16[32,192,256]{2,1,0:T(8,128)(2,1)S(1)}, u32[]{:S(2)}, u32[]{:S(2)}) async-start(bf16[32,192,256]{2,1,0:T(8,128)(2,1)} %copy-done), calls=%async_computation.1 | async-start | bytes 6291456 | tf_op jit(solution)/shard_map/all_to_all | solution.py:24

commit v2 on v1

v2 whole, which is shorter than its diff:
```python
import functools

import jax
import jax.numpy as jnp
from jax import lax
from jax.experimental import pallas as pl
from jax.experimental.pallas import tpu as pltpu
from jax.sharding import Mesh, PartitionSpec as P

BRICK = 256
STEPS = 4
LISTED = 6
PAIRS = STEPS * LISTED
TILES_DEV = 8
HALVES = 2
GROUP = ("mp_lo", "tx", "rep")
OWNERS = ("mp_hi", "mp_lo")


def exchanged(block, axis):
    return lax.all_to_all(block, axis, split_axis=0, concat_axis=0, tiled=True)


def routes(devices):
    everyone = range(devices)
    swap = [(i ^ 1, i) for i in everyone]
    near = [((i + (1 if i % 2 else 3)) % devices, i) for i in everyone]
    far = [((i + (3 if i % 4 == 1 else -4)) % devices, i) for i in everyone if i % 2]
    return swap, near, far


def product_kernel(chosen, left_ids, right_ids, weight, own, swapped, near, far, out, held, sems):
    copies = [
        pltpu.make_async_copy(block, held.at[i], sems.at[i])
        for i, block in enumerate((own, swapped, near, far))
    ]
    for copy in copies:
        copy.start()
    parts, rows, _ = out.shape
    half = parts // HALVES
    slab = rows // PAIRS
    width = BRICK // HALVES

    def brick(block, index):
        return held[block, :, pl.ds(pl.multiple_of(index * BRICK, BRICK), BRICK)]

    for first in range(0, PAIRS, 2):
        step = first // LISTED
        if first == 0:
            copies[0].wait()
        elif first == LISTED:
            for copy in copies[1:]:
                copy.wait()
        left_block = 0 if step == 0 else chosen[step]
        right_block = 0 if step == 0 else chosen[STEPS + step]
        pair = []
        for entry in (first, first + 1):
            left = brick(left_block, left_ids[entry]).astype(jnp.float32) * weight[:, step : step + 1]
            tile = lax.dot_general(
                left.astype(jnp.bfloat16),
                brick(right_block, right_ids[entry]),
                (((0,), (0,)), ((), ())),
                preferred_element_type=jnp.float32,
            )
            pair.append(tile.reshape(half, slab, BRICK))
        both = jnp.concatenate(pair, axis=1).astype(jnp.bfloat16)
        for side in range(HALVES):
            out[side * half : (side + 1) * half, first * slab : (first + 2) * slab, :] = both[
                :, :, side * width : (side + 1) * width
            ]


def sum_kernel(subsets, labels, got, out, total):
    parts, rows, _ = got.shape
    slab = rows // PAIRS
    plane = parts // HALVES
    total[...] = jnp.zeros_like(total)

    def one_part(part, carry):
        place = part // subsets % 4
        swapped = part + jnp.where(place % 2 == 0, subsets, -subsets)
        earlier = jnp.where(part % plane < 4 * subsets, part + plane - 4 * subsets, part - 4 * subsets)
        listed = (part, part, swapped, jnp.where(place == 3, earlier, part))
        for first in range(0, PAIRS, 2):
            start = listed[first // LISTED] * PAIRS + first
            both = got[part, first * slab : (first + 2) * slab, :].astype(jnp.float32)
            for side in range(2):
                tile = labels[start + side]
                total[tile] += both[side * slab : (side + 1) * slab]
        return carry

    lax.fori_loop(0, parts, one_part, 0)
    out[...] = total[...].reshape(out.shape).astype(out.dtype)


def body(jacobian, coupling, brick_left, brick_right, tile_target):
    own = jacobian[0]
    rows = own.shape[0]
    devices = lax.axis_size("tx")
    swap, near, far = routes(devices)
    place = lax.axis_index("tx") % 4
    parts = devices * lax.axis_size("rep") * HALVES
    owners = lax.axis_size("mp_hi") * lax.axis_size("mp_lo")
    slab = BRICK // (parts // HALVES)
    width = BRICK // HALVES
    tiles = owners * TILES_DEV

    near_block = lax.ppermute(own, "tx", near)
    far_block = lax.ppermute(own, "tx", far)
    swapped_block = lax.ppermute(own, "tx", swap)

    weight = coupling[:, 0]
    ids = jnp.concatenate([brick_left[0, 0], brick_right[0, 0]]).reshape(2, STEPS, LISTED)
    meta = jnp.concatenate([weight[2:], ids[:, 2:].transpose(1, 0, 2).reshape(2, -1).astype(jnp.float32)], axis=1)
    of_swapped = lax.ppermute(meta[0], "tx", swap)
    of_far = jnp.where(place == 3, lax.ppermute(meta[1], "tx", far), meta[1])
    meta = jnp.stack([of_swapped, of_far])
    weight = jnp.concatenate([weight[:2], meta[:, :rows]], axis=0)
    ids = jnp.concatenate(
        [ids[:, :2], meta[:, rows:].astype(jnp.int32).reshape(2, 2, LISTED).transpose(1, 0, 2)], axis=1
    )
    odd = place % 2
    chosen = [0, 0, 1, jnp.where(place == 3, 3, 0)] + [
        0,
        1 + odd,
        2,
        jnp.where(odd == 0, 2, jnp.where(place == 1, 3, 1)),
    ]
    chosen = jnp.stack([jnp.asarray(c, jnp.int32) for c in chosen])

    labels = exchanged(jnp.broadcast_to(tile_target[0], (parts, PAIRS)), GROUP)
    labels = labels.reshape(-1)

    smem = pl.BlockSpec(memory_space=pltpu.SMEM)
    vmem = pl.BlockSpec(memory_space=pltpu.VMEM)
    hbm = pl.BlockSpec(memory_space=pl.ANY)
    partials = pl.pallas_call(
        product_kernel,
        out_shape=jax.ShapeDtypeStruct((parts, PAIRS * slab, width), jnp.bfloat16),
        in_specs=[smem, smem, smem, vmem, hbm, hbm, hbm, hbm],
        out_specs=vmem,
        scratch_shapes=[pltpu.VMEM((4,) + own.shape, own.dtype), pltpu.SemaphoreType.DMA((4,))],
        compiler_params=pltpu.CompilerParams(vmem_limit_bytes=32 * 2**20),
        name="products",
    )(chosen, ids[0].reshape(-1), ids[1].reshape(-1), weight.T, own, swapped_block, near_block, far_block)
    got = exchanged(partials, GROUP)
    sums = pl.pallas_call(
        functools.partial(sum_kernel, lax.axis_size("rep")),
        out_shape=jax.ShapeDtypeStruct((tiles * slab, width), jnp.bfloat16),
        in_specs=[smem, vmem],
        out_specs=vmem,
        scratch_shapes=[pltpu.VMEM((tiles, slab, width), jnp.float32)],
        compiler_params=pltpu.CompilerParams(vmem_limit_bytes=32 * 2**20),
        name="sums",
    )(labels, got)
    sums = exchanged(sums, OWNERS).reshape(owners // HALVES, HALVES, TILES_DEV, slab, width)
    sums = jnp.sum(sums.astype(jnp.float32), axis=0)
    return jnp.concatenate([sums[side] for side in range(HALVES)], axis=-1)


def solution(mesh):
    shape = (mesh.shape["tx"], mesh.shape["mp"] // HALVES, HALVES, mesh.shape["rep"])
    mesh = Mesh(mesh.devices.reshape(shape), ("tx", "mp_hi", "mp_lo", "rep"))
    data = ("mp_hi", "mp_lo", "rep")
    in_specs = (
        P("tx", data, None),
        P(None, "tx", data),
        P("tx", data, None),
        P("tx", data, None),
        P("tx", data, None),
    )
    out_specs = P(OWNERS, ("tx", "rep"), None)
    return jax.shard_map(body, mesh=mesh, in_specs=in_specs, out_specs=out_specs, check_vma=False)
```

time: 144 us -> 128 us (0.89)
  the two profiles are of different devices: /device:TPU:3 before, /device:TPU:32 now
where the time goes in v2:
time: 128 us; the launch traced here: 127 us
  waiting for transfers between devices  41.6 us (32%)
  starting transfers between devices  33.2 us (26%)
  blocking collectives  32.9 us (26%)
  Pallas kernels  9.19 us (7%)
  local copies, waits for them, and re-layouts  6.21 us (5%)
  other arithmetic  3.8 us (3%)
    all_to_all x2, waiting for transfers between devices, exchanged(): return lax.all_to_all(block, axis, split_axis=0, concat_axis=0, tiled=True)  38.8 us
    all_to_all x1, blocking collectives, exchanged(): return lax.all_to_all(block, axis, split_axis=0, concat_axis=0, tiled=True)  32.9 us
    all_to_all x2, starting transfers between devices, exchanged(): return lax.all_to_all(block, axis, split_axis=0, concat_axis=0, tiled=True)  18.2 us
    ppermute x1, starting transfers between devices, body(): near_block = lax.ppermute(own, 'tx', near)  7.49 us
    pallas_call x1, Pallas kernels, body(): pl.pallas_call(functools.partial(sum_kernel, lax.axis_size('rep')), out_s...  5.99 us
    pallas_call x1, Pallas kernels, body(): pl.pallas_call(product_kernel, out_shape=jax.ShapeDtypeStruct((parts, PAI...  3.21 us
    unnamed x7, local copies, waits for them, and re-layouts  2.9 us
    ppermute x1, waiting for transfers between devices, body(): near_block = lax.ppermute(own, 'tx', near)  2.8 us
  transfers between devices with their start and end apart: 7, of which 2 were waited for; matrix products, arithmetic and copies ran while one was open for 5% of the time, Pallas kernels for 3%

profile of v2, /device:TPU:32, one launch (start us, length us, event | category | flops | bytes accessed | tf_op | source)
XLA Modules:
  0.0 127.0 jit_solution(18178234356004154679)
XLA Ops:
  0.0 1.9 %collective-permute-start.2 = (bf16[256,2048]{1,0:T(8,128)(2,1)}, bf16[256,2048]{1,0:T(8,128)(2,1)S(1)}, u32[]{:S(2)}, u32[]{:S(2)}) collective-permute-start(bf16[256,2048]{1,0:T(8,128)(2,1)} %bitcast.24), channel_id=1, source_target_pairs={{32,0},{0,32},{96,64},{64,96},{160,128},{128,160},{224,192},{192,2... | collective-permute-start | bytes 3145736 | tf_op jit(solution)/shard_map/ppermute | solution.py:110
  1.9 7.5 %collective-permute-start.3 = (bf16[256,2048]{1,0:T(8,128)(2,1)}, bf16[256,2048]{1,0:T(8,128)(2,1)S(1)}, u32[]{:S(2)}, u32[]{:S(2)}) collective-permute-start(bf16[256,2048]{1,0:T(8,128)(2,1)} %bitcast.25), channel_id=1, source_target_pairs={{96,0},{64,32},{160,64},{128,96},{224,128},{192,160},{288,192},{25... | collective-permute-start | bytes 3145736 | tf_op jit(solution)/shard_map/ppermute | solution.py:108
  9.4 2.3 %collective-permute-start.4 = (bf16[256,2048]{1,0:T(8,128)(2,1)}, bf16[256,2048]{1,0:T(8,128)(2,1)S(1)}, u32[]{:S(2)}, u32[]{:S(2)}) collective-permute-start(bf16[256,2048]{1,0:T(8,128)(2,1)} %bitcast.26), channel_id=1, source_target_pairs={{128,32},{480,96},{256,160},{96,224},{384,288},{224,352},{0,416},{... | collective-permute-start | bytes 3145736 | tf_op jit(solution)/shard_map/ppermute | solution.py:109
  11.8 0.5 broadcast.21
  12.2 1.2 reduce.14
  13.5 0.1 concatenate.20
  13.5 1.2 reduce.15
  14.8 0.1 concatenate.21
  14.9 0.1 convert_element_type.20
  15.0 0.7 fusion.6
  15.7 1.3 %collective-permute-start.1 = (f32[268]{0:T(512)S(1)}, f32[268]{0:T(512)S(1)}, u32[]{:S(2)}, u32[]{:S(2)}) collective-permute-start(f32[268]{0:T(512)S(1)} %get-tuple-element.6), channel_id=1, source_target_pairs={{128,32},{480,96},{256,160},{96,224},{384,288},{224,352},{0,416},{... | collective-permute-start | bytes 3224 | tf_op jit(solution)/shard_map/ppermute | solution.py:116
  17.0 1.9 %collective-permute-start = (f32[268]{0:T(512)S(1)}, f32[268]{0:T(512)S(1)}, u32[]{:S(2)}, u32[]{:S(2)}) collective-permute-start(f32[268]{0:T(512)S(1)} %get-tuple-element.5), channel_id=1, source_target_pairs={{32,0},{0,32},{96,64},{64,96},{160,128},{128,160},{224,192},{192,2... | collective-permute-start | bytes 3224 | tf_op jit(solution)/shard_map/ppermute | solution.py:115
  18.9 1.3 %broadcast_in_dim.2 = s32[64,1,24]{2,1,0:T(1,128)} broadcast(s32[24]{0:T(128)} %bitcast.34), dimensions={2} | broadcast | bytes 6240 | tf_op jit(solution)/shard_map/broadcast_in_dim | solution.py:131
  20.2 9.2 %all-to-all-start = ((s32[64,1,24]{2,1,0:T(1,128)}), s32[64,1,24]{2,1,0:T(1,128)S(1)}, u32[]{:S(2)}, u32[]{:S(2)}) async-start(s32[64,1,24]{2,1,0:T(1,128)} %broadcast_in_dim.2), calls=%async_computation | async-start | bytes 65536 | tf_op jit(solution)/shard_map/all_to_all | solution.py:21
  29.5 0.1 stack.24.chosen
  29.6 0.0 collective-permute-done.1
  29.6 0.0 collective-permute-done
  29.7 0.1 reshape.30
  29.8 0.1 reshape_squeeze.6.left_ids
  29.9 0.1 reshape_squeeze.7.right_ids
  29.9 0.1 copy.19
  30.1 0.0 collective-permute-done.2.swapped
  30.1 2.8 %collective-permute-done.3.near = bf16[256,2048]{1,0:T(8,128)(2,1)S(1)} collective-permute-done((bf16[256,2048]{1,0:T(8,128)(2,1)}, bf16[256,2048]{1,0:T(8,128)(2,1)S(1)}, u32[]{:S(2)}, u32[]{:S(2)}) %collective-permute-start.3) | collective-permute-done | bytes 1048608 | tf_op jit(solution)/shard_map/ppermute | solution.py:108
  32.9 0.0 collective-permute-done.4.far
  32.9 0.0 copy-start.1
  32.9 1.2 copy-done.1
  34.1 3.2 %products.1 = bf16[64,192,128]{2,1,0:T(8,128)(2,1)S(1)} custom-call(s32[8]{0:T(128)S(1)} %stack.24.chosen, s32[24]{0:T(128)S(1)} %reshape_squeeze.6.left_ids, s32[24]{0:T(128)S(1)} %reshape_squeeze.7.right_ids, f32[256,4]{1,0:T(8,128)S(1)} %bitcast.29, bf16[256,2048]{1,0:T(8,128)(2,1)S(1)} %bitcast.27, bf16[256,2048]{1,0:T(8,128)(2,1)S(1)} %collective-permute-done.2.swapped, ...), custom_call_target="tpu_custom_call" | custom-call | tf_op jit(solution)/shard_map/products/pallas_call | solution.py:137
  37.3 0.0 copy-start
  37.4 1.7 %copy-done = bf16[64,192,128]{2,1,0:T(8,128)(2,1)} copy-done((bf16[64,192,128]{2,1,0:T(8,128)(2,1)}, bf16[64,192,128]{2,1,0:T(8,128)(2,1)S(1)}, u32[]{:S(2)}) %copy-start) | copy-done | bytes 3145752
  39.0 0.0 all-to-all-done
  39.0 9.0 %all-to-all-start.1 = ((bf16[64,192,128]{2,1,0:T(8,128)(2,1)}), bf16[64,192,128]{2,1,0:T(8,128)(2,1)S(1)}, u32[]{:S(2)}, u32[]{:S(2)}) async-start(bf16[64,192,128]{2,1,0:T(8,128)(2,1)} %copy-done), calls=%async_computation.1 | async-start | bytes 6291456 | tf_op jit(solution)/shard_map/all_to_all | solution.py:21
  48.0 0.6 reduce.13
  48.7 0.1 reshape.29.labels
  48.8 38.8 %all-to-all-done.1.got = bf16[64,192,128]{2,1,0:T(8,128)(2,1)S(1)} async-done(((bf16[64,192,128]{2,1,0:T(8,128)(2,1)}), bf16[64,192,128]{2,1,0:T(8,128)(2,1)S(1)}, u32[]{:S(2)}, u32[]{:S(2)}) %all-to-all-start.1) | async-done | bytes 3145760 | tf_op jit(solution)/shard_map/all_to_all | solution.py:21
  87.5 6.0 %sums.1 = bf16[1024,128]{1,0:T(8,128)(2,1)S(1)} custom-call(s32[1536]{0:T(1024)S(1)} %reshape.29.labels, bf16[64,192,128]{2,1,0:T(8,128)(2,1)S(1)} %all-to-all-done.1.got), custom_call_target="tpu_custom_call" | custom-call | tf_op jit(solution)/shard_map/sums/pallas_call | solution.py:147
  93.5 32.9 %all_to_all.20 = bf16[16,64,128]{2,1,0:T(8,128)(2,1)S(1)} all-to-all(bf16[16,64,128]{2,1,0:T(8,128)(2,1)S(1)} %bitcast.28), channel_id=1, replica_groups=mesh['tx'=16,'mp_hi'=8,'mp_lo'=2,'rep'=2] {'mp_hi','mp_lo'}, dimensions={0} | all-to-all | bytes 524288 | tf_op jit(solution)/shard_map/all_to_all | solution.py:21
  126.4 0.6 pad_maximum_fusion
  (17 shorter events, 0.2 us)
Async XLA Ops:
  0.0 30.1 %collective-permute-start.2 = (bf16[256,2048]{1,0:T(8,128)(2,1)}, bf16[256,2048]{1,0:T(8,128)(2,1)S(1)}, u32[]{:S(2)}, u32[]{:S(2)}) collective-permute-start(bf16[256,2048]{1,0:T(8,128)(2,1)} %bitcast.24), channel_id=1, source_target_pairs={{32,0},{0,32},{96,64},{64,96},{160,128},{128,160},{224,192},{192,2... | collective-permute-start | bytes 3145736 | tf_op jit(solution)/shard_map/ppermute | solution.py:110
  1.9 31.0 %collective-permute-start.3 = (bf16[256,2048]{1,0:T(8,128)(2,1)}, bf16[256,2048]{1,0:T(8,128)(2,1)S(1)}, u32[]{:S(2)}, u32[]{:S(2)}) collective-permute-start(bf16[256,2048]{1,0:T(8,128)(2,1)} %bitcast.25), channel_id=1, source_target_pairs={{96,0},{64,32},{160,64},{128,96},{224,128},{192,160},{288,192},{25... | collective-permute-start | bytes 3145736 | tf_op jit(solution)/shard_map/ppermute | solution.py:108
  9.4 23.5 %collective-permute-start.4 = (bf16[256,2048]{1,0:T(8,128)(2,1)}, bf16[256,2048]{1,0:T(8,128)(2,1)S(1)}, u32[]{:S(2)}, u32[]{:S(2)}) collective-permute-start(bf16[256,2048]{1,0:T(8,128)(2,1)} %bitcast.26), channel_id=1, source_target_pairs={{128,32},{480,96},{256,160},{96,224},{384,288},{224,352},{0,416},{... | collective-permute-start | bytes 3145736 | tf_op jit(solution)/shard_map/ppermute | solution.py:109
  15.7 13.9 %collective-permute-start.1 = (f32[268]{0:T(512)S(1)}, f32[268]{0:T(512)S(1)}, u32[]{:S(2)}, u32[]{:S(2)}) collective-permute-start(f32[268]{0:T(512)S(1)} %get-tuple-element.6), channel_id=1, source_target_pairs={{128,32},{480,96},{256,160},{96,224},{384,288},{224,352},{0,416},{... | collective-permute-start | bytes 3224 | tf_op jit(solution)/shard_map/ppermute | solution.py:116
  17.0 12.6 %collective-permute-start = (f32[268]{0:T(512)S(1)}, f32[268]{0:T(512)S(1)}, u32[]{:S(2)}, u32[]{:S(2)}) collective-permute-start(f32[268]{0:T(512)S(1)} %get-tuple-element.5), channel_id=1, source_target_pairs={{32,0},{0,32},{96,64},{64,96},{160,128},{128,160},{224,192},{192,2... | collective-permute-start | bytes 3224 | tf_op jit(solution)/shard_map/ppermute | solution.py:115
  20.2 18.8 %all-to-all-start = ((s32[64,1,24]{2,1,0:T(1,128)}), s32[64,1,24]{2,1,0:T(1,128)S(1)}, u32[]{:S(2)}, u32[]{:S(2)}) async-start(s32[64,1,24]{2,1,0:T(1,128)} %broadcast_in_dim.2), calls=%async_computation | async-start | bytes 65536 | tf_op jit(solution)/shard_map/all_to_all | solution.py:21
  32.9 1.2 copy-start.1
  37.3 1.7 %copy-start = (bf16[64,192,128]{2,1,0:T(8,128)(2,1)}, bf16[64,192,128]{2,1,0:T(8,128)(2,1)S(1)}, u32[]{:S(2)}) copy-start(bf16[64,192,128]{2,1,0:T(8,128)(2,1)S(1)} %products.1) | copy-start | bytes 9437188
  39.0 48.5 %all-to-all-start.1 = ((bf16[64,192,128]{2,1,0:T(8,128)(2,1)}), bf16[64,192,128]{2,1,0:T(8,128)(2,1)S(1)}, u32[]{:S(2)}, u32[]{:S(2)}) async-start(bf16[64,192,128]{2,1,0:T(8,128)(2,1)} %copy-done), calls=%async_computation.1 | async-start | bytes 6291456 | tf_op jit(solution)/shard_map/all_to_all | solution.py:21

commit v3 on v2

v3 whole, which is shorter than its diff:
```python
import functools

import jax
import jax.numpy as jnp
from jax import lax
from jax.experimental import pallas as pl
from jax.experimental.pallas import tpu as pltpu
from jax.sharding import Mesh, PartitionSpec as P

BRICK = 256
STEPS = 4
LISTED = 6
PAIRS = STEPS * LISTED
TILES_DEV = 8
HALVES = 2
CHAINS = 4
GROUP = ("mp_lo", "tx", "rep")
OWNERS = ("mp_hi", "mp_lo")


def exchanged(block, axis):
    return lax.all_to_all(block, axis, split_axis=0, concat_axis=0, tiled=True)


def routes(devices):
    everyone = range(devices)
    swap = [(i ^ 1, i) for i in everyone]
    near = [((i + (1 if i % 2 else 3)) % devices, i) for i in everyone]
    far = [((i + (3 if i % 4 == 1 else -4)) % devices, i) for i in everyone if i % 2]
    return swap, near, far


def add_tiles(left_ids, right_ids, step, weight, left_block, right_block, out, offset):
    parts = out.shape[0]
    half = parts // HALVES
    slab = BRICK // half
    width = BRICK // HALVES

    def brick(block, index):
        return block[:, pl.ds(pl.multiple_of(index * BRICK, BRICK), BRICK)]

    for first in range(0, LISTED, 2):
        pair = []
        for entry in (first, first + 1):
            left = brick(left_block, left_ids[step * LISTED + entry]).astype(jnp.float32) * weight
            tile = lax.dot_general(
                left.astype(jnp.bfloat16),
                brick(right_block, right_ids[step * LISTED + entry]),
                (((0,), (0,)), ((), ())),
                preferred_element_type=jnp.float32,
            )
            pair.append(tile.reshape(half, slab, BRICK))
        both = jnp.concatenate(pair, axis=1).astype(jnp.bfloat16)
        rows = slice(offset + first * slab, offset + (first + 2) * slab)
        for side in range(HALVES):
            out[side * half : (side + 1) * half, rows, :] = both[:, :, side * width : (side + 1) * width]


def own_kernel(left_ids, right_ids, weight, own, out):
    add_tiles(left_ids, right_ids, 0, weight[...], own, own, out, 0)


def pair_kernel(place, left_ids, right_ids, weight, own, near, far, swapped, out, stage, sems):
    rows = out.shape[1] // (STEPS - 1)
    spot = place[0]
    even = spot % 2 == 0
    cases = (
        ((even, own, swapped), (jnp.logical_not(even), own, near)),
        ((None, swapped, near),),
        ((even, own, near), (spot == 1, own, far), (spot == 3, far, swapped)),
    )
    copies = []
    for step in range(1, STEPS):
        offset = (step - 1) * rows
        for when, left_block, right_block in cases[step - 1]:
            run = functools.partial(
                add_tiles, left_ids, right_ids, step, weight[:, step : step + 1], left_block, right_block, stage, offset
            )
            if when is None:
                run()
            else:
                pl.when(when)(run)
        done = pl.ds(offset, rows)
        copy = pltpu.make_async_copy(stage.at[:, done, :], out.at[:, done, :], sems.at[step - 1])
        copy.start()
        copies.append(copy)
    for copy in copies:
        copy.wait()


def sum_kernel(subsets, first_step, last_step, labels, got, *refs):
    before, out, totals = refs[:-CHAINS - 1], refs[-CHAINS - 1], refs[-CHAINS:]
    parts = got.shape[0]
    plane = parts // HALVES
    slab = totals[0].shape[1]
    for total in totals:
        total[...] = jnp.zeros_like(total)

    def one_part(part, carry):
        place = part // subsets % 4
        swapped = part + jnp.where(place % 2 == 0, subsets, -subsets)
        earlier = jnp.where(part % plane < 4 * subsets, part + plane - 4 * subsets, part - 4 * subsets)
        listed = (part, part, swapped, jnp.where(place == 3, earlier, part))
        for first in range(first_step * LISTED, last_step * LISTED, 2):
            start = listed[first // LISTED] * PAIRS + first
            row = (first - first_step * LISTED) * slab
            both = got[part, row : row + 2 * slab, :].astype(jnp.float32)
            for side in range(2):
                total = totals[(first + side) % CHAINS]
                total[labels[start + side]] += both[side * slab : (side + 1) * slab]
        return carry

    lax.fori_loop(0, parts, one_part, 0)
    whole = functools.reduce(lambda a, b: a + b, [total[...] for total in totals])
    if before:
        whole += before[0][...]
    out[...] = whole.reshape(out.shape).astype(out.dtype)


def body(jacobian, coupling, brick_left, brick_right, tile_target):
    own = jacobian[0]
    rows = own.shape[0]
    devices = lax.axis_size("tx")
    subsets = lax.axis_size("rep")
    swap, near, far = routes(devices)
    place = lax.axis_index("tx") % 4
    parts = devices * subsets * HALVES
    owners = lax.axis_size("mp_hi") * lax.axis_size("mp_lo")
    slab = BRICK // (parts // HALVES)
    width = BRICK // HALVES
    tiles = owners * TILES_DEV
    smem = pl.BlockSpec(memory_space=pltpu.SMEM)
    vmem = pl.BlockSpec(memory_space=pltpu.VMEM)
    params = pltpu.CompilerParams(vmem_limit_bytes=32 * 2**20)

    near_block = lax.ppermute(own, "tx", near)
    far_block = lax.ppermute(own, "tx", far)
    swapped_block = lax.ppermute(own, "tx", swap)
    weight = coupling[:, 0]
    left_ids, right_ids = brick_left[0, 0], brick_right[0, 0]
    cut = 2 * LISTED
    ids = [x[cut:].reshape(2, LISTED) for x in (left_ids, right_ids)]
    meta = jnp.concatenate([weight[2:]] + [x.astype(jnp.float32) for x in ids], axis=1)
    of_swapped = lax.ppermute(meta[0], "tx", swap)
    of_far = jnp.where(place == 3, lax.ppermute(meta[1], "tx", far), meta[1])

    early = pl.pallas_call(
        own_kernel,
        out_shape=jax.ShapeDtypeStruct((parts, LISTED * slab, width), jnp.bfloat16),
        in_specs=[smem, smem, vmem, vmem],
        out_specs=vmem,
        compiler_params=params,
        name="own_products",
    )(left_ids, right_ids, weight[0][:, None], own)
    listed = jnp.pad(tile_target[0].astype(jnp.bfloat16), ((0, slab - 1), (0, width - PAIRS)))
    early = jnp.concatenate([early, jnp.broadcast_to(listed, (parts, slab, width))], axis=1)
    early = exchanged(early, GROUP)
    labels = early[:, LISTED * slab, :PAIRS].astype(jnp.int32).reshape(-1)

    meta = jnp.stack([of_swapped, of_far])
    weight = jnp.concatenate([weight[:2], meta[:, :rows]], axis=0)
    ids = meta[:, rows:].astype(jnp.int32).reshape(2, 2, LISTED)
    left_ids = jnp.concatenate([left_ids[:cut], ids[:, 0].reshape(-1)])
    right_ids = jnp.concatenate([right_ids[:cut], ids[:, 1].reshape(-1)])
    late_shape = (parts, (STEPS - 1) * LISTED * slab, width)
    late = pl.pallas_call(
        pair_kernel,
        out_shape=jax.ShapeDtypeStruct(late_shape, jnp.bfloat16),
        in_specs=[smem, smem, smem, vmem, vmem, vmem, vmem, vmem],
        out_specs=pl.BlockSpec(memory_space=pltpu.HBM),
        scratch_shapes=[pltpu.VMEM(late_shape, jnp.bfloat16), pltpu.SemaphoreType.DMA((STEPS - 1,))],
        compiler_params=params,
        name="pair_products",
    )(place.reshape(1), left_ids, right_ids, weight.T, own, near_block, far_block, swapped_block)
    late = exchanged(late, GROUP)

    chains = [pltpu.VMEM((tiles, slab, width), jnp.float32) for _ in range(CHAINS)]
    first_sums = pl.pallas_call(
        functools.partial(sum_kernel, subsets, 0, 1),
        out_shape=jax.ShapeDtypeStruct((tiles, slab, width), jnp.float32),
        in_specs=[smem, vmem],
        out_specs=vmem,
        scratch_shapes=chains,
        compiler_params=params,
        name="own_sums",
    )(labels, early)
    sums = pl.pallas_call(
        functools.partial(sum_kernel, subsets, 1, STEPS),
        out_shape=jax.ShapeDtypeStruct((tiles * slab, width), jnp.bfloat16),
        in_specs=[smem, vmem, vmem],
        out_specs=vmem,
        scratch_shapes=chains,
        compiler_params=params,
        name="pair_sums",
    )(labels, late, first_sums)
    sums = exchanged(sums, OWNERS).reshape(owners // HALVES, HALVES, TILES_DEV, slab, width)
    sums = jnp.sum(sums.astype(jnp.float32), axis=0)
    return jnp.concatenate([sums[side] for side in range(HALVES)], axis=-1)


def solution(mesh):
    shape = (mesh.shape["tx"], mesh.shape["mp"] // HALVES, HALVES, mesh.shape["rep"])
    mesh = Mesh(mesh.devices.reshape(shape), ("tx", "mp_hi", "mp_lo", "rep"))
    data = ("mp_hi", "mp_lo", "rep")
    in_specs = (
        P("tx", data, None),
        P(None, "tx", data),
        P("tx", data, None),
        P("tx", data, None),
        P("tx", data, None),
    )
    out_specs = P(OWNERS, ("tx", "rep"), None)
    return jax.shard_map(body, mesh=mesh, in_specs=in_specs, out_specs=out_specs, check_vma=False)
```

time: 128 us -> 132 us (1.031)
  the two profiles are of different devices: /device:TPU:32 before, /device:TPU:64 now
where the time goes in v3:
time: 132 us
  waiting for transfers between devices  45.8 us (35%)
  starting transfers between devices  33.8 us (26%)
  blocking collectives  32.5 us (25%)
  Pallas kernels  10.6 us (8%)
  local copies, waits for them, and re-layouts  5.94 us (4%)
  other arithmetic  2.79 us (2%)
    all_to_all x1, blocking collectives, exchanged(): return lax.all_to_all(block, axis, split_axis=0, concat_axis=0, tiled=True)  32.5 us
    all_to_all x2, waiting for transfers between devices, exchanged(): return lax.all_to_all(block, axis, split_axis=0, concat_axis=0, tiled=True)  28.1 us
    all_to_all x2, starting transfers between devices, exchanged(): return lax.all_to_all(block, axis, split_axis=0, concat_axis=0, tiled=True)  16.9 us
    ppermute x1, waiting for transfers between devices, body(): near_block = lax.ppermute(own, 'tx', near)  11.6 us
    ppermute x1, starting transfers between devices, body(): near_block = lax.ppermute(own, 'tx', near)  6.92 us
    ppermute x1, waiting for transfers between devices, body(): of_far = jnp.where(place == 3, lax.ppermute(meta[1], 'tx', far), meta[1])  6.07 us
    unnamed x20, local copies, waits for them, and re-layouts  4.41 us
    pallas_call x1, Pallas kernels, body(): pl.pallas_call(pair_kernel, out_shape=jax.ShapeDtypeStruct(late_shape, jn...  4.33 us
  transfers between devices with their start and end apart: 7, of which 3 were waited for; matrix products, arithmetic and copies ran while one was open for 1% of the time, Pallas kernels for 5%

profile of v3, /device:TPU:64, one launch (start us, length us, event | category | flops | bytes accessed | tf_op | source)
XLA Modules:
  0.0 131.7 jit_solution(14141290341044123355)
XLA Ops:
  0.0 0.7 slice_bitcast_fusion.2
  0.7 0.1 copy.13.weight
  0.8 0.7 convert_bitcast_fusion
  1.5 0.0 copy-start
  1.5 1.2 copy-done
  2.7 0.0 copy-start.4
  2.7 0.7 copy-done.4
  3.4 0.0 copy-start.6
  3.4 0.7 copy-done.6
  4.0 1.1 own_products.1
  5.2 0.0 copy-start.1
  5.2 0.0 copy-start.8
  5.2 0.0 copy-start.5
  5.2 0.0 copy-start.7
  5.2 1.0 pad_maximum_fusion
  6.2 9.3 %all-to-all-start = ((bf16[64,56,128]{2,1,0:T(8,128)(2,1)}), bf16[64,56,128]{2,1,0:T(8,128)(2,1)S(1)}, u32[]{:S(2)}, u32[]{:S(2)}) async-start(bf16[64,56,128]{2,1,0:T(8,128)(2,1)} %pad_maximum_fusion), calls=%async_computation | async-start | bytes 1835008 | tf_op jit(solution)/shard_map/all_to_all | solution.py:22
  15.5 0.0 copy-done.1
  15.6 6.9 %collective-permute-start.2 = (bf16[256,2048]{1,0:T(8,128)(2,1)S(1)}, bf16[256,2048]{1,0:T(8,128)(2,1)S(1)}, u32[]{:S(2)}, u32[]{:S(2)}) collective-permute-start(bf16[256,2048]{1,0:T(8,128)(2,1)S(1)} %bitcast.27), channel_id=1, source_target_pairs={{96,0},{64,32},{160,64},{128,96},{224,128},{192,160},{288,192},{25... | collective-permute-start | bytes 3145736 | tf_op jit(solution)/shard_map/ppermute | solution.py:136
  22.5 3.7 %collective-permute-start.3 = (bf16[256,2048]{1,0:T(8,128)(2,1)S(1)}, bf16[256,2048]{1,0:T(8,128)(2,1)}, u32[]{:S(2)}, u32[]{:S(2)}) collective-permute-start(bf16[256,2048]{1,0:T(8,128)(2,1)S(1)} %bitcast.28), channel_id=1, source_target_pairs={{128,32},{480,96},{256,160},{96,224},{384,288},{224,352},{0,416},{... | collective-permute-start | bytes 3145736 | tf_op jit(solution)/shard_map/ppermute | solution.py:137
  26.1 1.9 %collective-permute-start.4 = (bf16[256,2048]{1,0:T(8,128)(2,1)S(1)}, bf16[256,2048]{1,0:T(8,128)(2,1)}, u32[]{:S(2)}, u32[]{:S(2)}) collective-permute-start(bf16[256,2048]{1,0:T(8,128)(2,1)S(1)} %bitcast.29), channel_id=1, source_target_pairs={{32,0},{0,32},{96,64},{64,96},{160,128},{128,160},{224,192},{192,2... | collective-permute-start | bytes 3145736 | tf_op jit(solution)/shard_map/ppermute | solution.py:138
  28.1 0.0 copy-done.8
  28.1 0.0 copy-done.5
  28.1 0.0 copy-done.7
  28.1 0.1 convert_reduce_fusion.1
  28.2 0.1 convert_element_type.49
  28.3 0.1 convert_element_type.51
  28.4 0.1 pad_maximum_fusion.3
  28.5 2.6 %collective-permute-start.1 = (f32[268]{0:T(512)S(1)}, f32[268]{0:T(512)S(1)}, u32[]{:S(2)}, u32[]{:S(2)}) collective-permute-start(f32[268]{0:T(512)S(1)} %get-tuple-element.6), channel_id=1, source_target_pairs={{128,32},{480,96},{256,160},{96,224},{384,288},{224,352},{0,416},{... | collective-permute-start | bytes 3224 | tf_op jit(solution)/shard_map/ppermute | solution.py:145
  31.0 1.9 %collective-permute-start = (f32[268]{0:T(512)S(1)}, f32[268]{0:T(512)S(1)}, u32[]{:S(2)}, u32[]{:S(2)}) collective-permute-start(f32[268]{0:T(512)S(1)} %get-tuple-element.5), channel_id=1, source_target_pairs={{32,0},{0,32},{96,64},{64,96},{160,128},{128,160},{224,192},{192,2... | collective-permute-start | bytes 3224 | tf_op jit(solution)/shard_map/ppermute | solution.py:144
  33.0 6.1 %collective-permute-done.1 = f32[268]{0:T(512)S(1)} collective-permute-done((f32[268]{0:T(512)S(1)}, f32[268]{0:T(512)S(1)}, u32[]{:S(2)}, u32[]{:S(2)}) %collective-permute-start.1) | collective-permute-done | bytes 1104 | tf_op jit(solution)/shard_map/ppermute | solution.py:145
  39.1 0.0 collective-permute-done
  39.1 0.1 copy.15
  39.3 0.1 reshape.44
  39.4 0.1 reshape_squeeze.6
  39.5 0.1 reshape_squeeze.7
  39.5 0.1 pad_add_fusion.left_ids
  39.6 0.1 pad_add_fusion.1.right_ids
  39.7 11.6 %collective-permute-done.2.near = bf16[256,2048]{1,0:T(8,128)(2,1)S(1)} collective-permute-done((bf16[256,2048]{1,0:T(8,128)(2,1)S(1)}, bf16[256,2048]{1,0:T(8,128)(2,1)S(1)}, u32[]{:S(2)}, u32[]{:S(2)}) %collective-permute-start.2) | collective-permute-done | bytes 1048608 | tf_op jit(solution)/shard_map/ppermute | solution.py:136
  51.3 0.0 collective-permute-done.3.far
  51.3 0.0 collective-permute-done.4.swapped
  51.3 4.3 %pair_products.1 = bf16[64,144,128]{2,1,0:T(8,128)(2,1)} custom-call(s32[1]{0:T(128)} %bitcast.5.place, s32[24]{0:T(128)S(1)} %pad_add_fusion.left_ids, s32[24]{0:T(128)S(1)} %pad_add_fusion.1.right_ids, f32[256,4]{1,0:T(8,128)S(1)} %bitcast.32, bf16[256,2048]{1,0:T(8,128)(2,1)S(1)} %bitcast.30, bf16[256,2048]{1,0:T(8,128)(2,1)S(1)} %collective-permute-done.2.near, ...), custom_call_target="tpu_custom_call" | custom-call | tf_op jit(solution)/shard_map/pair_products/pallas_call | solution.py:166
  55.6 0.0 all-to-all-done.got
  55.6 7.6 %all-to-all-start.1 = ((bf16[64,144,128]{2,1,0:T(8,128)(2,1)}), bf16[64,144,128]{2,1,0:T(8,128)(2,1)S(1)}, u32[]{:S(2)}, u32[]{:S(2)}) async-start(bf16[64,144,128]{2,1,0:T(8,128)(2,1)} %pair_products.1), calls=%async_computation.1 | async-start | bytes 4718592 | tf_op jit(solution)/shard_map/all_to_all | solution.py:22
  63.2 0.1 fusion
  63.4 0.1 reshape.45.labels
  63.4 1.7 %own_sums.1.refs_0_ = f32[128,8,128]{2,1,0:T(8,128)S(1)} custom-call(s32[1536]{0:T(1024)S(1)} %reshape.45.labels, bf16[64,56,128]{2,1,0:T(8,128)(2,1)S(1)} %all-to-all-done.got), custom_call_target="tpu_custom_call" | custom-call | tf_op jit(solution)/shard_map/own_sums/pallas_call | solution.py:178
  65.2 0.0 copy-start.2
  65.2 0.8 copy-done.2
  66.0 28.1 %all-to-all-done.1.got = bf16[64,144,128]{2,1,0:T(8,128)(2,1)S(1)} async-done(((bf16[64,144,128]{2,1,0:T(8,128)(2,1)}), bf16[64,144,128]{2,1,0:T(8,128)(2,1)S(1)}, u32[]{:S(2)}, u32[]{:S(2)}) %all-to-all-start.1) | async-done | bytes 2359328 | tf_op jit(solution)/shard_map/all_to_all | solution.py:22
  94.1 0.0 copy-start.3
  94.1 1.0 copy-done.3
  95.1 3.5 %pair_sums.1 = bf16[1024,128]{1,0:T(8,128)(2,1)S(1)} custom-call(s32[1536]{0:T(1024)S(1)} %reshape.45.labels, bf16[64,144,128]{2,1,0:T(8,128)(2,1)S(1)} %all-to-all-done.1.got, f32[128,8,128]{2,1,0:T(8,128)S(1)} %copy-done.3), custom_call_target="tpu_custom_call" | custom-call | tf_op jit(solution)/shard_map/pair_sums/pallas_call | solution.py:187
  98.6 32.5 %all_to_all.19 = bf16[16,64,128]{2,1,0:T(8,128)(2,1)S(1)} all-to-all(bf16[16,64,128]{2,1,0:T(8,128)(2,1)S(1)} %bitcast.31), channel_id=1, replica_groups=mesh['tx'=16,'mp_hi'=8,'mp_lo'=2,'rep'=2] {'mp_hi','mp_lo'}, dimensions={0} | all-to-all | bytes 524288 | tf_op jit(solution)/shard_map/all_to_all | solution.py:22
  131.1 0.6 pad_maximum_fusion.1
  (16 shorter events, 0.2 us)
Async XLA Ops:
  1.5 1.2 copy-start
  2.7 0.7 copy-start.4
  3.4 0.7 copy-start.6
  5.2 10.4 %copy-start.1 = (bf16[1,256,2048]{2,1,0:T(8,128)(2,1)S(1)}, bf16[1,256,2048]{2,1,0:T(8,128)(2,1)}, u32[]{:S(2)}) copy-start(bf16[1,256,2048]{2,1,0:T(8,128)(2,1)} %param.5) | copy-start | bytes 3145732
  5.2 22.9 %copy-start.8 = (f32[4,1,256]{2,1,0:T(1,128)S(1)}, f32[4,1,256]{2,1,0:T(1,128)}, u32[]{:S(2)}) copy-start(f32[4,1,256]{2,1,0:T(1,128)} %param.6) | copy-start | bytes 12292
  5.2 22.9 %copy-start.5 = (s32[1,1,24]{2,1,0:T(1,128)S(1)}, s32[1,1,24]{2,1,0:T(1,128)}, u32[]{:S(2)}) copy-start(s32[1,1,24]{2,1,0:T(1,128)} %param.7) | copy-start | bytes 292
  5.2 22.9 %copy-start.7 = (s32[1,1,24]{2,1,0:T(1,128)S(1)}, s32[1,1,24]{2,1,0:T(1,128)}, u32[]{:S(2)}) copy-start(s32[1,1,24]{2,1,0:T(1,128)} %param.8) | copy-start | bytes 292
  6.2 49.4 %all-to-all-start = ((bf16[64,56,128]{2,1,0:T(8,128)(2,1)}), bf16[64,56,128]{2,1,0:T(8,128)(2,1)S(1)}, u32[]{:S(2)}, u32[]{:S(2)}) async-start(bf16[64,56,128]{2,1,0:T(8,128)(2,1)} %pad_maximum_fusion), calls=%async_computation | async-start | bytes 1835008 | tf_op jit(solution)/shard_map/all_to_all | solution.py:22
  15.6 35.7 %collective-permute-start.2 = (bf16[256,2048]{1,0:T(8,128)(2,1)S(1)}, bf16[256,2048]{1,0:T(8,128)(2,1)S(1)}, u32[]{:S(2)}, u32[]{:S(2)}) collective-permute-start(bf16[256,2048]{1,0:T(8,128)(2,1)S(1)} %bitcast.27), channel_id=1, source_target_pairs={{96,0},{64,32},{160,64},{128,96},{224,128},{192,160},{288,192},{25... | collective-permute-start | bytes 3145736 | tf_op jit(solution)/shard_map/ppermute | solution.py:136
  22.5 28.8 %collective-permute-start.3 = (bf16[256,2048]{1,0:T(8,128)(2,1)S(1)}, bf16[256,2048]{1,0:T(8,128)(2,1)}, u32[]{:S(2)}, u32[]{:S(2)}) collective-permute-start(bf16[256,2048]{1,0:T(8,128)(2,1)S(1)} %bitcast.28), channel_id=1, source_target_pairs={{128,32},{480,96},{256,160},{96,224},{384,288},{224,352},{0,416},{... | collective-permute-start | bytes 3145736 | tf_op jit(solution)/shard_map/ppermute | solution.py:137
  26.1 25.2 %collective-permute-start.4 = (bf16[256,2048]{1,0:T(8,128)(2,1)S(1)}, bf16[256,2048]{1,0:T(8,128)(2,1)}, u32[]{:S(2)}, u32[]{:S(2)}) collective-permute-start(bf16[256,2048]{1,0:T(8,128)(2,1)S(1)} %bitcast.29), channel_id=1, source_target_pairs={{32,0},{0,32},{96,64},{64,96},{160,128},{128,160},{224,192},{192,2... | collective-permute-start | bytes 3145736 | tf_op jit(solution)/shard_map/ppermute | solution.py:138
  28.5 10.6 %collective-permute-start.1 = (f32[268]{0:T(512)S(1)}, f32[268]{0:T(512)S(1)}, u32[]{:S(2)}, u32[]{:S(2)}) collective-permute-start(f32[268]{0:T(512)S(1)} %get-tuple-element.6), channel_id=1, source_target_pairs={{128,32},{480,96},{256,160},{96,224},{384,288},{224,352},{0,416},{... | collective-permute-start | bytes 3224 | tf_op jit(solution)/shard_map/ppermute | solution.py:145
  31.0 8.1 %collective-permute-start = (f32[268]{0:T(512)S(1)}, f32[268]{0:T(512)S(1)}, u32[]{:S(2)}, u32[]{:S(2)}) collective-permute-start(f32[268]{0:T(512)S(1)} %get-tuple-element.5), channel_id=1, source_target_pairs={{32,0},{0,32},{96,64},{64,96},{160,128},{128,160},{224,192},{192,2... | collective-permute-start | bytes 3224 | tf_op jit(solution)/shard_map/ppermute | solution.py:144
  55.6 38.4 %all-to-all-start.1 = ((bf16[64,144,128]{2,1,0:T(8,128)(2,1)}), bf16[64,144,128]{2,1,0:T(8,128)(2,1)S(1)}, u32[]{:S(2)}, u32[]{:S(2)}) async-start(bf16[64,144,128]{2,1,0:T(8,128)(2,1)} %pair_products.1), calls=%async_computation.1 | async-start | bytes 4718592 | tf_op jit(solution)/shard_map/all_to_all | solution.py:22
  65.2 0.8 copy-start.2
  94.1 1.0 copy-start.3

commit v4 on v3

--- a/solution.py
+++ b/solution.py
@@ -170,6 +170,7 @@
         out_specs=pl.BlockSpec(memory_space=pltpu.HBM),
         scratch_shapes=[pltpu.VMEM(late_shape, jnp.bfloat16), pltpu.SemaphoreType.DMA((STEPS - 1,))],
         compiler_params=params,
+        cost_estimate=pl.CostEstimate(flops=10**11, bytes_accessed=2**23, transcendentals=0),
         name="pair_products",
     )(place.reshape(1), left_ids, right_ids, weight.T, own, near_block, far_block, swapped_block)
     late = exchanged(late, GROUP)

time: 132 us -> 122 us (0.924)
  waiting for transfers between devices: 45.8 us -> 37.7 us
  starting transfers between devices: 33.8 us -> 29.1 us
  local copies, waits for them, and re-layouts: 5.94 us -> 8.04 us
    ppermute x1, waiting for transfers between devices: 11.6 us -> 0.01 us  [body(): near_block = lax.ppermute(own, 'tx', near)]
    all_to_all x2, waiting for transfers between devices: 28.1 us -> 37.6 us  [exchanged(): return lax.all_to_all(block, axis, split_axis=0, concat_axis=0, tiled=True)]
    ppermute x1, waiting for transfers between devices: 6.07 us -> 0.01 us  [body(): of_far = jnp.where(place == 3, lax.ppermute(meta[1], 'tx', far), meta[1])]
    all_to_all x2, starting transfers between devices: 16.9 us -> 12.1 us  [exchanged(): return lax.all_to_all(block, axis, split_axis=0, concat_axis=0, tiled=True)]
    unnamed x20, local copies, waits for them, and re-layouts: 4.41 us -> 5.81 us
  transfers between devices with their start and end apart: 7 -> 7, of which waited for: 3 -> 2; matrix products, arithmetic and copies ran while one was open for 1% -> 4% of each run, Pallas kernels for 5% -> 5%
where the time goes in v4:
time: 122 us; the launch traced here: 121 us
  waiting for transfers between devices  37.7 us (31%)
  blocking collectives  32.5 us (27%)
  starting transfers between devices  29.1 us (24%)
  Pallas kernels  9.84 us (8%)
  local copies, waits for them, and re-layouts  8.04 us (7%)
  other arithmetic  3.46 us (3%)
    all_to_all x2, waiting for transfers between devices, exchanged(): return lax.all_to_all(block, axis, split_axis=0, concat_axis=0, tiled=True)  37.6 us
    all_to_all x1, blocking collectives, exchanged(): return lax.all_to_all(block, axis, split_axis=0, concat_axis=0, tiled=True)  32.5 us
    all_to_all x2, starting transfers between devices, exchanged(): return lax.all_to_all(block, axis, split_axis=0, concat_axis=0, tiled=True)  12.1 us
    ppermute x1, starting transfers between devices, body(): near_block = lax.ppermute(own, 'tx', near)  6.81 us
    unnamed x20, local copies, waits for them, and re-layouts  5.81 us
    ppermute x1, starting transfers between devices, body(): far_block = lax.ppermute(own, 'tx', far)  3.93 us
    pallas_call x1, Pallas kernels, body(): pl.pallas_call(pair_kernel, out_shape=jax.ShapeDtypeStruct(late_shape, jn...  3.56 us
    pallas_call x1, Pallas kernels, body(): pl.pallas_call(functools.partial(sum_kernel, subsets, 1, STEPS), out_shap...  3.44 us
  transfers between devices with their start and end apart: 7, of which 2 were waited for; matrix products, arithmetic and copies ran while one was open for 4% of the time, Pallas kernels for 5%

profile of v4, /device:TPU:64, one launch (start us, length us, event | category | flops | bytes accessed | tf_op | source)
XLA Modules:
  0.0 120.9 jit_solution(6885854783216010046)
XLA Ops:
  0.0 6.8 %collective-permute-start.2 = (bf16[256,2048]{1,0:T(8,128)(2,1)}, bf16[256,2048]{1,0:T(8,128)(2,1)S(1)}, u32[]{:S(2)}, u32[]{:S(2)}) collective-permute-start(bf16[256,2048]{1,0:T(8,128)(2,1)} %bitcast.26), channel_id=1, source_target_pairs={{96,0},{64,32},{160,64},{128,96},{224,128},{192,160},{288,192},{25... | collective-permute-start | bytes 3145736 | tf_op jit(solution)/shard_map/ppermute | solution.py:136
  6.8 3.9 %collective-permute-start.3 = (bf16[256,2048]{1,0:T(8,128)(2,1)}, bf16[256,2048]{1,0:T(8,128)(2,1)}, u32[]{:S(2)}, u32[]{:S(2)}) collective-permute-start(bf16[256,2048]{1,0:T(8,128)(2,1)} %bitcast.27), channel_id=1, source_target_pairs={{128,32},{480,96},{256,160},{96,224},{384,288},{224,352},{0,416},{... | collective-permute-start | bytes 3145736 | tf_op jit(solution)/shard_map/ppermute | solution.py:137
  10.8 1.9 %collective-permute-start.4 = (bf16[256,2048]{1,0:T(8,128)(2,1)}, bf16[256,2048]{1,0:T(8,128)(2,1)}, u32[]{:S(2)}, u32[]{:S(2)}) collective-permute-start(bf16[256,2048]{1,0:T(8,128)(2,1)} %bitcast.28), channel_id=1, source_target_pairs={{32,0},{0,32},{96,64},{64,96},{160,128},{128,160},{224,192},{192,2... | collective-permute-start | bytes 3145736 | tf_op jit(solution)/shard_map/ppermute | solution.py:138
  12.7 0.7 fusion.2
  13.4 0.8 convert_reduce_fusion.1
  14.1 0.1 convert_element_type.49
  14.2 0.1 convert_element_type.51
  14.3 0.1 pad_maximum_fusion.3
  14.4 2.5 %collective-permute-start.1 = (f32[268]{0:T(512)S(1)}, f32[268]{0:T(512)S(1)}, u32[]{:S(2)}, u32[]{:S(2)}) collective-permute-start(f32[268]{0:T(512)S(1)} %get-tuple-element.6), channel_id=1, source_target_pairs={{128,32},{480,96},{256,160},{96,224},{384,288},{224,352},{0,416},{... | collective-permute-start | bytes 3224 | tf_op jit(solution)/shard_map/ppermute | solution.py:145
  16.9 1.9 %collective-permute-start = (f32[268]{0:T(512)S(1)}, f32[268]{0:T(512)S(1)}, u32[]{:S(2)}, u32[]{:S(2)}) collective-permute-start(f32[268]{0:T(512)S(1)} %get-tuple-element.5), channel_id=1, source_target_pairs={{32,0},{0,32},{96,64},{64,96},{160,128},{128,160},{224,192},{192,2... | collective-permute-start | bytes 3224 | tf_op jit(solution)/shard_map/ppermute | solution.py:144
  18.8 0.7 slice_bitcast_fusion.2
  19.5 0.1 copy.13.weight
  19.6 0.7 convert_bitcast_fusion
  20.3 0.0 copy-start.3
  20.3 1.2 %copy-done.3 = bf16[1,256,2048]{2,1,0:T(8,128)(2,1)S(1)} copy-done((bf16[1,256,2048]{2,1,0:T(8,128)(2,1)S(1)}, bf16[1,256,2048]{2,1,0:T(8,128)(2,1)}, u32[]{:S(2)}) %copy-start.3) | copy-done | bytes 1048600
  21.5 0.0 copy-start.5
  21.5 0.7 copy-done.5
  22.2 0.0 copy-start.7
  22.2 0.7 copy-done.7
  22.8 1.1 own_products.1
  24.0 0.0 copy-start.6
  24.0 0.0 copy-start.8
  24.0 0.0 copy-start.4
  24.0 1.0 pad_maximum_fusion
  25.0 6.7 %all-to-all-start = ((bf16[64,56,128]{2,1,0:T(8,128)(2,1)}), bf16[64,56,128]{2,1,0:T(8,128)(2,1)S(1)}, u32[]{:S(2)}, u32[]{:S(2)}) async-start(bf16[64,56,128]{2,1,0:T(8,128)(2,1)} %pad_maximum_fusion), calls=%async_computation | async-start | bytes 1835008 | tf_op jit(solution)/shard_map/all_to_all | solution.py:22
  31.7 0.0 copy-done.6
  31.7 0.0 copy-done.8
  31.8 0.0 collective-permute-done.1
  31.8 0.0 collective-permute-done
  31.9 0.1 copy.15
  32.0 0.1 reshape.44
  32.1 0.1 reshape_squeeze.6
  32.2 0.1 reshape_squeeze.7
  32.3 0.1 pad_add_fusion.left_ids
  32.4 0.1 pad_add_fusion.1.right_ids
  32.4 0.0 collective-permute-done.2.near
  32.4 0.0 collective-permute-done.3.far
  32.4 0.0 collective-permute-done.4.swapped
  32.5 0.0 copy-done.4
  32.5 3.6 %pair_products.1 = bf16[64,144,128]{2,1,0:T(8,128)(2,1)S(1)} custom-call(s32[1]{0:T(128)} %bitcast.5.place, s32[24]{0:T(128)S(1)} %pad_add_fusion.left_ids, s32[24]{0:T(128)S(1)} %pad_add_fusion.1.right_ids, f32[256,4]{1,0:T(8,128)S(1)} %bitcast.32, bf16[256,2048]{1,0:T(8,128)(2,1)S(1)} %bitcast.30, bf16[256,2048]{1,0:T(8,128)(2,1)S(1)} %collective-permute-done.2.near, ...), custom_call_target="tpu_custom_call" | custom-call | flops 99999997952 | bytes 8388608 | tf_op jit(solution)/shard_map/pair_products/pallas_call | solution.py:166
  36.0 0.0 copy-start
  36.0 1.4 %copy-done = bf16[64,144,128]{2,1,0:T(8,128)(2,1)} copy-done((bf16[64,144,128]{2,1,0:T(8,128)(2,1)}, bf16[64,144,128]{2,1,0:T(8,128)(2,1)S(1)}, u32[]{:S(2)}) %copy-start) | copy-done | bytes 2359320
  37.4 9.6 %all-to-all-done.got = bf16[64,56,128]{2,1,0:T(8,128)(2,1)S(1)} async-done(((bf16[64,56,128]{2,1,0:T(8,128)(2,1)}), bf16[64,56,128]{2,1,0:T(8,128)(2,1)S(1)}, u32[]{:S(2)}, u32[]{:S(2)}) %all-to-all-start) | async-done | bytes 917536 | tf_op jit(solution)/shard_map/all_to_all | solution.py:22
  47.0 5.4 %all-to-all-start.1 = ((bf16[64,144,128]{2,1,0:T(8,128)(2,1)}), bf16[64,144,128]{2,1,0:T(8,128)(2,1)S(1)}, u32[]{:S(2)}, u32[]{:S(2)}) async-start(bf16[64,144,128]{2,1,0:T(8,128)(2,1)} %copy-done), calls=%async_computation.1 | async-start | bytes 4718592 | tf_op jit(solution)/shard_map/all_to_all | solution.py:22
  52.4 0.1 fusion
  52.6 0.1 reshape.45.labels
  52.6 1.7 %own_sums.1.refs_0_ = f32[128,8,128]{2,1,0:T(8,128)S(1)} custom-call(s32[1536]{0:T(1024)S(1)} %reshape.45.labels, bf16[64,56,128]{2,1,0:T(8,128)(2,1)S(1)} %all-to-all-done.got), custom_call_target="tpu_custom_call" | custom-call | tf_op jit(solution)/shard_map/own_sums/pallas_call | solution.py:179
  54.4 0.0 copy-start.1
  54.4 0.8 copy-done.1
  55.2 28.1 %all-to-all-done.1.got = bf16[64,144,128]{2,1,0:T(8,128)(2,1)S(1)} async-done(((bf16[64,144,128]{2,1,0:T(8,128)(2,1)}), bf16[64,144,128]{2,1,0:T(8,128)(2,1)S(1)}, u32[]{:S(2)}, u32[]{:S(2)}) %all-to-all-start.1) | async-done | bytes 2359328 | tf_op jit(solution)/shard_map/all_to_all | solution.py:22
  83.3 0.0 copy-start.2
  83.3 1.0 copy-done.2
  84.3 3.4 %pair_sums.1 = bf16[1024,128]{1,0:T(8,128)(2,1)S(1)} custom-call(s32[1536]{0:T(1024)S(1)} %reshape.45.labels, bf16[64,144,128]{2,1,0:T(8,128)(2,1)S(1)} %all-to-all-done.1.got, f32[128,8,128]{2,1,0:T(8,128)S(1)} %copy-done.2), custom_call_target="tpu_custom_call" | custom-call | tf_op jit(solution)/shard_map/pair_sums/pallas_call | solution.py:188
  87.7 32.5 %all_to_all.19 = bf16[16,64,128]{2,1,0:T(8,128)(2,1)S(1)} all-to-all(bf16[16,64,128]{2,1,0:T(8,128)(2,1)S(1)} %bitcast.31), channel_id=1, replica_groups=mesh['tx'=16,'mp_hi'=8,'mp_lo'=2,'rep'=2] {'mp_hi','mp_lo'}, dimensions={0} | all-to-all | bytes 524288 | tf_op jit(solution)/shard_map/all_to_all | solution.py:22
  120.3 0.6 pad_maximum_fusion.1
  (15 shorter events, 0.2 us)
Async XLA Ops:
  0.0 32.4 %collective-permute-start.2 = (bf16[256,2048]{1,0:T(8,128)(2,1)}, bf16[256,2048]{1,0:T(8,128)(2,1)S(1)}, u32[]{:S(2)}, u32[]{:S(2)}) collective-permute-start(bf16[256,2048]{1,0:T(8,128)(2,1)} %bitcast.26), channel_id=1, source_target_pairs={{96,0},{64,32},{160,64},{128,96},{224,128},{192,160},{288,192},{25... | collective-permute-start | bytes 3145736 | tf_op jit(solution)/shard_map/ppermute | solution.py:136
  6.8 25.6 %collective-permute-start.3 = (bf16[256,2048]{1,0:T(8,128)(2,1)}, bf16[256,2048]{1,0:T(8,128)(2,1)}, u32[]{:S(2)}, u32[]{:S(2)}) collective-permute-start(bf16[256,2048]{1,0:T(8,128)(2,1)} %bitcast.27), channel_id=1, source_target_pairs={{128,32},{480,96},{256,160},{96,224},{384,288},{224,352},{0,416},{... | collective-permute-start | bytes 3145736 | tf_op jit(solution)/shard_map/ppermute | solution.py:137
  10.8 21.7 %collective-permute-start.4 = (bf16[256,2048]{1,0:T(8,128)(2,1)}, bf16[256,2048]{1,0:T(8,128)(2,1)}, u32[]{:S(2)}, u32[]{:S(2)}) collective-permute-start(bf16[256,2048]{1,0:T(8,128)(2,1)} %bitcast.28), channel_id=1, source_target_pairs={{32,0},{0,32},{96,64},{64,96},{160,128},{128,160},{224,192},{192,2... | collective-permute-start | bytes 3145736 | tf_op jit(solution)/shard_map/ppermute | solution.py:138
  14.4 17.4 %collective-permute-start.1 = (f32[268]{0:T(512)S(1)}, f32[268]{0:T(512)S(1)}, u32[]{:S(2)}, u32[]{:S(2)}) collective-permute-start(f32[268]{0:T(512)S(1)} %get-tuple-element.6), channel_id=1, source_target_pairs={{128,32},{480,96},{256,160},{96,224},{384,288},{224,352},{0,416},{... | collective-permute-start | bytes 3224 | tf_op jit(solution)/shard_map/ppermute | solution.py:145
  16.9 15.0 %collective-permute-start = (f32[268]{0:T(512)S(1)}, f32[268]{0:T(512)S(1)}, u32[]{:S(2)}, u32[]{:S(2)}) collective-permute-start(f32[268]{0:T(512)S(1)} %get-tuple-element.5), channel_id=1, source_target_pairs={{32,0},{0,32},{96,64},{64,96},{160,128},{128,160},{224,192},{192,2... | collective-permute-start | bytes 3224 | tf_op jit(solution)/shard_map/ppermute | solution.py:144
  20.3 1.2 %copy-start.3 = (bf16[1,256,2048]{2,1,0:T(8,128)(2,1)S(1)}, bf16[1,256,2048]{2,1,0:T(8,128)(2,1)}, u32[]{:S(2)}) copy-start(bf16[1,256,2048]{2,1,0:T(8,128)(2,1)} %param.5) | copy-start | bytes 3145732
  21.5 0.7 copy-start.5
  22.2 0.7 copy-start.7
  24.0 7.7 %copy-start.6 = (s32[1,1,24]{2,1,0:T(1,128)S(1)}, s32[1,1,24]{2,1,0:T(1,128)}, u32[]{:S(2)}) copy-start(s32[1,1,24]{2,1,0:T(1,128)} %param.7) | copy-start | bytes 292
  24.0 7.7 %copy-start.8 = (s32[1,1,24]{2,1,0:T(1,128)S(1)}, s32[1,1,24]{2,1,0:T(1,128)}, u32[]{:S(2)}) copy-start(s32[1,1,24]{2,1,0:T(1,128)} %param.8) | copy-start | bytes 292
  24.0 8.4 %copy-start.4 = (bf16[1,256,2048]{2,1,0:T(8,128)(2,1)S(1)}, bf16[1,256,2048]{2,1,0:T(8,128)(2,1)}, u32[]{:S(2)}) copy-start(bf16[1,256,2048]{2,1,0:T(8,128)(2,1)} %param.5) | copy-start | bytes 3145732
  25.0 22.0 %all-to-all-start = ((bf16[64,56,128]{2,1,0:T(8,128)(2,1)}), bf16[64,56,128]{2,1,0:T(8,128)(2,1)S(1)}, u32[]{:S(2)}, u32[]{:S(2)}) async-start(bf16[64,56,128]{2,1,0:T(8,128)(2,1)} %pad_maximum_fusion), calls=%async_computation | async-start | bytes 1835008 | tf_op jit(solution)/shard_map/all_to_all | solution.py:22
  36.0 1.4 %copy-start = (bf16[64,144,128]{2,1,0:T(8,128)(2,1)}, bf16[64,144,128]{2,1,0:T(8,128)(2,1)S(1)}, u32[]{:S(2)}) copy-start(bf16[64,144,128]{2,1,0:T(8,128)(2,1)S(1)} %pair_products.1) | copy-start | bytes 7077892
  47.0 36.2 %all-to-all-start.1 = ((bf16[64,144,128]{2,1,0:T(8,128)(2,1)}), bf16[64,144,128]{2,1,0:T(8,128)(2,1)S(1)}, u32[]{:S(2)}, u32[]{:S(2)}) async-start(bf16[64,144,128]{2,1,0:T(8,128)(2,1)} %copy-done), calls=%async_computation.1 | async-start | bytes 4718592 | tf_op jit(solution)/shard_map/all_to_all | solution.py:22
  54.4 0.8 copy-start.1
  83.3 1.0 copy-start.2

commit v5 on v2

v5 whole, which is shorter than its diff:
```python
import functools

import jax
import jax.numpy as jnp
from jax import lax
from jax.experimental import pallas as pl
from jax.experimental.pallas import tpu as pltpu
from jax.sharding import Mesh, PartitionSpec as P

BRICK = 256
STEPS = 4
LISTED = 6
PAIRS = STEPS * LISTED
TILES_DEV = 8
HALVES = 2
COST = 10**11
GROUP = ("mp_lo", "tx", "rep")
OWNERS = ("mp_hi", "mp_lo")


def exchanged(block, axis):
    return lax.all_to_all(block, axis, split_axis=0, concat_axis=0, tiled=True)


def routes(devices):
    everyone = range(devices)
    swap = [(i ^ 1, i) for i in everyone]
    near = [((i + (1 if i % 2 else 3)) % devices, i) for i in everyone]
    far = [((i + (3 if i % 4 == 1 else -4)) % devices, i) for i in everyone if i % 2]
    return swap, near, far


def column(row):
    return jnp.broadcast_to(row, (BRICK, row.shape[1])).T


def column(row):
    return jnp.broadcast_to(row, (BRICK, row.shape[1])).T


def add_tiles(left_ids, right_ids, weight, left_block, right_block, out, slot, then=None):
    parts = out.shape[0]
    half = parts // HALVES
    slab = BRICK // half
    width = BRICK // HALVES

    def brick(block, index):
        return block[:, pl.ds(pl.multiple_of(index * BRICK, BRICK), BRICK)]

    for first in range(0, LISTED, 2):
        pair = []
        for entry in (first, first + 1):
            left = brick(left_block, left_ids(entry)).astype(jnp.float32) * weight
            tile = lax.dot_general(
                left.astype(jnp.bfloat16),
                brick(right_block, right_ids(entry)),
                (((0,), (0,)), ((), ())),
                preferred_element_type=jnp.float32,
            )
            pair.append(tile.reshape(half, slab, BRICK))
        both = jnp.concatenate(pair, axis=1).astype(jnp.bfloat16)
        row = (slot * LISTED + first) * slab
        for side in range(HALVES):
            out[side * half : (side + 1) * half, row : row + 2 * slab, :] = both[
                :, :, side * width : (side + 1) * width
            ]
        if then is not None:
            then(row, 2 * slab)


def fetched(pairs, sems):
    copies = [pltpu.make_async_copy(src, dst, sems.at[i]) for i, (src, dst) in enumerate(pairs)]
    for copy in copies:
        copy.start()
    return copies


def own_kernel(*refs):
    place, left_hbm, right_hbm, targets_hbm, coupling_hbm, whole, out, own, *metas = refs[:11]
    left_ids, right_ids, lists, targets, coupling, numbers, sems = refs[11:]
    pairs = (
        (left_hbm, left_ids),
        (right_hbm, right_ids),
        (left_hbm, lists.at[0]),
        (right_hbm, lists.at[1]),
        (targets_hbm, targets),
        (coupling_hbm, coupling),
        (whole.at[0], own),
    )
    for copy in fetched(pairs, sems):
        copy.wait()
    rows = own.shape[0]
    for step, meta in enumerate(metas, 1):
        here = slice(step * LISTED, (step + 1) * LISTED)
        meta[...] = jnp.zeros_like(meta)
        meta[0:1, 0:rows] = coupling[step]
        for side in range(2):
            first = rows + side * LISTED
            meta[0:1, first : first + LISTED] = lists[side, 0, :, here].astype(jnp.float32)
    even = place[0] % 2 == 0
    numbers[...] = jnp.zeros_like(numbers)
    for slot, other in enumerate((0, 3, 2, 1)):
        these, those = (targets[0, :, i * LISTED : (i + 1) * LISTED] for i in (slot, other))
        here = slice(slot * LISTED, (slot + 1) * LISTED)
        numbers[0:1, here] = jnp.where(even, those, these).astype(jnp.float32)
    slab = numbers.shape[0]
    below = jnp.broadcast_to(numbers[...].astype(jnp.bfloat16)[None], (out.shape[0],) + numbers.shape)
    out[:, 2 * LISTED * slab :, :] = below
    add_tiles(lambda i: left_ids[0, 0, i], lambda i: right_ids[0, 0, i], column(coupling[0]), own, own, out, 0)


def pair_of(metas, lists, slot, rows, *blocks_and_out):
    first = slot * 2 * LISTED
    weight = column(metas[slot : slot + 1, 0:rows])
    return (lambda i: lists[first + i], lambda i: lists[first + LISTED + i], weight) + blocks_and_out


def last_kernel(lists, metas, own, far, swapped, _, out, stage, sems):
    rows = own.shape[0]
    height = stage.shape[1]
    spot = lists[2 * LISTED]

    def run(left_block, right_block):
        copies = []

        def send(row, size):
            part = stage.at[:, pl.ds(row, size), :]
            copies.append(
                pltpu.make_async_copy(part, out.at[:, pl.ds(height + row, size), :], sems.at[len(copies)])
            )
            copies[-1].start()

        add_tiles(*pair_of(metas, lists, 0, rows, left_block, right_block, stage, 0), send)
        for copy in copies:
            copy.wait()

    pl.when(spot % 2 == 0)(lambda: run(own, swapped))
    pl.when(spot == 1)(lambda: run(own, far))
    pl.when(spot == 3)(lambda: run(far, swapped))


def near_kernel(lists, metas, whole, swapped, near, out, own, sems):
    (load,) = fetched([(whole.at[0], own)], sems)
    rows = own.shape[0]
    add_tiles(*pair_of(metas, lists, 1, rows, swapped, near, out, 1))
    load.wait()
    add_tiles(*pair_of(metas, lists, 0, rows, own, near, out, 0))


def add_up(labels, starts, got, part, totals):
    slab = totals[0].shape[1]
    for slot, start in enumerate(starts):
        for first in range(0, LISTED, 2):
            row = (slot * LISTED + first) * slab
            both = got[part, row : row + 2 * slab, :].astype(jnp.float32)
            for side in range(2):
                total = totals[first + side]
                total[labels[start + first + side]] += both[side * slab : (side + 1) * slab]


def together(totals):
    return functools.reduce(lambda a, b: a + b, [total[...] for total in totals])


def first_sum_kernel(subsets, labels, got, out, *totals):
    parts = got.shape[0]
    plane = parts // HALVES
    for total in totals:
        total[...] = jnp.zeros_like(total)

    def one_part(part, carry):
        earlier = jnp.where(part % plane < 4 * subsets, part + plane - 4 * subsets, part - 4 * subsets)
        lister = jnp.where(part // subsets % 4 == 3, earlier, part)
        add_up(labels, [part * PAIRS, lister * PAIRS + 3 * LISTED], got, part, totals)
        return carry

    lax.fori_loop(0, parts, one_part, 0)
    out[...] = together(totals)


def near_sum_kernel(subsets, labels, got, before, out, held, sems, *totals):
    (load,) = fetched([(before, held)], sems)
    for total in totals:
        total[...] = jnp.zeros_like(total)

    def one_part(part, carry):
        lister = part + jnp.where(part // subsets % 2 == 0, subsets, -subsets)
        add_up(labels, [part * PAIRS + LISTED, lister * PAIRS + 2 * LISTED], got, part, totals)
        return carry

    lax.fori_loop(0, got.shape[0], one_part, 0)
    load.wait()
    out[...] = together((held,) + totals).reshape(out.shape).astype(out.dtype)


def body(jacobian, coupling, brick_left, brick_right, tile_target):
    rows = jacobian.shape[1]
    devices = lax.axis_size("tx")
    subsets = lax.axis_size("rep")
    swap, near, far = routes(devices)
    parts = devices * subsets * HALVES
    owners = lax.axis_size("mp_hi") * lax.axis_size("mp_lo")
    slab = BRICK // (parts // HALVES)
    width = BRICK // HALVES
    tiles = owners * TILES_DEV
    smem = pl.BlockSpec(memory_space=pltpu.SMEM)
    vmem = pl.BlockSpec(memory_space=pltpu.VMEM)
    hbm = pl.BlockSpec(memory_space=pl.ANY)
    params = pltpu.CompilerParams(vmem_limit_bytes=24 * 2**20)
    args = [pltpu.with_memory_space_constraint(x, pltpu.HBM) for x in (brick_left, brick_right, tile_target, coupling)]
    whole = pltpu.with_memory_space_constraint(jacobian, pltpu.HBM)
    held = pltpu.VMEM(jacobian.shape[1:], jacobian.dtype)
    copied = pltpu.SemaphoreType.DMA

    swapped_block = lax.ppermute(jacobian[0], "tx", swap)
    far_block = lax.ppermute(jacobian[0], "tx", far)
    near_block = lax.ppermute(jacobian[0], "tx", near)
    place = lax.axis_index("tx") & 3
    spot = place.reshape(1).astype(jnp.int32)

    first = pltpu.HBM((parts, (2 * LISTED + 1) * slab, width), jnp.bfloat16)
    stage = pltpu.VMEM((parts, LISTED * slab, width), jnp.bfloat16)
    meta = jax.ShapeDtypeStruct((1, rows + width), jnp.float32)
    buffer, own, of_one, of_two, of_three = pl.pallas_call(
        own_kernel,
        out_shape=(first, held, meta, meta, meta),
        in_specs=[smem] + [hbm] * 5,
        out_specs=[vmem] * 5,
        scratch_shapes=[
            pltpu.SMEM(brick_left.shape, jnp.int32),
            pltpu.SMEM(brick_right.shape, jnp.int32),
            pltpu.VMEM((2,) + brick_left.shape, jnp.int32),
            pltpu.VMEM(tile_target.shape, jnp.int32),
            pltpu.VMEM(coupling.shape, coupling.dtype),
            pltpu.VMEM((slab, width), jnp.float32),
            copied((7,)),
        ],
        compiler_params=params,
        name="own_products",
    )(spot, *args, whole)
    of_far = lax.ppermute(of_three, "tx", far)
    of_swapped = lax.ppermute(of_two, "tx", swap)
    even = place % 2 == 0

    def listed(metas):
        return metas[:, rows : rows + 2 * LISTED].astype(jnp.int32).reshape(-1)

    last = jnp.where(even, of_one, jnp.where(place == 1, of_three, of_far))
    buffer = pl.pallas_call(
        last_kernel,
        out_shape=first,
        in_specs=[smem] + [vmem] * 4 + [hbm],
        out_specs=hbm,
        scratch_shapes=[stage, copied((LISTED // 2,))],
        input_output_aliases={5: 0},
        compiler_params=params,
        name="last_products",
    )(jnp.concatenate([listed(last), spot]), last, own, far_block, swapped_block, buffer)
    got = exchanged(buffer, GROUP)
    labels = got[:, 2 * LISTED * slab, :PAIRS].astype(jnp.int32).reshape(-1)

    metas = jnp.concatenate([jnp.where(even, of_three, of_one), of_swapped], axis=0)
    second = pl.pallas_call(
        near_kernel,
        out_shape=jax.ShapeDtypeStruct((parts, 2 * LISTED * slab, width), jnp.bfloat16),
        in_specs=[smem, vmem, hbm, vmem, vmem],
        out_specs=vmem,
        scratch_shapes=[held, copied((1,))],
        compiler_params=params,
        cost_estimate=pl.CostEstimate(flops=COST, bytes_accessed=2**23, transcendentals=0),
        name="near_products",
    )(listed(metas), metas, whole, swapped_block, near_block)
    second = exchanged(second, GROUP)

    chains = [pltpu.VMEM((tiles, slab, width), jnp.float32) for _ in range(LISTED)]
    sums = pl.pallas_call(
        functools.partial(first_sum_kernel, subsets),
        out_shape=jax.ShapeDtypeStruct((tiles, slab, width), jnp.float32),
        in_specs=[smem, vmem],
        out_specs=vmem,
        scratch_shapes=chains,
        compiler_params=params,
        name="first_sums",
    )(labels, got)
    sums = pl.pallas_call(
        functools.partial(near_sum_kernel, subsets),
        out_shape=jax.ShapeDtypeStruct((tiles * slab, width), jnp.bfloat16),
        in_specs=[smem, vmem, hbm],
        out_specs=vmem,
        scratch_shapes=[chains[0], copied((1,))] + chains,
        compiler_params=params,
        name="near_sums",
    )(labels, second, pltpu.with_memory_space_constraint(sums, pltpu.HBM))
    sums = exchanged(sums, OWNERS).reshape(owners // HALVES, HALVES, TILES_DEV, slab, width)
    sums = jnp.sum(sums.astype(jnp.float32), axis=0)
    return jnp.concatenate([sums[side] for side in range(HALVES)], axis=-1)


def solution(mesh):
    shape = (mesh.shape["tx"], mesh.shape["mp"] // HALVES, HALVES, mesh.shape["rep"])
    mesh = Mesh(mesh.devices.reshape(shape), ("tx", "mp_hi", "mp_lo", "rep"))
    data = ("mp_hi", "mp_lo", "rep")
    in_specs = (
        P("tx", data, None),
        P(None, "tx", data),
        P("tx", data, None),
        P("tx", data, None),
        P("tx", data, None),
    )
    out_specs = P(OWNERS, ("tx", "rep"), None)
    return jax.shard_map(body, mesh=mesh, in_specs=in_specs, out_specs=out_specs, check_vma=False)
```

time: 128 us -> 121 us (0.945)
  starting transfers between devices: 33.2 us -> 28.2 us
  Pallas kernels: 9.19 us -> 13.8 us
  other arithmetic: 3.8 us -> 0.89 us
  local copies, waits for them, and re-layouts: 6.21 us -> 4.26 us
  waiting for transfers between devices: 41.6 us -> 40.2 us
    all_to_all x2, waiting for transfers between devices: 38.8 us -> 32.8 us  [exchanged(): return lax.all_to_all(block, axis, split_axis=0, concat_axis=0, tiled=True)]
    ppermute x5, waiting for transfers between devices: 2.81 us -> 7.47 us  [the longest x1 6.37 us: body(): near_block = lax.ppermute(jacobian[0], 'tx', near)]
    pallas_call x2 -> x5, Pallas kernels: 9.19 us -> 13.8 us  [the longest x1 3.2 us: body(): pl.pallas_call(near_kernel, out_shape=jax.ShapeDtypeStruct((parts, 2 * LI...]
    all_to_all x2, starting transfers between devices: 18.2 us -> 13.7 us  [exchanged(): return lax.all_to_all(block, axis, split_axis=0, concat_axis=0, tiled=True)]
    unnamed x2 -> x0, other arithmetic: 2.43 us -> none
    broadcast_in_dim x1 -> x0, local copies, waits for them, and re-layouts: 1.29 us -> none  [body(): labels = exchanged(jnp.broadcast_to(tile_target[0], (parts, PAIRS)), GROUP)]
    unnamed x7 -> x8, local copies, waits for them, and re-layouts: 2.9 us -> 4.09 us
  transfers between devices with their start and end apart: 7 -> 7, of which waited for: 2 -> 5; matrix products, arithmetic and copies ran while one was open for 5% -> 0% of each run, Pallas kernels for 3% -> 9%
where the time goes in v5:
time: 121 us
  waiting for transfers between devices  40.2 us (33%)
  blocking collectives  33 us (27%)
  starting transfers between devices  28.2 us (23%)
  Pallas kernels  13.8 us (11%)
  local copies, waits for them, and re-layouts  4.26 us (4%)
    all_to_all x1, blocking collectives, exchanged(): return lax.all_to_all(block, axis, split_axis=0, concat_axis=0, tiled=True)  33 us
    all_to_all x2, waiting for transfers between devices, exchanged(): return lax.all_to_all(block, axis, split_axis=0, concat_axis=0, tiled=True)  32.8 us
    all_to_all x2, starting transfers between devices, exchanged(): return lax.all_to_all(block, axis, split_axis=0, concat_axis=0, tiled=True)  13.7 us
    ppermute x1, waiting for transfers between devices, body(): near_block = lax.ppermute(jacobian[0], 'tx', near)  6.37 us
    ppermute x1, starting transfers between devices, body(): far_block = lax.ppermute(jacobian[0], 'tx', far)  5.09 us
    ppermute x1, starting transfers between devices, body(): near_block = lax.ppermute(jacobian[0], 'tx', near)  4.32 us
    unnamed x8, local copies, waits for them, and re-layouts  4.09 us
    pallas_call x1, Pallas kernels, body(): pl.pallas_call(near_kernel, out_shape=jax.ShapeDtypeStruct((parts, 2 * LI...  3.2 us
  transfers between devices with their start and end apart: 7, of which 5 were waited for; matrix products, arithmetic and copies ran while one was open for 0% of the time, Pallas kernels for 9%

profile of v5, /device:TPU:32, one launch (start us, length us, event | category | flops | bytes accessed | tf_op | source)
XLA Modules:
  0.0 120.6 jit_solution(11270461672152368362)
XLA Ops:
  0.0 1.9 %collective-permute-start.2 = (bf16[256,2048]{1,0:T(8,128)(2,1)}, bf16[256,2048]{1,0:T(8,128)(2,1)S(1)}, u32[]{:S(2)}, u32[]{:S(2)}) collective-permute-start(bf16[256,2048]{1,0:T(8,128)(2,1)} %bitcast.13), channel_id=1, source_target_pairs={{32,0},{0,32},{96,64},{64,96},{160,128},{128,160},{224,192},{192,2... | collective-permute-start | bytes 3145736 | tf_op jit(solution)/shard_map/ppermute | solution.py:215
  1.9 5.1 %collective-permute-start.1 = (bf16[256,2048]{1,0:T(8,128)(2,1)}, bf16[256,2048]{1,0:T(8,128)(2,1)S(1)}, u32[]{:S(2)}, u32[]{:S(2)}) collective-permute-start(bf16[256,2048]{1,0:T(8,128)(2,1)} %bitcast.14), channel_id=1, source_target_pairs={{128,32},{480,96},{256,160},{96,224},{384,288},{224,352},{0,416},{... | collective-permute-start | bytes 3145736 | tf_op jit(solution)/shard_map/ppermute | solution.py:216
  7.0 4.3 %collective-permute-start.4 = (bf16[256,2048]{1,0:T(8,128)(2,1)}, bf16[256,2048]{1,0:T(8,128)(2,1)}, u32[]{:S(2)}, u32[]{:S(2)}) collective-permute-start(bf16[256,2048]{1,0:T(8,128)(2,1)} %bitcast.15), channel_id=1, source_target_pairs={{96,0},{64,32},{160,64},{128,96},{224,128},{192,160},{288,192},{25... | collective-permute-start | bytes 3145736 | tf_op jit(solution)/shard_map/ppermute | solution.py:217
  11.4 3.2 %own_products.1 = (bf16[64,104,128]{2,1,0:T(8,128)(2,1)}, bf16[256,2048]{1,0:T(8,128)(2,1)S(1)}, f32[1,384]{1,0:T(1,128)S(1)}, f32[1,384]{1,0:T(1,128)S(1)}, f32[1,384]{1,0:T(1,128)S(1)}) custom-call(s32[1]{0:T(128)} %bitcast.refs_0_, s32[1,1,24]{2,1,0:T(1,128)} %refs_1_.1, s32[1,1,24]{2,1,0:T(1,128)} %refs_2_.1, s32[1,1,24]{2,1,0:T(1,128)} %refs_3_.1, ...), custom_call_target="tpu_custom_call" | custom-call | tf_op jit(solution)/shard_map/own_products/pallas_call | solution.py:224
  14.5 0.0 copy-start.2
  14.5 1.0 copy-done.2
  15.5 1.3 %collective-permute-start = (f32[1,384]{1,0:T(1,128)S(1)}, f32[1,384]{1,0:T(1,128)S(1)}, u32[]{:S(2)}, u32[]{:S(2)}) collective-permute-start(f32[1,384]{1,0:T(1,128)S(1)} %get-tuple-element.11), channel_id=1, source_target_pairs={{128,32},{480,96},{256,160},{96,224},{384,288},{224,352},{0,416},{... | collective-permute-start | bytes 4616 | tf_op jit(solution)/shard_map/ppermute | solution.py:241
  16.8 1.9 %collective-permute-start.3 = (f32[1,384]{1,0:T(1,128)S(1)}, f32[1,384]{1,0:T(1,128)S(1)}, u32[]{:S(2)}, u32[]{:S(2)}) collective-permute-start(f32[1,384]{1,0:T(1,128)S(1)} %get-tuple-element.14), channel_id=1, source_target_pairs={{32,0},{0,32},{96,64},{64,96},{160,128},{128,160},{224,192},{192,2... | collective-permute-start | bytes 4616 | tf_op jit(solution)/shard_map/ppermute | solution.py:242
  18.7 0.8 collective-permute-done
  19.6 0.3 collective-permute-done.3
  19.8 0.1 reshape.21.lists
  19.9 0.1 pad_add_fusion.lists
  20.0 0.0 collective-permute-done.2.swapped
  20.0 0.0 collective-permute-done.1.far
  20.0 0.0 copy-start.3
  20.0 1.2 %copy-done.3 = bf16[256,2048]{1,0:T(8,128)(2,1)S(1)} copy-done((bf16[256,2048]{1,0:T(8,128)(2,1)S(1)}, bf16[256,2048]{1,0:T(8,128)(2,1)}, u32[]{:S(2)}) %copy-start.3) | copy-done | bytes 1048600
  21.3 2.0 %last_products.1 = bf16[64,104,128]{2,1,0:T(8,128)(2,1)} custom-call(s32[13]{0:T(128)S(1)} %pad_add_fusion.lists, f32[1,384]{1,0:T(1,128)S(1)} %get-tuple-element.18.metas, bf16[256,2048]{1,0:T(8,128)(2,1)S(1)} %copy-done.3, bf16[256,2048]{1,0:T(8,128)(2,1)S(1)} %collective-permute-done.1.far, ...), custom_call_target="tpu_custom_call", output_to_operand_aliasing={{}: (5, {})} | custom-call | tf_op jit(solution)/shard_map/last_products/pallas_call | solution.py:249
  23.2 8.0 %all-to-all-start = ((bf16[64,104,128]{2,1,0:T(8,128)(2,1)}), bf16[64,104,128]{2,1,0:T(8,128)(2,1)S(1)}, u32[]{:S(2)}, u32[]{:S(2)}) async-start(bf16[64,104,128]{2,1,0:T(8,128)(2,1)} %last_products.1), calls=%async_computation | async-start | bytes 3407872 | tf_op jit(solution)/shard_map/all_to_all | solution.py:22
  31.2 6.4 %collective-permute-done.4.near = bf16[256,2048]{1,0:T(8,128)(2,1)} collective-permute-done((bf16[256,2048]{1,0:T(8,128)(2,1)}, bf16[256,2048]{1,0:T(8,128)(2,1)}, u32[]{:S(2)}, u32[]{:S(2)}) %collective-permute-start.4) | collective-permute-done | bytes 1048608 | tf_op jit(solution)/shard_map/ppermute | solution.py:217
  37.6 3.2 %near_products.1 = bf16[64,96,128]{2,1,0:T(8,128)(2,1)S(1)} custom-call(s32[24]{0:T(128)S(1)} %reshape.21.lists, f32[2,384]{1,0:T(2,128)S(1)} %pad_maximum_fusion.1.metas, bf16[1,256,2048]{2,1,0:T(8,128)(2,1)} %whole.1, bf16[256,2048]{1,0:T(8,128)(2,1)S(1)} %collective-permute-done.2.swapped, bf16[256,2048]{1,0:T(8,128)(2,1)} %collective-permute-done.4.near), custom_call_target="tpu_custom_call" | custom-call | flops 99999997952 | bytes 8388608 | tf_op jit(solution)/shard_map/near_products/pallas_call | solution.py:263
  40.8 0.0 copy-start.1
  40.8 1.1 copy-done.1
  41.9 13.6 %all-to-all-done.got = bf16[64,104,128]{2,1,0:T(8,128)(2,1)S(1)} async-done(((bf16[64,104,128]{2,1,0:T(8,128)(2,1)}), bf16[64,104,128]{2,1,0:T(8,128)(2,1)S(1)}, u32[]{:S(2)}, u32[]{:S(2)}) %all-to-all-start) | async-done | bytes 1703968 | tf_op jit(solution)/shard_map/all_to_all | solution.py:22
  55.5 5.7 %all-to-all-start.1 = ((bf16[64,96,128]{2,1,0:T(8,128)(2,1)}), bf16[64,96,128]{2,1,0:T(8,128)(2,1)S(1)}, u32[]{:S(2)}, u32[]{:S(2)}) async-start(bf16[64,96,128]{2,1,0:T(8,128)(2,1)} %copy-done.1), calls=%async_computation.1 | async-start | bytes 3145728 | tf_op jit(solution)/shard_map/all_to_all | solution.py:22
  61.3 0.1 fusion
  61.4 0.1 reshape.22.labels
  61.5 2.8 %first_sums.1.before = f32[128,8,128]{2,1,0:T(8,128)S(1)} custom-call(s32[1536]{0:T(1024)S(1)} %reshape.22.labels, bf16[64,104,128]{2,1,0:T(8,128)(2,1)S(1)} %all-to-all-done.got), custom_call_target="tpu_custom_call" | custom-call | tf_op jit(solution)/shard_map/first_sums/pallas_call | solution.py:276
  64.2 0.0 copy-start
  64.2 0.8 copy-done
  65.0 19.2 %all-to-all-done.1.got = bf16[64,96,128]{2,1,0:T(8,128)(2,1)S(1)} async-done(((bf16[64,96,128]{2,1,0:T(8,128)(2,1)}), bf16[64,96,128]{2,1,0:T(8,128)(2,1)S(1)}, u32[]{:S(2)}, u32[]{:S(2)}) %all-to-all-start.1) | async-done | bytes 1572896 | tf_op jit(solution)/shard_map/all_to_all | solution.py:22
  84.2 2.7 %near_sums.1 = bf16[1024,128]{1,0:T(8,128)(2,1)S(1)} custom-call(s32[1536]{0:T(1024)S(1)} %reshape.22.labels, bf16[64,96,128]{2,1,0:T(8,128)(2,1)S(1)} %all-to-all-done.1.got, f32[128,8,128]{2,1,0:T(8,128)} %copy-done), custom_call_target="tpu_custom_call" | custom-call | tf_op jit(solution)/shard_map/near_sums/pallas_call | solution.py:285
  86.9 33.0 %all_to_all.19 = bf16[16,64,128]{2,1,0:T(8,128)(2,1)S(1)} all-to-all(bf16[16,64,128]{2,1,0:T(8,128)(2,1)S(1)} %bitcast.11), channel_id=1, replica_groups=mesh['tx'=16,'mp_hi'=8,'mp_lo'=2,'rep'=2] {'mp_hi','mp_lo'}, dimensions={0} | all-to-all | bytes 524288 | tf_op jit(solution)/shard_map/all_to_all | solution.py:22
  120.0 0.6 pad_maximum_fusion
  (6 shorter events, 0.1 us)
Async XLA Ops:
  0.0 20.0 %collective-permute-start.2 = (bf16[256,2048]{1,0:T(8,128)(2,1)}, bf16[256,2048]{1,0:T(8,128)(2,1)S(1)}, u32[]{:S(2)}, u32[]{:S(2)}) collective-permute-start(bf16[256,2048]{1,0:T(8,128)(2,1)} %bitcast.13), channel_id=1, source_target_pairs={{32,0},{0,32},{96,64},{64,96},{160,128},{128,160},{224,192},{192,2... | collective-permute-start | bytes 3145736 | tf_op jit(solution)/shard_map/ppermute | solution.py:215
  1.9 18.1 %collective-permute-start.1 = (bf16[256,2048]{1,0:T(8,128)(2,1)}, bf16[256,2048]{1,0:T(8,128)(2,1)S(1)}, u32[]{:S(2)}, u32[]{:S(2)}) collective-permute-start(bf16[256,2048]{1,0:T(8,128)(2,1)} %bitcast.14), channel_id=1, source_target_pairs={{128,32},{480,96},{256,160},{96,224},{384,288},{224,352},{0,416},{... | collective-permute-start | bytes 3145736 | tf_op jit(solution)/shard_map/ppermute | solution.py:216
  7.0 30.6 %collective-permute-start.4 = (bf16[256,2048]{1,0:T(8,128)(2,1)}, bf16[256,2048]{1,0:T(8,128)(2,1)}, u32[]{:S(2)}, u32[]{:S(2)}) collective-permute-start(bf16[256,2048]{1,0:T(8,128)(2,1)} %bitcast.15), channel_id=1, source_target_pairs={{96,0},{64,32},{160,64},{128,96},{224,128},{192,160},{288,192},{25... | collective-permute-start | bytes 3145736 | tf_op jit(solution)/shard_map/ppermute | solution.py:217
  14.5 1.0 copy-start.2
  15.5 4.1 %collective-permute-start = (f32[1,384]{1,0:T(1,128)S(1)}, f32[1,384]{1,0:T(1,128)S(1)}, u32[]{:S(2)}, u32[]{:S(2)}) collective-permute-start(f32[1,384]{1,0:T(1,128)S(1)} %get-tuple-element.11), channel_id=1, source_target_pairs={{128,32},{480,96},{256,160},{96,224},{384,288},{224,352},{0,416},{... | collective-permute-start | bytes 4616 | tf_op jit(solution)/shard_map/ppermute | solution.py:241
  16.8 3.0 %collective-permute-start.3 = (f32[1,384]{1,0:T(1,128)S(1)}, f32[1,384]{1,0:T(1,128)S(1)}, u32[]{:S(2)}, u32[]{:S(2)}) collective-permute-start(f32[1,384]{1,0:T(1,128)S(1)} %get-tuple-element.14), channel_id=1, source_target_pairs={{32,0},{0,32},{96,64},{64,96},{160,128},{128,160},{224,192},{192,2... | collective-permute-start | bytes 4616 | tf_op jit(solution)/shard_map/ppermute | solution.py:242
  20.0 1.2 %copy-start.3 = (bf16[256,2048]{1,0:T(8,128)(2,1)S(1)}, bf16[256,2048]{1,0:T(8,128)(2,1)}, u32[]{:S(2)}) copy-start(bf16[256,2048]{1,0:T(8,128)(2,1)} %copy-done.2) | copy-start | bytes 3145732
  23.2 32.3 %all-to-all-start = ((bf16[64,104,128]{2,1,0:T(8,128)(2,1)}), bf16[64,104,128]{2,1,0:T(8,128)(2,1)S(1)}, u32[]{:S(2)}, u32[]{:S(2)}) async-start(bf16[64,104,128]{2,1,0:T(8,128)(2,1)} %last_products.1), calls=%async_computation | async-start | bytes 3407872 | tf_op jit(solution)/shard_map/all_to_all | solution.py:22
  40.8 1.1 copy-start.1
  55.5 28.6 %all-to-all-start.1 = ((bf16[64,96,128]{2,1,0:T(8,128)(2,1)}), bf16[64,96,128]{2,1,0:T(8,128)(2,1)S(1)}, u32[]{:S(2)}, u32[]{:S(2)}) async-start(bf16[64,96,128]{2,1,0:T(8,128)(2,1)} %copy-done.1), calls=%async_computation.1 | async-start | bytes 3145728 | tf_op jit(solution)/shard_map/all_to_all | solution.py:22
  64.2 0.8 copy-start

commit v6 on v5

--- a/solution.py
+++ b/solution.py
@@ -14,6 +14,7 @@
 TILES_DEV = 8
 HALVES = 2
 COST = 10**11
+TAIL = 16
 GROUP = ("mp_lo", "tx", "rep")
 OWNERS = ("mp_hi", "mp_lo")
 
@@ -45,7 +46,11 @@
     width = BRICK // HALVES
 
     def brick(block, index):
-        return block[:, pl.ds(pl.multiple_of(index * BRICK, BRICK), BRICK)]
+        columns = pl.ds(pl.multiple_of(index * BRICK, BRICK), BRICK)
+        if not isinstance(block, tuple):
+            return block[:, columns]
+        top, tail = block
+        return jnp.concatenate([top[:, columns], tail[0:TAIL, columns].astype(jnp.bfloat16)], axis=0)
 
     for first in range(0, LISTED, 2):
         pair = []
@@ -76,8 +81,8 @@
 
 
 def own_kernel(*refs):
-    place, left_hbm, right_hbm, targets_hbm, coupling_hbm, whole, out, own, *metas = refs[:11]
-    left_ids, right_ids, lists, targets, coupling, numbers, sems = refs[11:]
+    place, left_hbm, right_hbm, targets_hbm, coupling_hbm, whole, out, own, top, *metas = refs[:12]
+    left_ids, right_ids, lists, targets, coupling, numbers, sems = refs[12:]
     pairs = (
         (left_hbm, left_ids),
         (right_hbm, right_ids),
@@ -90,13 +95,17 @@
     for copy in fetched(pairs, sems):
         copy.wait()
     rows = own.shape[0]
+    top[...] = own[: rows - TAIL, :]
     for step, meta in enumerate(metas, 1):
         here = slice(step * LISTED, (step + 1) * LISTED)
         meta[...] = jnp.zeros_like(meta)
-        meta[0:1, 0:rows] = coupling[step]
+        row = meta.shape[0] // (TAIL + 8) * TAIL
+        if row > 0:
+            meta[0:row, :] = own[rows - row :, :].astype(jnp.float32)
+        meta[row : row + 1, 0:rows] = coupling[step]
         for side in range(2):
             first = rows + side * LISTED
-            meta[0:1, first : first + LISTED] = lists[side, 0, :, here].astype(jnp.float32)
+            meta[row : row + 1, first : first + LISTED] = lists[side, 0, :, here].astype(jnp.float32)
     even = place[0] % 2 == 0
     numbers[...] = jnp.zeros_like(numbers)
     for slot, other in enumerate((0, 3, 2, 1)):
@@ -115,7 +124,8 @@
     return (lambda i: lists[first + i], lambda i: lists[first + LISTED + i], weight) + blocks_and_out
 
 
-def last_kernel(lists, metas, own, far, swapped, _, out, stage, sems):
+def last_kernel(lists, metas, own, *refs):
+    far, swapped, (_, out, stage, sems) = refs[0], refs[1:3], refs[3:]
     rows = own.shape[0]
     height = stage.shape[1]
     spot = lists[2 * LISTED]
@@ -139,7 +149,8 @@
     pl.when(spot == 3)(lambda: run(far, swapped))
 
 
-def near_kernel(lists, metas, whole, swapped, near, out, own, sems):
+def near_kernel(lists, metas, whole, top, tail, near, out, own, sems):
+    swapped = (top, tail)
     (load,) = fetched([(whole.at[0], own)], sems)
     rows = own.shape[0]
     add_tiles(*pair_of(metas, lists, 1, rows, swapped, near, out, 1))
@@ -212,20 +223,27 @@
     held = pltpu.VMEM(jacobian.shape[1:], jacobian.dtype)
     copied = pltpu.SemaphoreType.DMA
 
-    swapped_block = lax.ppermute(jacobian[0], "tx", swap)
+    near_block = lax.ppermute(jacobian[0], "tx", near)
     far_block = lax.ppermute(jacobian[0], "tx", far)
-    near_block = lax.ppermute(jacobian[0], "tx", near)
     place = lax.axis_index("tx") & 3
     spot = place.reshape(1).astype(jnp.int32)
 
     first = pltpu.HBM((parts, (2 * LISTED + 1) * slab, width), jnp.bfloat16)
     stage = pltpu.VMEM((parts, LISTED * slab, width), jnp.bfloat16)
     meta = jax.ShapeDtypeStruct((1, rows + width), jnp.float32)
-    buffer, own, of_one, of_two, of_three = pl.pallas_call(
+    tall = jax.ShapeDtypeStruct((TAIL + 8, jacobian.shape[2]), jnp.float32)
+    buffer, own, top, of_one, of_two, of_three = pl.pallas_call(
         own_kernel,
-        out_shape=(first, held, meta, meta, meta),
+        out_shape=(
+            first,
+            held,
+            jax.ShapeDtypeStruct((rows - TAIL, jacobian.shape[2]), jacobian.dtype),
+            meta,
+            tall,
+            meta,
+        ),
         in_specs=[smem] + [hbm] * 5,
-        out_specs=[vmem] * 5,
+        out_specs=[vmem] * 6,
         scratch_shapes=[
             pltpu.SMEM(brick_left.shape, jnp.int32),
             pltpu.SMEM(brick_right.shape, jnp.int32),
@@ -238,9 +256,13 @@
         compiler_params=params,
         name="own_products",
     )(spot, *args, whole)
+    swapped_top = lax.ppermute(top, "tx", swap)
     of_far = lax.ppermute(of_three, "tx", far)
     of_swapped = lax.ppermute(of_two, "tx", swap)
     even = place % 2 == 0
+
+    def meta_row(tail):
+        return tail[TAIL : TAIL + 1, : rows + width]
 
     def listed(metas):
         return metas[:, rows : rows + 2 * LISTED].astype(jnp.int32).reshape(-1)
@@ -249,27 +271,27 @@
     buffer = pl.pallas_call(
         last_kernel,
         out_shape=first,
-        in_specs=[smem] + [vmem] * 4 + [hbm],
+        in_specs=[smem] + [vmem] * 5 + [hbm],
         out_specs=hbm,
         scratch_shapes=[stage, copied((LISTED // 2,))],
-        input_output_aliases={5: 0},
+        input_output_aliases={6: 0},
         compiler_params=params,
         name="last_products",
-    )(jnp.concatenate([listed(last), spot]), last, own, far_block, swapped_block, buffer)
+    )(jnp.concatenate([listed(last), spot]), last, own, far_block, swapped_top, of_swapped, buffer)
     got = exchanged(buffer, GROUP)
     labels = got[:, 2 * LISTED * slab, :PAIRS].astype(jnp.int32).reshape(-1)
 
-    metas = jnp.concatenate([jnp.where(even, of_three, of_one), of_swapped], axis=0)
+    metas = jnp.concatenate([jnp.where(even, of_three, of_one), meta_row(of_swapped)], axis=0)
     second = pl.pallas_call(
         near_kernel,
         out_shape=jax.ShapeDtypeStruct((parts, 2 * LISTED * slab, width), jnp.bfloat16),
-        in_specs=[smem, vmem, hbm, vmem, vmem],
+        in_specs=[smem, vmem, hbm, vmem, vmem, vmem],
         out_specs=vmem,
         scratch_shapes=[held, copied((1,))],
         compiler_params=params,
         cost_estimate=pl.CostEstimate(flops=COST, bytes_accessed=2**23, transcendentals=0),
         name="near_products",
-    )(listed(metas), metas, whole, swapped_block, near_block)
+    )(listed(metas), metas, whole, swapped_top, of_swapped, near_block)
     second = exchanged(second, GROUP)
 
     chains = [pltpu.VMEM((tiles, slab, width), jnp.float32) for _ in range(LISTED)]

time: 121 us -> 119 us (0.983)
  local copies, waits for them, and re-layouts: 4.26 us -> 2.11 us
    ppermute x1, starting transfers between devices: 1.28 us -> 3.75 us  [body(): of_far = lax.ppermute(of_three, 'tx', far)]
    unnamed x8 -> x4, local copies, waits for them, and re-layouts: 4.09 us -> 1.93 us
    all_to_all x2, starting transfers between devices: 13.7 us -> 11.6 us  [exchanged(): return lax.all_to_all(block, axis, split_axis=0, concat_axis=0, tiled=True)]
  transfers between devices with their start and end apart: 7 -> 7, of which waited for: 5 -> 4; matrix products, arithmetic and copies ran while one was open for 0% -> 0% of each run, Pallas kernels for 9% -> 10%
where the time goes in v6:
time: 119 us
  waiting for transfers between devices  40.2 us (34%)
  blocking collectives  33 us (28%)
  starting transfers between devices  27.9 us (23%)
  Pallas kernels  14.3 us (12%)
  local copies, waits for them, and re-layouts  2.11 us (2%)
    all_to_all x1, blocking collectives, exchanged(): return lax.all_to_all(block, axis, split_axis=0, concat_axis=0, tiled=True)  33 us
    all_to_all x2, waiting for transfers between devices, exchanged(): return lax.all_to_all(block, axis, split_axis=0, concat_axis=0, tiled=True)  32.8 us
    all_to_all x2, starting transfers between devices, exchanged(): return lax.all_to_all(block, axis, split_axis=0, concat_axis=0, tiled=True)  11.6 us
    ppermute x1, waiting for transfers between devices, body(): near_block = lax.ppermute(jacobian[0], 'tx', near)  6.11 us
    ppermute x1, starting transfers between devices, body(): far_block = lax.ppermute(jacobian[0], 'tx', far)  4.41 us
    ppermute x1, starting transfers between devices, body(): near_block = lax.ppermute(jacobian[0], 'tx', near)  4.32 us
    ppermute x1, starting transfers between devices, body(): of_far = lax.ppermute(of_three, 'tx', far)  3.75 us
    pallas_call x1, Pallas kernels, body(): pl.pallas_call(own_kernel, out_shape=(first, held, jax.ShapeDtypeStruct((...  3.5 us
  transfers between devices with their start and end apart: 7, of which 4 were waited for; matrix products, arithmetic and copies ran while one was open for 0% of the time, Pallas kernels for 10%

profile of v6, /device:TPU:32, one launch (start us, length us, event | category | flops | bytes accessed | tf_op | source)
XLA Modules:
  0.0 118.7 jit_solution(16553414812091188744)
XLA Ops:
  0.0 4.4 %collective-permute-start.1 = (bf16[256,2048]{1,0:T(8,128)(2,1)}, bf16[256,2048]{1,0:T(8,128)(2,1)S(1)}, u32[]{:S(2)}, u32[]{:S(2)}) collective-permute-start(bf16[256,2048]{1,0:T(8,128)(2,1)} %bitcast.13), channel_id=1, source_target_pairs={{128,32},{480,96},{256,160},{96,224},{384,288},{224,352},{0,416},{... | collective-permute-start | bytes 3145736 | tf_op jit(solution)/shard_map/ppermute | solution.py:227
  4.4 4.3 %collective-permute-start.4 = (bf16[256,2048]{1,0:T(8,128)(2,1)}, bf16[256,2048]{1,0:T(8,128)(2,1)}, u32[]{:S(2)}, u32[]{:S(2)}) collective-permute-start(bf16[256,2048]{1,0:T(8,128)(2,1)} %bitcast.14), channel_id=1, source_target_pairs={{96,0},{64,32},{160,64},{128,96},{224,128},{192,160},{288,192},{25... | collective-permute-start | bytes 3145736 | tf_op jit(solution)/shard_map/ppermute | solution.py:226
  8.8 3.5 %own_products.1 = (bf16[64,104,128]{2,1,0:T(8,128)(2,1)}, bf16[256,2048]{1,0:T(8,128)(2,1)S(1)}, bf16[240,2048]{1,0:T(8,128)(2,1)}, f32[1,384]{1,0:T(1,128)S(1)}...) custom-call(s32[1]{0:T(128)} %bitcast.refs_0_, s32[1,1,24]{2,1,0:T(1,128)} %refs_1_.1, s32[1,1,24]{2,1,0:T(1,128)} %refs_2_.1, ...), custom_call_target="tpu_custom_call" | custom-call | tf_op jit(solution)/shard_map/own_products/pallas_call | solution.py:235
  12.3 1.9 %collective-permute-start.2 = (bf16[240,2048]{1,0:T(8,128)(2,1)}, bf16[240,2048]{1,0:T(8,128)(2,1)S(1)}, u32[]{:S(2)}, u32[]{:S(2)}) collective-permute-start(bf16[240,2048]{1,0:T(8,128)(2,1)} %get-tuple-element.14), channel_id=1, source_target_pairs={{32,0},{0,32},{96,64},{64,96},{160,128},{128,160},{224,192},{192,2... | collective-permute-start | bytes 2949128 | tf_op jit(solution)/shard_map/ppermute | solution.py:259
  14.2 3.7 %collective-permute-start = (f32[1,384]{1,0:T(1,128)S(1)}, f32[1,384]{1,0:T(1,128)S(1)}, u32[]{:S(2)}, u32[]{:S(2)}) collective-permute-start(f32[1,384]{1,0:T(1,128)S(1)} %get-tuple-element.12), channel_id=1, source_target_pairs={{128,32},{480,96},{256,160},{96,224},{384,288},{224,352},{0,416},{... | collective-permute-start | bytes 4616 | tf_op jit(solution)/shard_map/ppermute | solution.py:260
  17.9 1.9 %collective-permute-start.3 = (f32[24,2048]{1,0:T(8,128)S(1)}, f32[24,2048]{1,0:T(8,128)S(1)}, u32[]{:S(2)}, u32[]{:S(2)}) collective-permute-start(f32[24,2048]{1,0:T(8,128)S(1)} %get-tuple-element.15), channel_id=1, source_target_pairs={{32,0},{0,32},{96,64},{64,96},{160,128},{128,160},{224,192},{192,2... | collective-permute-start | bytes 589832 | tf_op jit(solution)/shard_map/ppermute | solution.py:261
  19.9 0.0 collective-permute-done
  19.9 0.1 pad_add_fusion.lists
  20.0 1.3 %collective-permute-done.3.refs_2_.tail = f32[24,2048]{1,0:T(8,128)S(1)} collective-permute-done((f32[24,2048]{1,0:T(8,128)S(1)}, f32[24,2048]{1,0:T(8,128)S(1)}, u32[]{:S(2)}, u32[]{:S(2)}) %collective-permute-start.3) | collective-permute-done | bytes 196640 | tf_op jit(solution)/shard_map/ppermute | solution.py:261
  21.3 0.1 reshape.21.lists
  21.4 0.0 collective-permute-done.2.refs_1_.top
  21.4 0.0 collective-permute-done.1.refs_0_
  21.4 2.0 %last_products.1 = bf16[64,104,128]{2,1,0:T(8,128)(2,1)} custom-call(s32[13]{0:T(128)S(1)} %pad_add_fusion.lists, f32[1,384]{1,0:T(1,128)S(1)} %get-tuple-element.20.metas, bf16[256,2048]{1,0:T(8,128)(2,1)S(1)} %get-tuple-element.13.own, bf16[256,2048]{1,0:T(8,128)(2,1)S(1)} %collective-permute-done.1.refs_0_, ...), custom_call_target="tpu_custom_call", output_to_operand_aliasing={{}: (6, {})} | custom-call | tf_op jit(solution)/shard_map/last_products/pallas_call | solution.py:271
  23.4 5.8 %all-to-all-start = ((bf16[64,104,128]{2,1,0:T(8,128)(2,1)}), bf16[64,104,128]{2,1,0:T(8,128)(2,1)S(1)}, u32[]{:S(2)}, u32[]{:S(2)}) async-start(bf16[64,104,128]{2,1,0:T(8,128)(2,1)} %last_products.1), calls=%async_computation | async-start | bytes 3407872 | tf_op jit(solution)/shard_map/all_to_all | solution.py:23
  29.2 6.1 %collective-permute-done.4.near = bf16[256,2048]{1,0:T(8,128)(2,1)} collective-permute-done((bf16[256,2048]{1,0:T(8,128)(2,1)}, bf16[256,2048]{1,0:T(8,128)(2,1)}, u32[]{:S(2)}, u32[]{:S(2)}) %collective-permute-start.4) | collective-permute-done | bytes 1048608 | tf_op jit(solution)/shard_map/ppermute | solution.py:226
  35.3 3.4 %near_products.1 = bf16[64,96,128]{2,1,0:T(8,128)(2,1)S(1)} custom-call(s32[24]{0:T(128)S(1)} %reshape.21.lists, f32[2,384]{1,0:T(2,128)S(1)} %pad_maximum_fusion.1.metas, bf16[1,256,2048]{2,1,0:T(8,128)(2,1)} %whole.1, bf16[240,2048]{1,0:T(8,128)(2,1)S(1)} %collective-permute-done.2.refs_1_.top, f32[24,2048]{1,0:T(8,128)S(1)} %collective-permute-done.3.refs_2_.tail, ...), custom_call_target="tpu_custom_call" | custom-call | flops 99999997952 | bytes 8388608 | tf_op jit(solution)/shard_map/near_products/pallas_call | solution.py:285
  38.7 0.0 copy-start.1
  38.7 1.1 copy-done.1
  39.9 13.7 %all-to-all-done.got = bf16[64,104,128]{2,1,0:T(8,128)(2,1)S(1)} async-done(((bf16[64,104,128]{2,1,0:T(8,128)(2,1)}), bf16[64,104,128]{2,1,0:T(8,128)(2,1)S(1)}, u32[]{:S(2)}, u32[]{:S(2)}) %all-to-all-start) | async-done | bytes 1703968 | tf_op jit(solution)/shard_map/all_to_all | solution.py:23
  53.5 5.8 %all-to-all-start.1 = ((bf16[64,96,128]{2,1,0:T(8,128)(2,1)}), bf16[64,96,128]{2,1,0:T(8,128)(2,1)S(1)}, u32[]{:S(2)}, u32[]{:S(2)}) async-start(bf16[64,96,128]{2,1,0:T(8,128)(2,1)} %copy-done.1), calls=%async_computation.1 | async-start | bytes 3145728 | tf_op jit(solution)/shard_map/all_to_all | solution.py:23
  59.3 0.1 fusion
  59.4 0.1 reshape.22.labels
  59.5 2.8 %first_sums.1.before = f32[128,8,128]{2,1,0:T(8,128)S(1)} custom-call(s32[1536]{0:T(1024)S(1)} %reshape.22.labels, bf16[64,104,128]{2,1,0:T(8,128)(2,1)S(1)} %all-to-all-done.got), custom_call_target="tpu_custom_call" | custom-call | tf_op jit(solution)/shard_map/first_sums/pallas_call | solution.py:298
  62.3 0.0 copy-start
  62.3 0.8 copy-done
  63.1 19.1 %all-to-all-done.1.got = bf16[64,96,128]{2,1,0:T(8,128)(2,1)S(1)} async-done(((bf16[64,96,128]{2,1,0:T(8,128)(2,1)}), bf16[64,96,128]{2,1,0:T(8,128)(2,1)S(1)}, u32[]{:S(2)}, u32[]{:S(2)}) %all-to-all-start.1) | async-done | bytes 1572896 | tf_op jit(solution)/shard_map/all_to_all | solution.py:23
  82.2 2.7 %near_sums.1 = bf16[1024,128]{1,0:T(8,128)(2,1)S(1)} custom-call(s32[1536]{0:T(1024)S(1)} %reshape.22.labels, bf16[64,96,128]{2,1,0:T(8,128)(2,1)S(1)} %all-to-all-done.1.got, f32[128,8,128]{2,1,0:T(8,128)} %copy-done), custom_call_target="tpu_custom_call" | custom-call | tf_op jit(solution)/shard_map/near_sums/pallas_call | solution.py:307
  85.0 33.0 %all_to_all.19 = bf16[16,64,128]{2,1,0:T(8,128)(2,1)S(1)} all-to-all(bf16[16,64,128]{2,1,0:T(8,128)(2,1)S(1)} %bitcast.11), channel_id=1, replica_groups=mesh['tx'=16,'mp_hi'=8,'mp_lo'=2,'rep'=2] {'mp_hi','mp_lo'}, dimensions={0} | all-to-all | bytes 524288 | tf_op jit(solution)/shard_map/all_to_all | solution.py:23
  118.0 0.6 pad_maximum_fusion
  (7 shorter events, 0.1 us)
Async XLA Ops:
  0.0 21.4 %collective-permute-start.1 = (bf16[256,2048]{1,0:T(8,128)(2,1)}, bf16[256,2048]{1,0:T(8,128)(2,1)S(1)}, u32[]{:S(2)}, u32[]{:S(2)}) collective-permute-start(bf16[256,2048]{1,0:T(8,128)(2,1)} %bitcast.13), channel_id=1, source_target_pairs={{128,32},{480,96},{256,160},{96,224},{384,288},{224,352},{0,416},{... | collective-permute-start | bytes 3145736 | tf_op jit(solution)/shard_map/ppermute | solution.py:227
  4.4 30.9 %collective-permute-start.4 = (bf16[256,2048]{1,0:T(8,128)(2,1)}, bf16[256,2048]{1,0:T(8,128)(2,1)}, u32[]{:S(2)}, u32[]{:S(2)}) collective-permute-start(bf16[256,2048]{1,0:T(8,128)(2,1)} %bitcast.14), channel_id=1, source_target_pairs={{96,0},{64,32},{160,64},{128,96},{224,128},{192,160},{288,192},{25... | collective-permute-start | bytes 3145736 | tf_op jit(solution)/shard_map/ppermute | solution.py:226
  12.3 9.1 %collective-permute-start.2 = (bf16[240,2048]{1,0:T(8,128)(2,1)}, bf16[240,2048]{1,0:T(8,128)(2,1)S(1)}, u32[]{:S(2)}, u32[]{:S(2)}) collective-permute-start(bf16[240,2048]{1,0:T(8,128)(2,1)} %get-tuple-element.14), channel_id=1, source_target_pairs={{32,0},{0,32},{96,64},{64,96},{160,128},{128,160},{224,192},{192,2... | collective-permute-start | bytes 2949128 | tf_op jit(solution)/shard_map/ppermute | solution.py:259
  14.2 5.7 %collective-permute-start = (f32[1,384]{1,0:T(1,128)S(1)}, f32[1,384]{1,0:T(1,128)S(1)}, u32[]{:S(2)}, u32[]{:S(2)}) collective-permute-start(f32[1,384]{1,0:T(1,128)S(1)} %get-tuple-element.12), channel_id=1, source_target_pairs={{128,32},{480,96},{256,160},{96,224},{384,288},{224,352},{0,416},{... | collective-permute-start | bytes 4616 | tf_op jit(solution)/shard_map/ppermute | solution.py:260
  17.9 3.3 %collective-permute-start.3 = (f32[24,2048]{1,0:T(8,128)S(1)}, f32[24,2048]{1,0:T(8,128)S(1)}, u32[]{:S(2)}, u32[]{:S(2)}) collective-permute-start(f32[24,2048]{1,0:T(8,128)S(1)} %get-tuple-element.15), channel_id=1, source_target_pairs={{32,0},{0,32},{96,64},{64,96},{160,128},{128,160},{224,192},{192,2... | collective-permute-start | bytes 589832 | tf_op jit(solution)/shard_map/ppermute | solution.py:261
  23.4 30.1 %all-to-all-start = ((bf16[64,104,128]{2,1,0:T(8,128)(2,1)}), bf16[64,104,128]{2,1,0:T(8,128)(2,1)S(1)}, u32[]{:S(2)}, u32[]{:S(2)}) async-start(bf16[64,104,128]{2,1,0:T(8,128)(2,1)} %last_products.1), calls=%async_computation | async-start | bytes 3407872 | tf_op jit(solution)/shard_map/all_to_all | solution.py:23
  38.7 1.1 copy-start.1
  53.5 28.7 %all-to-all-start.1 = ((bf16[64,96,128]{2,1,0:T(8,128)(2,1)}), bf16[64,96,128]{2,1,0:T(8,128)(2,1)S(1)}, u32[]{:S(2)}, u32[]{:S(2)}) async-start(bf16[64,96,128]{2,1,0:T(8,128)(2,1)} %copy-done.1), calls=%async_computation.1 | async-start | bytes 3145728 | tf_op jit(solution)/shard_map/all_to_all | solution.py:23
  62.3 0.8 copy-start

commit v7 on v6

--- a/solution.py
+++ b/solution.py
@@ -28,7 +28,7 @@
     swap = [(i ^ 1, i) for i in everyone]
     near = [((i + (1 if i % 2 else 3)) % devices, i) for i in everyone]
     far = [((i + (3 if i % 4 == 1 else -4)) % devices, i) for i in everyone if i % 2]
-    return swap, near, far
+    return swap, near, far, [(source, to) for source, to in far if to % 4 == 3]
 
 
 def column(row):
@@ -73,6 +73,11 @@
             then(row, 2 * slab)
 
 
+def quarters(whole, held):
+    rows = held.shape[0] // 4
+    return [(whole.at[0, pl.ds(i * rows, rows), :], held.at[pl.ds(i * rows, rows), :]) for i in range(4)]
+
+
 def fetched(pairs, sems):
     copies = [pltpu.make_async_copy(src, dst, sems.at[i]) for i, (src, dst) in enumerate(pairs)]
     for copy in copies:
@@ -90,24 +95,14 @@
         (right_hbm, lists.at[1]),
         (targets_hbm, targets),
         (coupling_hbm, coupling),
-        (whole.at[0], own),
-    )
-    for copy in fetched(pairs, sems):
+    ) + tuple(quarters(whole, own))
+    copies = fetched(pairs, sems)
+    for meta in metas:
+        meta[...] = jnp.zeros_like(meta)
+    numbers[...] = jnp.zeros_like(numbers)
+    for copy in copies[:6]:
         copy.wait()
-    rows = own.shape[0]
-    top[...] = own[: rows - TAIL, :]
-    for step, meta in enumerate(metas, 1):
-        here = slice(step * LISTED, (step + 1) * LISTED)
-        meta[...] = jnp.zeros_like(meta)
-        row = meta.shape[0] // (TAIL + 8) * TAIL
-        if row > 0:
-            meta[0:row, :] = own[rows - row :, :].astype(jnp.float32)
-        meta[row : row + 1, 0:rows] = coupling[step]
-        for side in range(2):
-            first = rows + side * LISTED
-            meta[row : row + 1, first : first + LISTED] = lists[side, 0, :, here].astype(jnp.float32)
     even = place[0] % 2 == 0
-    numbers[...] = jnp.zeros_like(numbers)
     for slot, other in enumerate((0, 3, 2, 1)):
         these, those = (targets[0, :, i * LISTED : (i + 1) * LISTED] for i in (slot, other))
         here = slice(slot * LISTED, (slot + 1) * LISTED)
@@ -115,6 +110,18 @@
     slab = numbers.shape[0]
     below = jnp.broadcast_to(numbers[...].astype(jnp.bfloat16)[None], (out.shape[0],) + numbers.shape)
     out[:, 2 * LISTED * slab :, :] = below
+    rows = own.shape[0]
+    for step, meta in enumerate(metas, 1):
+        here = slice(step * LISTED, (step + 1) * LISTED)
+        row = meta.shape[0] // (TAIL + 8) * TAIL
+        meta[row : row + 1, 0:rows] = coupling[step]
+        for side in range(2):
+            first = rows + side * LISTED
+            meta[row : row + 1, first : first + LISTED] = lists[side, 0, :, here].astype(jnp.float32)
+    for copy in copies[6:]:
+        copy.wait()
+    top[...] = own[: rows - TAIL, :]
+    metas[1][0:TAIL, :] = own[rows - TAIL :, :].astype(jnp.float32)
     add_tiles(lambda i: left_ids[0, 0, i], lambda i: right_ids[0, 0, i], column(coupling[0]), own, own, out, 0)
 
 
@@ -151,10 +158,11 @@
 
 def near_kernel(lists, metas, whole, top, tail, near, out, own, sems):
     swapped = (top, tail)
-    (load,) = fetched([(whole.at[0], own)], sems)
+    loads = fetched(quarters(whole, own), sems)
     rows = own.shape[0]
     add_tiles(*pair_of(metas, lists, 1, rows, swapped, near, out, 1))
-    load.wait()
+    for load in loads:
+        load.wait()
     add_tiles(*pair_of(metas, lists, 0, rows, own, near, out, 0))
 
 
@@ -208,7 +216,7 @@
     rows = jacobian.shape[1]
     devices = lax.axis_size("tx")
     subsets = lax.axis_size("rep")
-    swap, near, far = routes(devices)
+    swap, near, far, listing = routes(devices)
     parts = devices * subsets * HALVES
     owners = lax.axis_size("mp_hi") * lax.axis_size("mp_lo")
     slab = BRICK // (parts // HALVES)
@@ -237,7 +245,7 @@
         out_shape=(
             first,
             held,
-            jax.ShapeDtypeStruct((rows - TAIL, jacobian.shape[2]), jacobian.dtype),
+            pltpu.VMEM((rows - TAIL, jacobian.shape[2]), jacobian.dtype),
             meta,
             tall,
             meta,
@@ -251,13 +259,13 @@
             pltpu.VMEM(tile_target.shape, jnp.int32),
             pltpu.VMEM(coupling.shape, coupling.dtype),
             pltpu.VMEM((slab, width), jnp.float32),
-            copied((7,)),
+            copied((10,)),
         ],
         compiler_params=params,
         name="own_products",
     )(spot, *args, whole)
     swapped_top = lax.ppermute(top, "tx", swap)
-    of_far = lax.ppermute(of_three, "tx", far)
+    of_far = lax.ppermute(of_three, "tx", listing)
     of_swapped = lax.ppermute(of_two, "tx", swap)
     even = place % 2 == 0
 
@@ -287,7 +295,7 @@
         out_shape=jax.ShapeDtypeStruct((parts, 2 * LISTED * slab, width), jnp.bfloat16),
         in_specs=[smem, vmem, hbm, vmem, vmem, vmem],
         out_specs=vmem,
-        scratch_shapes=[held, copied((1,))],
+        scratch_shapes=[held, copied((4,))],
         compiler_params=params,
         cost_estimate=pl.CostEstimate(flops=COST, bytes_accessed=2**23, transcendentals=0),
         name="near_products",

time: 119 us -> 119 us (level)
    ppermute x1, starting transfers between devices: 3.75 us -> 0.66 us  [body(): of_far = lax.ppermute(of_three, 'tx', listing)]
    all_to_all x2, starting transfers between devices: 11.6 us -> 14.6 us  [exchanged(): return lax.all_to_all(block, axis, split_axis=0, concat_axis=0, tiled=True)]
where the time goes in v7:
time: 119 us
  waiting for transfers between devices  39.9 us (34%)
  blocking collectives  33 us (28%)
  starting transfers between devices  28.3 us (24%)
  Pallas kernels  14.3 us (12%)
  local copies, waits for them, and re-layouts  2.11 us (2%)
    all_to_all x1, blocking collectives, exchanged(): return lax.all_to_all(block, axis, split_axis=0, concat_axis=0, tiled=True)  33 us
    all_to_all x2, waiting for transfers between devices, exchanged(): return lax.all_to_all(block, axis, split_axis=0, concat_axis=0, tiled=True)  32.8 us
    all_to_all x2, starting transfers between devices, exchanged(): return lax.all_to_all(block, axis, split_axis=0, concat_axis=0, tiled=True)  14.6 us
    ppermute x1, waiting for transfers between devices, body(): near_block = lax.ppermute(jacobian[0], 'tx', near)  6.17 us
    ppermute x1, starting transfers between devices, body(): far_block = lax.ppermute(jacobian[0], 'tx', far)  4.41 us
    ppermute x1, starting transfers between devices, body(): near_block = lax.ppermute(jacobian[0], 'tx', near)  4.32 us
    pallas_call x1, Pallas kernels, body(): pl.pallas_call(own_kernel, out_shape=(first, held, pltpu.VMEM((rows - TAI...  3.44 us
    pallas_call x1, Pallas kernels, body(): pl.pallas_call(near_kernel, out_shape=jax.ShapeDtypeStruct((parts, 2 * LI...  3.39 us
  transfers between devices with their start and end apart: 7, of which 4 were waited for; matrix products, arithmetic and copies ran while one was open for 0% of the time, Pallas kernels for 10%

profile of v7, /device:TPU:32, one launch (start us, length us, event | category | flops | bytes accessed | tf_op | source)
XLA Modules:
  0.0 118.7 jit_solution(5227328879689633728)
XLA Ops:
  0.0 4.4 %collective-permute-start.1 = (bf16[256,2048]{1,0:T(8,128)(2,1)}, bf16[256,2048]{1,0:T(8,128)(2,1)S(1)}, u32[]{:S(2)}, u32[]{:S(2)}) collective-permute-start(bf16[256,2048]{1,0:T(8,128)(2,1)} %bitcast.13), channel_id=1, source_target_pairs={{128,32},{480,96},{256,160},{96,224},{384,288},{224,352},{0,416},{... | collective-permute-start | bytes 3145736 | tf_op jit(solution)/shard_map/ppermute | solution.py:235
  4.4 4.3 %collective-permute-start.4 = (bf16[256,2048]{1,0:T(8,128)(2,1)}, bf16[256,2048]{1,0:T(8,128)(2,1)}, u32[]{:S(2)}, u32[]{:S(2)}) collective-permute-start(bf16[256,2048]{1,0:T(8,128)(2,1)} %bitcast.14), channel_id=1, source_target_pairs={{96,0},{64,32},{160,64},{128,96},{224,128},{192,160},{288,192},{25... | collective-permute-start | bytes 3145736 | tf_op jit(solution)/shard_map/ppermute | solution.py:234
  8.8 3.4 %own_products.1 = (bf16[64,104,128]{2,1,0:T(8,128)(2,1)}, bf16[256,2048]{1,0:T(8,128)(2,1)S(1)}, bf16[240,2048]{1,0:T(8,128)(2,1)}, f32[1,384]{1,0:T(1,128)S(1)}...) custom-call(s32[1]{0:T(128)} %bitcast.refs_0_, s32[1,1,24]{2,1,0:T(1,128)} %refs_1_.1, s32[1,1,24]{2,1,0:T(1,128)} %refs_2_.1, ...), custom_call_target="tpu_custom_call" | custom-call | tf_op jit(solution)/shard_map/own_products/pallas_call | solution.py:243
  12.2 1.9 %collective-permute-start.2 = (bf16[240,2048]{1,0:T(8,128)(2,1)}, bf16[240,2048]{1,0:T(8,128)(2,1)S(1)}, u32[]{:S(2)}, u32[]{:S(2)}) collective-permute-start(bf16[240,2048]{1,0:T(8,128)(2,1)} %get-tuple-element.14), channel_id=1, source_target_pairs={{32,0},{0,32},{96,64},{64,96},{160,128},{128,160},{224,192},{192,2... | collective-permute-start | bytes 2949128 | tf_op jit(solution)/shard_map/ppermute | solution.py:267
  14.1 0.7 collective-permute-start
  14.8 2.4 %collective-permute-start.3 = (f32[24,2048]{1,0:T(8,128)S(1)}, f32[24,2048]{1,0:T(8,128)S(1)}, u32[]{:S(2)}, u32[]{:S(2)}) collective-permute-start(f32[24,2048]{1,0:T(8,128)S(1)} %get-tuple-element.15), channel_id=1, source_target_pairs={{32,0},{0,32},{96,64},{64,96},{160,128},{128,160},{224,192},{192,2... | collective-permute-start | bytes 589832 | tf_op jit(solution)/shard_map/ppermute | solution.py:269
  17.2 0.0 collective-permute-done
  17.3 0.1 pad_add_fusion.lists
  17.3 0.9 collective-permute-done.3.refs_2_.tail
  18.3 0.1 reshape.21.lists
  18.4 0.0 collective-permute-done.2.refs_1_.top
  18.4 0.0 collective-permute-done.1.refs_0_
  18.4 2.0 %last_products.1 = bf16[64,104,128]{2,1,0:T(8,128)(2,1)} custom-call(s32[13]{0:T(128)S(1)} %pad_add_fusion.lists, f32[1,384]{1,0:T(1,128)S(1)} %get-tuple-element.20.metas, bf16[256,2048]{1,0:T(8,128)(2,1)S(1)} %get-tuple-element.13.own, bf16[256,2048]{1,0:T(8,128)(2,1)S(1)} %collective-permute-done.1.refs_0_, ...), custom_call_target="tpu_custom_call", output_to_operand_aliasing={{}: (6, {})} | custom-call | tf_op jit(solution)/shard_map/last_products/pallas_call | solution.py:279
  20.4 8.8 %all-to-all-start = ((bf16[64,104,128]{2,1,0:T(8,128)(2,1)}), bf16[64,104,128]{2,1,0:T(8,128)(2,1)S(1)}, u32[]{:S(2)}, u32[]{:S(2)}) async-start(bf16[64,104,128]{2,1,0:T(8,128)(2,1)} %last_products.1), calls=%async_computation | async-start | bytes 3407872 | tf_op jit(solution)/shard_map/all_to_all | solution.py:23
  29.2 6.2 %collective-permute-done.4.near = bf16[256,2048]{1,0:T(8,128)(2,1)} collective-permute-done((bf16[256,2048]{1,0:T(8,128)(2,1)}, bf16[256,2048]{1,0:T(8,128)(2,1)}, u32[]{:S(2)}, u32[]{:S(2)}) %collective-permute-start.4) | collective-permute-done | bytes 1048608 | tf_op jit(solution)/shard_map/ppermute | solution.py:234
  35.3 3.4 %near_products.1 = bf16[64,96,128]{2,1,0:T(8,128)(2,1)S(1)} custom-call(s32[24]{0:T(128)S(1)} %reshape.21.lists, f32[2,384]{1,0:T(2,128)S(1)} %pad_maximum_fusion.1.metas, bf16[1,256,2048]{2,1,0:T(8,128)(2,1)} %whole.1, bf16[240,2048]{1,0:T(8,128)(2,1)S(1)} %collective-permute-done.2.refs_1_.top, f32[24,2048]{1,0:T(8,128)S(1)} %collective-permute-done.3.refs_2_.tail, ...), custom_call_target="tpu_custom_call" | custom-call | flops 99999997952 | bytes 8388608 | tf_op jit(solution)/shard_map/near_products/pallas_call | solution.py:293
  38.7 0.0 copy-start.1
  38.7 1.1 copy-done.1
  39.9 13.6 %all-to-all-done.got = bf16[64,104,128]{2,1,0:T(8,128)(2,1)S(1)} async-done(((bf16[64,104,128]{2,1,0:T(8,128)(2,1)}), bf16[64,104,128]{2,1,0:T(8,128)(2,1)S(1)}, u32[]{:S(2)}, u32[]{:S(2)}) %all-to-all-start) | async-done | bytes 1703968 | tf_op jit(solution)/shard_map/all_to_all | solution.py:23
  53.5 5.8 %all-to-all-start.1 = ((bf16[64,96,128]{2,1,0:T(8,128)(2,1)}), bf16[64,96,128]{2,1,0:T(8,128)(2,1)S(1)}, u32[]{:S(2)}, u32[]{:S(2)}) async-start(bf16[64,96,128]{2,1,0:T(8,128)(2,1)} %copy-done.1), calls=%async_computation.1 | async-start | bytes 3145728 | tf_op jit(solution)/shard_map/all_to_all | solution.py:23
  59.3 0.1 fusion
  59.4 0.1 reshape.22.labels
  59.5 2.8 %first_sums.1.before = f32[128,8,128]{2,1,0:T(8,128)S(1)} custom-call(s32[1536]{0:T(1024)S(1)} %reshape.22.labels, bf16[64,104,128]{2,1,0:T(8,128)(2,1)S(1)} %all-to-all-done.got), custom_call_target="tpu_custom_call" | custom-call | tf_op jit(solution)/shard_map/first_sums/pallas_call | solution.py:306
  62.3 0.0 copy-start
  62.3 0.8 copy-done
  63.1 19.1 %all-to-all-done.1.got = bf16[64,96,128]{2,1,0:T(8,128)(2,1)S(1)} async-done(((bf16[64,96,128]{2,1,0:T(8,128)(2,1)}), bf16[64,96,128]{2,1,0:T(8,128)(2,1)S(1)}, u32[]{:S(2)}, u32[]{:S(2)}) %all-to-all-start.1) | async-done | bytes 1572896 | tf_op jit(solution)/shard_map/all_to_all | solution.py:23
  82.2 2.7 %near_sums.1 = bf16[1024,128]{1,0:T(8,128)(2,1)S(1)} custom-call(s32[1536]{0:T(1024)S(1)} %reshape.22.labels, bf16[64,96,128]{2,1,0:T(8,128)(2,1)S(1)} %all-to-all-done.1.got, f32[128,8,128]{2,1,0:T(8,128)} %copy-done), custom_call_target="tpu_custom_call" | custom-call | tf_op jit(solution)/shard_map/near_sums/pallas_call | solution.py:315
  85.0 33.0 %all_to_all.19 = bf16[16,64,128]{2,1,0:T(8,128)(2,1)S(1)} all-to-all(bf16[16,64,128]{2,1,0:T(8,128)(2,1)S(1)} %bitcast.11), channel_id=1, replica_groups=mesh['tx'=16,'mp_hi'=8,'mp_lo'=2,'rep'=2] {'mp_hi','mp_lo'}, dimensions={0} | all-to-all | bytes 524288 | tf_op jit(solution)/shard_map/all_to_all | solution.py:23
  118.0 0.6 pad_maximum_fusion
  (7 shorter events, 0.1 us)
Async XLA Ops:
  0.0 18.4 %collective-permute-start.1 = (bf16[256,2048]{1,0:T(8,128)(2,1)}, bf16[256,2048]{1,0:T(8,128)(2,1)S(1)}, u32[]{:S(2)}, u32[]{:S(2)}) collective-permute-start(bf16[256,2048]{1,0:T(8,128)(2,1)} %bitcast.13), channel_id=1, source_target_pairs={{128,32},{480,96},{256,160},{96,224},{384,288},{224,352},{0,416},{... | collective-permute-start | bytes 3145736 | tf_op jit(solution)/shard_map/ppermute | solution.py:235
  4.4 30.9 %collective-permute-start.4 = (bf16[256,2048]{1,0:T(8,128)(2,1)}, bf16[256,2048]{1,0:T(8,128)(2,1)}, u32[]{:S(2)}, u32[]{:S(2)}) collective-permute-start(bf16[256,2048]{1,0:T(8,128)(2,1)} %bitcast.14), channel_id=1, source_target_pairs={{96,0},{64,32},{160,64},{128,96},{224,128},{192,160},{288,192},{25... | collective-permute-start | bytes 3145736 | tf_op jit(solution)/shard_map/ppermute | solution.py:234
  12.2 6.2 %collective-permute-start.2 = (bf16[240,2048]{1,0:T(8,128)(2,1)}, bf16[240,2048]{1,0:T(8,128)(2,1)S(1)}, u32[]{:S(2)}, u32[]{:S(2)}) collective-permute-start(bf16[240,2048]{1,0:T(8,128)(2,1)} %get-tuple-element.14), channel_id=1, source_target_pairs={{32,0},{0,32},{96,64},{64,96},{160,128},{128,160},{224,192},{192,2... | collective-permute-start | bytes 2949128 | tf_op jit(solution)/shard_map/ppermute | solution.py:267
  14.1 3.1 %collective-permute-start = (f32[1,384]{1,0:T(1,128)S(1)}, f32[1,384]{1,0:T(1,128)S(1)}, u32[]{:S(2)}, u32[]{:S(2)}) collective-permute-start(f32[1,384]{1,0:T(1,128)S(1)} %get-tuple-element.12), channel_id=1, source_target_pairs={{480,96},{96,224},{224,352},{352,480},{481,97},{97,225},{225,353},... | collective-permute-start | bytes 4616 | tf_op jit(solution)/shard_map/ppermute | solution.py:268
  14.8 3.5 %collective-permute-start.3 = (f32[24,2048]{1,0:T(8,128)S(1)}, f32[24,2048]{1,0:T(8,128)S(1)}, u32[]{:S(2)}, u32[]{:S(2)}) collective-permute-start(f32[24,2048]{1,0:T(8,128)S(1)} %get-tuple-element.15), channel_id=1, source_target_pairs={{32,0},{0,32},{96,64},{64,96},{160,128},{128,160},{224,192},{192,2... | collective-permute-start | bytes 589832 | tf_op jit(solution)/shard_map/ppermute | solution.py:269
  20.4 33.1 %all-to-all-start = ((bf16[64,104,128]{2,1,0:T(8,128)(2,1)}), bf16[64,104,128]{2,1,0:T(8,128)(2,1)S(1)}, u32[]{:S(2)}, u32[]{:S(2)}) async-start(bf16[64,104,128]{2,1,0:T(8,128)(2,1)} %last_products.1), calls=%async_computation | async-start | bytes 3407872 | tf_op jit(solution)/shard_map/all_to_all | solution.py:23
  38.7 1.1 copy-start.1
  53.5 28.8 %all-to-all-start.1 = ((bf16[64,96,128]{2,1,0:T(8,128)(2,1)}), bf16[64,96,128]{2,1,0:T(8,128)(2,1)S(1)}, u32[]{:S(2)}, u32[]{:S(2)}) async-start(bf16[64,96,128]{2,1,0:T(8,128)(2,1)} %copy-done.1), calls=%async_computation.1 | async-start | bytes 3145728 | tf_op jit(solution)/shard_map/all_to_all | solution.py:23
  62.3 0.8 copy-start

commit v8 on v7

--- a/solution.py
+++ b/solution.py
@@ -29,10 +29,6 @@
     near = [((i + (1 if i % 2 else 3)) % devices, i) for i in everyone]
     far = [((i + (3 if i % 4 == 1 else -4)) % devices, i) for i in everyone if i % 2]
     return swap, near, far, [(source, to) for source, to in far if to % 4 == 3]
-
-
-def column(row):
-    return jnp.broadcast_to(row, (BRICK, row.shape[1])).T
 
 
 def column(row):

time: 119 us -> 119 us (level)
  no operation moved by 1% of the time
where the time goes in v8:
time: 119 us
  waiting for transfers between devices  39.9 us (34%)
  blocking collectives  33 us (28%)
  starting transfers between devices  28.3 us (24%)
  Pallas kernels  14.3 us (12%)
  local copies, waits for them, and re-layouts  2.11 us (2%)
    all_to_all x1, blocking collectives, exchanged(): return lax.all_to_all(block, axis, split_axis=0, concat_axis=0, tiled=True)  33 us
    all_to_all x2, waiting for transfers between devices, exchanged(): return lax.all_to_all(block, axis, split_axis=0, concat_axis=0, tiled=True)  32.7 us
    all_to_all x2, starting transfers between devices, exchanged(): return lax.all_to_all(block, axis, split_axis=0, concat_axis=0, tiled=True)  14.6 us
    ppermute x1, waiting for transfers between devices, body(): near_block = lax.ppermute(jacobian[0], 'tx', near)  6.17 us
    ppermute x1, starting transfers between devices, body(): far_block = lax.ppermute(jacobian[0], 'tx', far)  4.41 us
    ppermute x1, starting transfers between devices, body(): near_block = lax.ppermute(jacobian[0], 'tx', near)  4.32 us
    pallas_call x1, Pallas kernels, body(): pl.pallas_call(own_kernel, out_shape=(first, held, pltpu.VMEM((rows - TAI...  3.46 us
    pallas_call x1, Pallas kernels, body(): pl.pallas_call(near_kernel, out_shape=jax.ShapeDtypeStruct((parts, 2 * LI...  3.39 us
  transfers between devices with their start and end apart: 7, of which 4 were waited for; matrix products, arithmetic and copies ran while one was open for 0% of the time, Pallas kernels for 10%

profile of v8, /device:TPU:32, one launch (start us, length us, event | category | flops | bytes accessed | tf_op | source)
XLA Modules:
  0.0 118.7 jit_solution(5227328879689633728)
XLA Ops:
  0.0 4.4 %collective-permute-start.1 = (bf16[256,2048]{1,0:T(8,128)(2,1)}, bf16[256,2048]{1,0:T(8,128)(2,1)S(1)}, u32[]{:S(2)}, u32[]{:S(2)}) collective-permute-start(bf16[256,2048]{1,0:T(8,128)(2,1)} %bitcast.13), channel_id=1, source_target_pairs={{128,32},{480,96},{256,160},{96,224},{384,288},{224,352},{0,416},{... | collective-permute-start | bytes 3145736 | tf_op jit(solution)/shard_map/ppermute | solution.py:231
  4.4 4.3 %collective-permute-start.4 = (bf16[256,2048]{1,0:T(8,128)(2,1)}, bf16[256,2048]{1,0:T(8,128)(2,1)}, u32[]{:S(2)}, u32[]{:S(2)}) collective-permute-start(bf16[256,2048]{1,0:T(8,128)(2,1)} %bitcast.14), channel_id=1, source_target_pairs={{96,0},{64,32},{160,64},{128,96},{224,128},{192,160},{288,192},{25... | collective-permute-start | bytes 3145736 | tf_op jit(solution)/shard_map/ppermute | solution.py:230
  8.8 3.5 %own_products.1 = (bf16[64,104,128]{2,1,0:T(8,128)(2,1)}, bf16[256,2048]{1,0:T(8,128)(2,1)S(1)}, bf16[240,2048]{1,0:T(8,128)(2,1)}, f32[1,384]{1,0:T(1,128)S(1)}...) custom-call(s32[1]{0:T(128)} %bitcast.refs_0_, s32[1,1,24]{2,1,0:T(1,128)} %refs_1_.1, s32[1,1,24]{2,1,0:T(1,128)} %refs_2_.1, ...), custom_call_target="tpu_custom_call" | custom-call | tf_op jit(solution)/shard_map/own_products/pallas_call | solution.py:239
  12.2 1.9 %collective-permute-start.2 = (bf16[240,2048]{1,0:T(8,128)(2,1)}, bf16[240,2048]{1,0:T(8,128)(2,1)S(1)}, u32[]{:S(2)}, u32[]{:S(2)}) collective-permute-start(bf16[240,2048]{1,0:T(8,128)(2,1)} %get-tuple-element.14), channel_id=1, source_target_pairs={{32,0},{0,32},{96,64},{64,96},{160,128},{128,160},{224,192},{192,2... | collective-permute-start | bytes 2949128 | tf_op jit(solution)/shard_map/ppermute | solution.py:263
  14.2 0.7 collective-permute-start
  14.8 2.4 %collective-permute-start.3 = (f32[24,2048]{1,0:T(8,128)S(1)}, f32[24,2048]{1,0:T(8,128)S(1)}, u32[]{:S(2)}, u32[]{:S(2)}) collective-permute-start(f32[24,2048]{1,0:T(8,128)S(1)} %get-tuple-element.15), channel_id=1, source_target_pairs={{32,0},{0,32},{96,64},{64,96},{160,128},{128,160},{224,192},{192,2... | collective-permute-start | bytes 589832 | tf_op jit(solution)/shard_map/ppermute | solution.py:265
  17.3 0.0 collective-permute-done
  17.3 0.1 pad_add_fusion.lists
  17.4 0.9 collective-permute-done.3.refs_2_.tail
  18.3 0.1 reshape.21.lists
  18.4 0.0 collective-permute-done.2.refs_1_.top
  18.4 0.0 collective-permute-done.1.refs_0_
  18.4 2.0 %last_products.1 = bf16[64,104,128]{2,1,0:T(8,128)(2,1)} custom-call(s32[13]{0:T(128)S(1)} %pad_add_fusion.lists, f32[1,384]{1,0:T(1,128)S(1)} %get-tuple-element.20.metas, bf16[256,2048]{1,0:T(8,128)(2,1)S(1)} %get-tuple-element.13.own, bf16[256,2048]{1,0:T(8,128)(2,1)S(1)} %collective-permute-done.1.refs_0_, ...), custom_call_target="tpu_custom_call", output_to_operand_aliasing={{}: (6, {})} | custom-call | tf_op jit(solution)/shard_map/last_products/pallas_call | solution.py:275
  20.4 8.7 %all-to-all-start = ((bf16[64,104,128]{2,1,0:T(8,128)(2,1)}), bf16[64,104,128]{2,1,0:T(8,128)(2,1)S(1)}, u32[]{:S(2)}, u32[]{:S(2)}) async-start(bf16[64,104,128]{2,1,0:T(8,128)(2,1)} %last_products.1), calls=%async_computation | async-start | bytes 3407872 | tf_op jit(solution)/shard_map/all_to_all | solution.py:23
  29.2 6.2 %collective-permute-done.4.near = bf16[256,2048]{1,0:T(8,128)(2,1)} collective-permute-done((bf16[256,2048]{1,0:T(8,128)(2,1)}, bf16[256,2048]{1,0:T(8,128)(2,1)}, u32[]{:S(2)}, u32[]{:S(2)}) %collective-permute-start.4) | collective-permute-done | bytes 1048608 | tf_op jit(solution)/shard_map/ppermute | solution.py:230
  35.3 3.4 %near_products.1 = bf16[64,96,128]{2,1,0:T(8,128)(2,1)S(1)} custom-call(s32[24]{0:T(128)S(1)} %reshape.21.lists, f32[2,384]{1,0:T(2,128)S(1)} %pad_maximum_fusion.1.metas, bf16[1,256,2048]{2,1,0:T(8,128)(2,1)} %whole.1, bf16[240,2048]{1,0:T(8,128)(2,1)S(1)} %collective-permute-done.2.refs_1_.top, f32[24,2048]{1,0:T(8,128)S(1)} %collective-permute-done.3.refs_2_.tail, ...), custom_call_target="tpu_custom_call" | custom-call | flops 99999997952 | bytes 8388608 | tf_op jit(solution)/shard_map/near_products/pallas_call | solution.py:289
  38.7 0.0 copy-start.1
  38.7 1.1 copy-done.1
  39.9 13.6 %all-to-all-done.got = bf16[64,104,128]{2,1,0:T(8,128)(2,1)S(1)} async-done(((bf16[64,104,128]{2,1,0:T(8,128)(2,1)}), bf16[64,104,128]{2,1,0:T(8,128)(2,1)S(1)}, u32[]{:S(2)}, u32[]{:S(2)}) %all-to-all-start) | async-done | bytes 1703968 | tf_op jit(solution)/shard_map/all_to_all | solution.py:23
  53.5 5.8 %all-to-all-start.1 = ((bf16[64,96,128]{2,1,0:T(8,128)(2,1)}), bf16[64,96,128]{2,1,0:T(8,128)(2,1)S(1)}, u32[]{:S(2)}, u32[]{:S(2)}) async-start(bf16[64,96,128]{2,1,0:T(8,128)(2,1)} %copy-done.1), calls=%async_computation.1 | async-start | bytes 3145728 | tf_op jit(solution)/shard_map/all_to_all | solution.py:23
  59.3 0.1 fusion
  59.4 0.1 reshape.22.labels
  59.5 2.8 %first_sums.1.before = f32[128,8,128]{2,1,0:T(8,128)S(1)} custom-call(s32[1536]{0:T(1024)S(1)} %reshape.22.labels, bf16[64,104,128]{2,1,0:T(8,128)(2,1)S(1)} %all-to-all-done.got), custom_call_target="tpu_custom_call" | custom-call | tf_op jit(solution)/shard_map/first_sums/pallas_call | solution.py:302
  62.3 0.0 copy-start
  62.3 0.8 copy-done
  63.1 19.1 %all-to-all-done.1.got = bf16[64,96,128]{2,1,0:T(8,128)(2,1)S(1)} async-done(((bf16[64,96,128]{2,1,0:T(8,128)(2,1)}), bf16[64,96,128]{2,1,0:T(8,128)(2,1)S(1)}, u32[]{:S(2)}, u32[]{:S(2)}) %all-to-all-start.1) | async-done | bytes 1572896 | tf_op jit(solution)/shard_map/all_to_all | solution.py:23
  82.2 2.7 %near_sums.1 = bf16[1024,128]{1,0:T(8,128)(2,1)S(1)} custom-call(s32[1536]{0:T(1024)S(1)} %reshape.22.labels, bf16[64,96,128]{2,1,0:T(8,128)(2,1)S(1)} %all-to-all-done.1.got, f32[128,8,128]{2,1,0:T(8,128)} %copy-done), custom_call_target="tpu_custom_call" | custom-call | tf_op jit(solution)/shard_map/near_sums/pallas_call | solution.py:311
  85.0 33.0 %all_to_all.19 = bf16[16,64,128]{2,1,0:T(8,128)(2,1)S(1)} all-to-all(bf16[16,64,128]{2,1,0:T(8,128)(2,1)S(1)} %bitcast.11), channel_id=1, replica_groups=mesh['tx'=16,'mp_hi'=8,'mp_lo'=2,'rep'=2] {'mp_hi','mp_lo'}, dimensions={0} | all-to-all | bytes 524288 | tf_op jit(solution)/shard_map/all_to_all | solution.py:23
  118.0 0.6 pad_maximum_fusion
  (7 shorter events, 0.1 us)
Async XLA Ops:
  0.0 18.4 %collective-permute-start.1 = (bf16[256,2048]{1,0:T(8,128)(2,1)}, bf16[256,2048]{1,0:T(8,128)(2,1)S(1)}, u32[]{:S(2)}, u32[]{:S(2)}) collective-permute-start(bf16[256,2048]{1,0:T(8,128)(2,1)} %bitcast.13), channel_id=1, source_target_pairs={{128,32},{480,96},{256,160},{96,224},{384,288},{224,352},{0,416},{... | collective-permute-start | bytes 3145736 | tf_op jit(solution)/shard_map/ppermute | solution.py:231
  4.4 30.9 %collective-permute-start.4 = (bf16[256,2048]{1,0:T(8,128)(2,1)}, bf16[256,2048]{1,0:T(8,128)(2,1)}, u32[]{:S(2)}, u32[]{:S(2)}) collective-permute-start(bf16[256,2048]{1,0:T(8,128)(2,1)} %bitcast.14), channel_id=1, source_target_pairs={{96,0},{64,32},{160,64},{128,96},{224,128},{192,160},{288,192},{25... | collective-permute-start | bytes 3145736 | tf_op jit(solution)/shard_map/ppermute | solution.py:230
  12.2 6.2 %collective-permute-start.2 = (bf16[240,2048]{1,0:T(8,128)(2,1)}, bf16[240,2048]{1,0:T(8,128)(2,1)S(1)}, u32[]{:S(2)}, u32[]{:S(2)}) collective-permute-start(bf16[240,2048]{1,0:T(8,128)(2,1)} %get-tuple-element.14), channel_id=1, source_target_pairs={{32,0},{0,32},{96,64},{64,96},{160,128},{128,160},{224,192},{192,2... | collective-permute-start | bytes 2949128 | tf_op jit(solution)/shard_map/ppermute | solution.py:263
  14.2 3.1 %collective-permute-start = (f32[1,384]{1,0:T(1,128)S(1)}, f32[1,384]{1,0:T(1,128)S(1)}, u32[]{:S(2)}, u32[]{:S(2)}) collective-permute-start(f32[1,384]{1,0:T(1,128)S(1)} %get-tuple-element.12), channel_id=1, source_target_pairs={{480,96},{96,224},{224,352},{352,480},{481,97},{97,225},{225,353},... | collective-permute-start | bytes 4616 | tf_op jit(solution)/shard_map/ppermute | solution.py:264
  14.8 3.5 %collective-permute-start.3 = (f32[24,2048]{1,0:T(8,128)S(1)}, f32[24,2048]{1,0:T(8,128)S(1)}, u32[]{:S(2)}, u32[]{:S(2)}) collective-permute-start(f32[24,2048]{1,0:T(8,128)S(1)} %get-tuple-element.15), channel_id=1, source_target_pairs={{32,0},{0,32},{96,64},{64,96},{160,128},{128,160},{224,192},{192,2... | collective-permute-start | bytes 589832 | tf_op jit(solution)/shard_map/ppermute | solution.py:265
  20.4 33.0 %all-to-all-start = ((bf16[64,104,128]{2,1,0:T(8,128)(2,1)}), bf16[64,104,128]{2,1,0:T(8,128)(2,1)S(1)}, u32[]{:S(2)}, u32[]{:S(2)}) async-start(bf16[64,104,128]{2,1,0:T(8,128)(2,1)} %last_products.1), calls=%async_computation | async-start | bytes 3407872 | tf_op jit(solution)/shard_map/all_to_all | solution.py:23
  38.7 1.1 copy-start.1
  53.5 28.8 %all-to-all-start.1 = ((bf16[64,96,128]{2,1,0:T(8,128)(2,1)}), bf16[64,96,128]{2,1,0:T(8,128)(2,1)S(1)}, u32[]{:S(2)}, u32[]{:S(2)}) async-start(bf16[64,96,128]{2,1,0:T(8,128)(2,1)} %copy-done.1), calls=%async_computation.1 | async-start | bytes 3145728 | tf_op jit(solution)/shard_map/all_to_all | solution.py:23
  62.3 0.8 copy-start

commit v9 on v8

--- a/solution.py
+++ b/solution.py
@@ -193,17 +193,18 @@
     out[...] = together(totals)
 
 
-def near_sum_kernel(subsets, labels, got, before, out, held, sems, *totals):
-    (load,) = fetched([(before, held)], sems)
+def near_sum_kernel(subsets, numbers, got, before, out, labels, held, sems, *totals):
+    listing, load = fetched([(numbers, labels), (before, held)], sems)
     for total in totals:
         total[...] = jnp.zeros_like(total)
+    listing.wait()
 
     def one_part(part, carry):
         lister = part + jnp.where(part // subsets % 2 == 0, subsets, -subsets)
         add_up(labels, [part * PAIRS + LISTED, lister * PAIRS + 2 * LISTED], got, part, totals)
         return carry
 
-    lax.fori_loop(0, got.shape[0], one_part, 0)
+    lax.fori_loop(0, got.shape[0], one_part, 0, unroll=4)
     load.wait()
     out[...] = together((held,) + totals).reshape(out.shape).astype(out.dtype)
 
@@ -311,9 +312,9 @@
     sums = pl.pallas_call(
         functools.partial(near_sum_kernel, subsets),
         out_shape=jax.ShapeDtypeStruct((tiles * slab, width), jnp.bfloat16),
-        in_specs=[smem, vmem, hbm],
+        in_specs=[hbm, vmem, hbm],
         out_specs=vmem,
-        scratch_shapes=[chains[0], copied((1,))] + chains,
+        scratch_shapes=[pltpu.SMEM((parts * PAIRS,), jnp.int32), chains[0], copied((2,))] + chains,
         compiler_params=params,
         name="near_sums",
     )(labels, second, pltpu.with_memory_space_constraint(sums, pltpu.HBM))

time: 119 us -> 119 us (level)
  no operation moved by 1% of the time
where the time goes in v9:
time: 119 us; the launch traced here: 118 us
  waiting for transfers between devices  39.9 us (34%)
  blocking collectives  33 us (28%)
  starting transfers between devices  28.3 us (24%)
  Pallas kernels  13.8 us (12%)
  local copies, waits for them, and re-layouts  2.11 us (2%)
    all_to_all x1, blocking collectives, exchanged(): return lax.all_to_all(block, axis, split_axis=0, concat_axis=0, tiled=True)  33 us
    all_to_all x2, waiting for transfers between devices, exchanged(): return lax.all_to_all(block, axis, split_axis=0, concat_axis=0, tiled=True)  32.8 us
    all_to_all x2, starting transfers between devices, exchanged(): return lax.all_to_all(block, axis, split_axis=0, concat_axis=0, tiled=True)  14.6 us
    ppermute x1, waiting for transfers between devices, body(): near_block = lax.ppermute(jacobian[0], 'tx', near)  6.15 us
    ppermute x1, starting transfers between devices, body(): far_block = lax.ppermute(jacobian[0], 'tx', far)  4.41 us
    ppermute x1, starting transfers between devices, body(): near_block = lax.ppermute(jacobian[0], 'tx', near)  4.32 us
    pallas_call x1, Pallas kernels, body(): pl.pallas_call(own_kernel, out_shape=(first, held, pltpu.VMEM((rows - TAI...  3.47 us
    pallas_call x1, Pallas kernels, body(): pl.pallas_call(near_kernel, out_shape=jax.ShapeDtypeStruct((parts, 2 * LI...  3.38 us
  transfers between devices with their start and end apart: 7, of which 4 were waited for; matrix products, arithmetic and copies ran while one was open for 0% of the time, Pallas kernels for 10%

profile of v9, /device:TPU:32, one launch (start us, length us, event | category | flops | bytes accessed | tf_op | source)
XLA Modules:
  0.0 118.2 jit_solution(11868360517394526523)
XLA Ops:
  0.0 4.4 %collective-permute-start.1 = (bf16[256,2048]{1,0:T(8,128)(2,1)}, bf16[256,2048]{1,0:T(8,128)(2,1)S(1)}, u32[]{:S(2)}, u32[]{:S(2)}) collective-permute-start(bf16[256,2048]{1,0:T(8,128)(2,1)} %bitcast.13), channel_id=1, source_target_pairs={{128,32},{480,96},{256,160},{96,224},{384,288},{224,352},{0,416},{... | collective-permute-start | bytes 3145736 | tf_op jit(solution)/shard_map/ppermute | solution.py:232
  4.4 4.3 %collective-permute-start.4 = (bf16[256,2048]{1,0:T(8,128)(2,1)}, bf16[256,2048]{1,0:T(8,128)(2,1)}, u32[]{:S(2)}, u32[]{:S(2)}) collective-permute-start(bf16[256,2048]{1,0:T(8,128)(2,1)} %bitcast.14), channel_id=1, source_target_pairs={{96,0},{64,32},{160,64},{128,96},{224,128},{192,160},{288,192},{25... | collective-permute-start | bytes 3145736 | tf_op jit(solution)/shard_map/ppermute | solution.py:231
  8.8 3.5 %own_products.1 = (bf16[64,104,128]{2,1,0:T(8,128)(2,1)}, bf16[256,2048]{1,0:T(8,128)(2,1)S(1)}, bf16[240,2048]{1,0:T(8,128)(2,1)}, f32[1,384]{1,0:T(1,128)S(1)}...) custom-call(s32[1]{0:T(128)} %bitcast.refs_0_, s32[1,1,24]{2,1,0:T(1,128)} %refs_1_.1, s32[1,1,24]{2,1,0:T(1,128)} %refs_2_.1, ...), custom_call_target="tpu_custom_call" | custom-call | tf_op jit(solution)/shard_map/own_products/pallas_call | solution.py:240
  12.2 1.9 %collective-permute-start.2 = (bf16[240,2048]{1,0:T(8,128)(2,1)}, bf16[240,2048]{1,0:T(8,128)(2,1)S(1)}, u32[]{:S(2)}, u32[]{:S(2)}) collective-permute-start(bf16[240,2048]{1,0:T(8,128)(2,1)} %get-tuple-element.14), channel_id=1, source_target_pairs={{32,0},{0,32},{96,64},{64,96},{160,128},{128,160},{224,192},{192,2... | collective-permute-start | bytes 2949128 | tf_op jit(solution)/shard_map/ppermute | solution.py:264
  14.2 0.7 collective-permute-start
  14.8 2.4 %collective-permute-start.3 = (f32[24,2048]{1,0:T(8,128)S(1)}, f32[24,2048]{1,0:T(8,128)S(1)}, u32[]{:S(2)}, u32[]{:S(2)}) collective-permute-start(f32[24,2048]{1,0:T(8,128)S(1)} %get-tuple-element.15), channel_id=1, source_target_pairs={{32,0},{0,32},{96,64},{64,96},{160,128},{128,160},{224,192},{192,2... | collective-permute-start | bytes 589832 | tf_op jit(solution)/shard_map/ppermute | solution.py:266
  17.3 0.0 collective-permute-done
  17.3 0.1 pad_add_fusion.lists
  17.4 0.9 collective-permute-done.3.refs_2_.tail
  18.3 0.1 reshape.21.lists
  18.4 0.0 collective-permute-done.2.refs_1_.top
  18.4 0.0 collective-permute-done.1.refs_0_
  18.4 2.0 %last_products.1 = bf16[64,104,128]{2,1,0:T(8,128)(2,1)} custom-call(s32[13]{0:T(128)S(1)} %pad_add_fusion.lists, f32[1,384]{1,0:T(1,128)S(1)} %get-tuple-element.20.metas, bf16[256,2048]{1,0:T(8,128)(2,1)S(1)} %get-tuple-element.13.own, bf16[256,2048]{1,0:T(8,128)(2,1)S(1)} %collective-permute-done.1.refs_0_, ...), custom_call_target="tpu_custom_call", output_to_operand_aliasing={{}: (6, {})} | custom-call | tf_op jit(solution)/shard_map/last_products/pallas_call | solution.py:276
  20.4 8.8 %all-to-all-start = ((bf16[64,104,128]{2,1,0:T(8,128)(2,1)}), bf16[64,104,128]{2,1,0:T(8,128)(2,1)S(1)}, u32[]{:S(2)}, u32[]{:S(2)}) async-start(bf16[64,104,128]{2,1,0:T(8,128)(2,1)} %last_products.1), calls=%async_computation | async-start | bytes 3407872 | tf_op jit(solution)/shard_map/all_to_all | solution.py:23
  29.2 6.1 %collective-permute-done.4.near = bf16[256,2048]{1,0:T(8,128)(2,1)} collective-permute-done((bf16[256,2048]{1,0:T(8,128)(2,1)}, bf16[256,2048]{1,0:T(8,128)(2,1)}, u32[]{:S(2)}, u32[]{:S(2)}) %collective-permute-start.4) | collective-permute-done | bytes 1048608 | tf_op jit(solution)/shard_map/ppermute | solution.py:231
  35.3 3.4 %near_products.1 = bf16[64,96,128]{2,1,0:T(8,128)(2,1)S(1)} custom-call(s32[24]{0:T(128)S(1)} %reshape.21.lists, f32[2,384]{1,0:T(2,128)S(1)} %pad_maximum_fusion.1.metas, bf16[1,256,2048]{2,1,0:T(8,128)(2,1)} %whole.1, bf16[240,2048]{1,0:T(8,128)(2,1)S(1)} %collective-permute-done.2.refs_1_.top, f32[24,2048]{1,0:T(8,128)S(1)} %collective-permute-done.3.refs_2_.tail, ...), custom_call_target="tpu_custom_call" | custom-call | flops 99999997952 | bytes 8388608 | tf_op jit(solution)/shard_map/near_products/pallas_call | solution.py:290
  38.7 0.0 copy-start.1
  38.7 1.1 copy-done.1
  39.9 13.6 %all-to-all-done.got = bf16[64,104,128]{2,1,0:T(8,128)(2,1)S(1)} async-done(((bf16[64,104,128]{2,1,0:T(8,128)(2,1)}), bf16[64,104,128]{2,1,0:T(8,128)(2,1)S(1)}, u32[]{:S(2)}, u32[]{:S(2)}) %all-to-all-start) | async-done | bytes 1703968 | tf_op jit(solution)/shard_map/all_to_all | solution.py:23
  53.5 5.8 %all-to-all-start.1 = ((bf16[64,96,128]{2,1,0:T(8,128)(2,1)}), bf16[64,96,128]{2,1,0:T(8,128)(2,1)S(1)}, u32[]{:S(2)}, u32[]{:S(2)}) async-start(bf16[64,96,128]{2,1,0:T(8,128)(2,1)} %copy-done.1), calls=%async_computation.1 | async-start | bytes 3145728 | tf_op jit(solution)/shard_map/all_to_all | solution.py:23
  59.3 0.1 fusion
  59.4 0.1 reshape.22.labels.numbers
  59.5 2.8 %first_sums.1.before = f32[128,8,128]{2,1,0:T(8,128)S(1)} custom-call(s32[1536]{0:T(1024)S(1)} %reshape.22.labels.numbers, bf16[64,104,128]{2,1,0:T(8,128)(2,1)S(1)} %all-to-all-done.got), custom_call_target="tpu_custom_call" | custom-call | tf_op jit(solution)/shard_map/first_sums/pallas_call | solution.py:303
  62.3 0.0 copy-start
  62.3 0.8 copy-done
  63.1 19.1 %all-to-all-done.1.got = bf16[64,96,128]{2,1,0:T(8,128)(2,1)S(1)} async-done(((bf16[64,96,128]{2,1,0:T(8,128)(2,1)}), bf16[64,96,128]{2,1,0:T(8,128)(2,1)S(1)}, u32[]{:S(2)}, u32[]{:S(2)}) %all-to-all-start.1) | async-done | bytes 1572896 | tf_op jit(solution)/shard_map/all_to_all | solution.py:23
  82.2 2.3 %near_sums.1 = bf16[1024,128]{1,0:T(8,128)(2,1)S(1)} custom-call(s32[1536]{0:T(1024)S(1)} %reshape.22.labels.numbers, bf16[64,96,128]{2,1,0:T(8,128)(2,1)S(1)} %all-to-all-done.1.got, f32[128,8,128]{2,1,0:T(8,128)} %copy-done), custom_call_target="tpu_custom_call" | custom-call | tf_op jit(solution)/shard_map/near_sums/pallas_call | solution.py:312
  84.5 33.0 %all_to_all.19 = bf16[16,64,128]{2,1,0:T(8,128)(2,1)S(1)} all-to-all(bf16[16,64,128]{2,1,0:T(8,128)(2,1)S(1)} %bitcast.11), channel_id=1, replica_groups=mesh['tx'=16,'mp_hi'=8,'mp_lo'=2,'rep'=2] {'mp_hi','mp_lo'}, dimensions={0} | all-to-all | bytes 524288 | tf_op jit(solution)/shard_map/all_to_all | solution.py:23
  117.6 0.6 pad_maximum_fusion
  (7 shorter events, 0.1 us)
Async XLA Ops:
  0.0 18.4 %collective-permute-start.1 = (bf16[256,2048]{1,0:T(8,128)(2,1)}, bf16[256,2048]{1,0:T(8,128)(2,1)S(1)}, u32[]{:S(2)}, u32[]{:S(2)}) collective-permute-start(bf16[256,2048]{1,0:T(8,128)(2,1)} %bitcast.13), channel_id=1, source_target_pairs={{128,32},{480,96},{256,160},{96,224},{384,288},{224,352},{0,416},{... | collective-permute-start | bytes 3145736 | tf_op jit(solution)/shard_map/ppermute | solution.py:232
  4.4 30.9 %collective-permute-start.4 = (bf16[256,2048]{1,0:T(8,128)(2,1)}, bf16[256,2048]{1,0:T(8,128)(2,1)}, u32[]{:S(2)}, u32[]{:S(2)}) collective-permute-start(bf16[256,2048]{1,0:T(8,128)(2,1)} %bitcast.14), channel_id=1, source_target_pairs={{96,0},{64,32},{160,64},{128,96},{224,128},{192,160},{288,192},{25... | collective-permute-start | bytes 3145736 | tf_op jit(solution)/shard_map/ppermute | solution.py:231
  12.2 6.2 %collective-permute-start.2 = (bf16[240,2048]{1,0:T(8,128)(2,1)}, bf16[240,2048]{1,0:T(8,128)(2,1)S(1)}, u32[]{:S(2)}, u32[]{:S(2)}) collective-permute-start(bf16[240,2048]{1,0:T(8,128)(2,1)} %get-tuple-element.14), channel_id=1, source_target_pairs={{32,0},{0,32},{96,64},{64,96},{160,128},{128,160},{224,192},{192,2... | collective-permute-start | bytes 2949128 | tf_op jit(solution)/shard_map/ppermute | solution.py:264
  14.2 3.1 %collective-permute-start = (f32[1,384]{1,0:T(1,128)S(1)}, f32[1,384]{1,0:T(1,128)S(1)}, u32[]{:S(2)}, u32[]{:S(2)}) collective-permute-start(f32[1,384]{1,0:T(1,128)S(1)} %get-tuple-element.12), channel_id=1, source_target_pairs={{480,96},{96,224},{224,352},{352,480},{481,97},{97,225},{225,353},... | collective-permute-start | bytes 4616 | tf_op jit(solution)/shard_map/ppermute | solution.py:265
  14.8 3.5 %collective-permute-start.3 = (f32[24,2048]{1,0:T(8,128)S(1)}, f32[24,2048]{1,0:T(8,128)S(1)}, u32[]{:S(2)}, u32[]{:S(2)}) collective-permute-start(f32[24,2048]{1,0:T(8,128)S(1)} %get-tuple-element.15), channel_id=1, source_target_pairs={{32,0},{0,32},{96,64},{64,96},{160,128},{128,160},{224,192},{192,2... | collective-permute-start | bytes 589832 | tf_op jit(solution)/shard_map/ppermute | solution.py:266
  20.4 33.1 %all-to-all-start = ((bf16[64,104,128]{2,1,0:T(8,128)(2,1)}), bf16[64,104,128]{2,1,0:T(8,128)(2,1)S(1)}, u32[]{:S(2)}, u32[]{:S(2)}) async-start(bf16[64,104,128]{2,1,0:T(8,128)(2,1)} %last_products.1), calls=%async_computation | async-start | bytes 3407872 | tf_op jit(solution)/shard_map/all_to_all | solution.py:23
  38.7 1.1 copy-start.1
  53.5 28.7 %all-to-all-start.1 = ((bf16[64,96,128]{2,1,0:T(8,128)(2,1)}), bf16[64,96,128]{2,1,0:T(8,128)(2,1)S(1)}, u32[]{:S(2)}, u32[]{:S(2)}) async-start(bf16[64,96,128]{2,1,0:T(8,128)(2,1)} %copy-done.1), calls=%async_computation.1 | async-start | bytes 3145728 | tf_op jit(solution)/shard_map/all_to_all | solution.py:23
  62.3 0.8 copy-start

commit v10 on v9

--- a/solution.py
+++ b/solution.py
@@ -204,7 +204,7 @@
         add_up(labels, [part * PAIRS + LISTED, lister * PAIRS + 2 * LISTED], got, part, totals)
         return carry
 
-    lax.fori_loop(0, got.shape[0], one_part, 0, unroll=4)
+    lax.fori_loop(0, got.shape[0], one_part, 0, unroll=8)
     load.wait()
     out[...] = together((held,) + totals).reshape(out.shape).astype(out.dtype)
 

time: 119 us -> 119 us (level)
  no operation moved by 1% of the time
where the time goes in v10:
time: 119 us; the launch traced here: 118 us
  waiting for transfers between devices  39.9 us (34%)
  blocking collectives  33 us (28%)
  starting transfers between devices  28.3 us (24%)
  Pallas kernels  13.8 us (12%)
  local copies, waits for them, and re-layouts  2.11 us (2%)
    all_to_all x1, blocking collectives, exchanged(): return lax.all_to_all(block, axis, split_axis=0, concat_axis=0, tiled=True)  33 us
    all_to_all x2, waiting for transfers between devices, exchanged(): return lax.all_to_all(block, axis, split_axis=0, concat_axis=0, tiled=True)  32.8 us
    all_to_all x2, starting transfers between devices, exchanged(): return lax.all_to_all(block, axis, split_axis=0, concat_axis=0, tiled=True)  14.6 us
    ppermute x1, waiting for transfers between devices, body(): near_block = lax.ppermute(jacobian[0], 'tx', near)  6.16 us
    ppermute x1, starting transfers between devices, body(): far_block = lax.ppermute(jacobian[0], 'tx', far)  4.41 us
    ppermute x1, starting transfers between devices, body(): near_block = lax.ppermute(jacobian[0], 'tx', near)  4.32 us
    pallas_call x1, Pallas kernels, body(): pl.pallas_call(own_kernel, out_shape=(first, held, pltpu.VMEM((rows - TAI...  3.44 us
    pallas_call x1, Pallas kernels, body(): pl.pallas_call(near_kernel, out_shape=jax.ShapeDtypeStruct((parts, 2 * LI...  3.38 us
  transfers between devices with their start and end apart: 7, of which 4 were waited for; matrix products, arithmetic and copies ran while one was open for 0% of the time, Pallas kernels for 10%

profile of v10, /device:TPU:32, one launch (start us, length us, event | category | flops | bytes accessed | tf_op | source)
XLA Modules:
  0.0 118.2 jit_solution(16927536256741932423)
XLA Ops:
  0.0 4.4 %collective-permute-start.1 = (bf16[256,2048]{1,0:T(8,128)(2,1)}, bf16[256,2048]{1,0:T(8,128)(2,1)S(1)}, u32[]{:S(2)}, u32[]{:S(2)}) collective-permute-start(bf16[256,2048]{1,0:T(8,128)(2,1)} %bitcast.13), channel_id=1, source_target_pairs={{128,32},{480,96},{256,160},{96,224},{384,288},{224,352},{0,416},{... | collective-permute-start | bytes 3145736 | tf_op jit(solution)/shard_map/ppermute | solution.py:232
  4.4 4.3 %collective-permute-start.4 = (bf16[256,2048]{1,0:T(8,128)(2,1)}, bf16[256,2048]{1,0:T(8,128)(2,1)}, u32[]{:S(2)}, u32[]{:S(2)}) collective-permute-start(bf16[256,2048]{1,0:T(8,128)(2,1)} %bitcast.14), channel_id=1, source_target_pairs={{96,0},{64,32},{160,64},{128,96},{224,128},{192,160},{288,192},{25... | collective-permute-start | bytes 3145736 | tf_op jit(solution)/shard_map/ppermute | solution.py:231
  8.8 3.4 %own_products.1 = (bf16[64,104,128]{2,1,0:T(8,128)(2,1)}, bf16[256,2048]{1,0:T(8,128)(2,1)S(1)}, bf16[240,2048]{1,0:T(8,128)(2,1)}, f32[1,384]{1,0:T(1,128)S(1)}...) custom-call(s32[1]{0:T(128)} %bitcast.refs_0_, s32[1,1,24]{2,1,0:T(1,128)} %refs_1_.1, s32[1,1,24]{2,1,0:T(1,128)} %refs_2_.1, ...), custom_call_target="tpu_custom_call" | custom-call | tf_op jit(solution)/shard_map/own_products/pallas_call | solution.py:240
  12.2 1.9 %collective-permute-start.2 = (bf16[240,2048]{1,0:T(8,128)(2,1)}, bf16[240,2048]{1,0:T(8,128)(2,1)S(1)}, u32[]{:S(2)}, u32[]{:S(2)}) collective-permute-start(bf16[240,2048]{1,0:T(8,128)(2,1)} %get-tuple-element.14), channel_id=1, source_target_pairs={{32,0},{0,32},{96,64},{64,96},{160,128},{128,160},{224,192},{192,2... | collective-permute-start | bytes 2949128 | tf_op jit(solution)/shard_map/ppermute | solution.py:264
  14.1 0.7 collective-permute-start
  14.8 2.4 %collective-permute-start.3 = (f32[24,2048]{1,0:T(8,128)S(1)}, f32[24,2048]{1,0:T(8,128)S(1)}, u32[]{:S(2)}, u32[]{:S(2)}) collective-permute-start(f32[24,2048]{1,0:T(8,128)S(1)} %get-tuple-element.15), channel_id=1, source_target_pairs={{32,0},{0,32},{96,64},{64,96},{160,128},{128,160},{224,192},{192,2... | collective-permute-start | bytes 589832 | tf_op jit(solution)/shard_map/ppermute | solution.py:266
  17.2 0.0 collective-permute-done
  17.3 0.1 pad_add_fusion.lists
  17.3 0.9 collective-permute-done.3.refs_2_.tail
  18.3 0.1 reshape.21.lists
  18.4 0.0 collective-permute-done.2.refs_1_.top
  18.4 0.0 collective-permute-done.1.refs_0_
  18.4 2.0 %last_products.1 = bf16[64,104,128]{2,1,0:T(8,128)(2,1)} custom-call(s32[13]{0:T(128)S(1)} %pad_add_fusion.lists, f32[1,384]{1,0:T(1,128)S(1)} %get-tuple-element.20.metas, bf16[256,2048]{1,0:T(8,128)(2,1)S(1)} %get-tuple-element.13.own, bf16[256,2048]{1,0:T(8,128)(2,1)S(1)} %collective-permute-done.1.refs_0_, ...), custom_call_target="tpu_custom_call", output_to_operand_aliasing={{}: (6, {})} | custom-call | tf_op jit(solution)/shard_map/last_products/pallas_call | solution.py:276
  20.4 8.8 %all-to-all-start = ((bf16[64,104,128]{2,1,0:T(8,128)(2,1)}), bf16[64,104,128]{2,1,0:T(8,128)(2,1)S(1)}, u32[]{:S(2)}, u32[]{:S(2)}) async-start(bf16[64,104,128]{2,1,0:T(8,128)(2,1)} %last_products.1), calls=%async_computation | async-start | bytes 3407872 | tf_op jit(solution)/shard_map/all_to_all | solution.py:23
  29.2 6.2 %collective-permute-done.4.near = bf16[256,2048]{1,0:T(8,128)(2,1)} collective-permute-done((bf16[256,2048]{1,0:T(8,128)(2,1)}, bf16[256,2048]{1,0:T(8,128)(2,1)}, u32[]{:S(2)}, u32[]{:S(2)}) %collective-permute-start.4) | collective-permute-done | bytes 1048608 | tf_op jit(solution)/shard_map/ppermute | solution.py:231
  35.3 3.4 %near_products.1 = bf16[64,96,128]{2,1,0:T(8,128)(2,1)S(1)} custom-call(s32[24]{0:T(128)S(1)} %reshape.21.lists, f32[2,384]{1,0:T(2,128)S(1)} %pad_maximum_fusion.1.metas, bf16[1,256,2048]{2,1,0:T(8,128)(2,1)} %whole.1, bf16[240,2048]{1,0:T(8,128)(2,1)S(1)} %collective-permute-done.2.refs_1_.top, f32[24,2048]{1,0:T(8,128)S(1)} %collective-permute-done.3.refs_2_.tail, ...), custom_call_target="tpu_custom_call" | custom-call | flops 99999997952 | bytes 8388608 | tf_op jit(solution)/shard_map/near_products/pallas_call | solution.py:290
  38.7 0.0 copy-start.1
  38.7 1.1 copy-done.1
  39.9 13.6 %all-to-all-done.got = bf16[64,104,128]{2,1,0:T(8,128)(2,1)S(1)} async-done(((bf16[64,104,128]{2,1,0:T(8,128)(2,1)}), bf16[64,104,128]{2,1,0:T(8,128)(2,1)S(1)}, u32[]{:S(2)}, u32[]{:S(2)}) %all-to-all-start) | async-done | bytes 1703968 | tf_op jit(solution)/shard_map/all_to_all | solution.py:23
  53.5 5.8 %all-to-all-start.1 = ((bf16[64,96,128]{2,1,0:T(8,128)(2,1)}), bf16[64,96,128]{2,1,0:T(8,128)(2,1)S(1)}, u32[]{:S(2)}, u32[]{:S(2)}) async-start(bf16[64,96,128]{2,1,0:T(8,128)(2,1)} %copy-done.1), calls=%async_computation.1 | async-start | bytes 3145728 | tf_op jit(solution)/shard_map/all_to_all | solution.py:23
  59.3 0.1 fusion
  59.4 0.1 reshape.22.labels.numbers
  59.5 2.8 %first_sums.1.before = f32[128,8,128]{2,1,0:T(8,128)S(1)} custom-call(s32[1536]{0:T(1024)S(1)} %reshape.22.labels.numbers, bf16[64,104,128]{2,1,0:T(8,128)(2,1)S(1)} %all-to-all-done.got), custom_call_target="tpu_custom_call" | custom-call | tf_op jit(solution)/shard_map/first_sums/pallas_call | solution.py:303
  62.3 0.0 copy-start
  62.3 0.8 copy-done
  63.1 19.1 %all-to-all-done.1.got = bf16[64,96,128]{2,1,0:T(8,128)(2,1)S(1)} async-done(((bf16[64,96,128]{2,1,0:T(8,128)(2,1)}), bf16[64,96,128]{2,1,0:T(8,128)(2,1)S(1)}, u32[]{:S(2)}, u32[]{:S(2)}) %all-to-all-start.1) | async-done | bytes 1572896 | tf_op jit(solution)/shard_map/all_to_all | solution.py:23
  82.2 2.2 %near_sums.1 = bf16[1024,128]{1,0:T(8,128)(2,1)S(1)} custom-call(s32[1536]{0:T(1024)S(1)} %reshape.22.labels.numbers, bf16[64,96,128]{2,1,0:T(8,128)(2,1)S(1)} %all-to-all-done.1.got, f32[128,8,128]{2,1,0:T(8,128)} %copy-done), custom_call_target="tpu_custom_call" | custom-call | tf_op jit(solution)/shard_map/near_sums/pallas_call | solution.py:312
  84.5 33.0 %all_to_all.19 = bf16[16,64,128]{2,1,0:T(8,128)(2,1)S(1)} all-to-all(bf16[16,64,128]{2,1,0:T(8,128)(2,1)S(1)} %bitcast.11), channel_id=1, replica_groups=mesh['tx'=16,'mp_hi'=8,'mp_lo'=2,'rep'=2] {'mp_hi','mp_lo'}, dimensions={0} | all-to-all | bytes 524288 | tf_op jit(solution)/shard_map/all_to_all | solution.py:23
  117.5 0.6 pad_maximum_fusion
  (7 shorter events, 0.1 us)
Async XLA Ops:
  0.0 18.4 %collective-permute-start.1 = (bf16[256,2048]{1,0:T(8,128)(2,1)}, bf16[256,2048]{1,0:T(8,128)(2,1)S(1)}, u32[]{:S(2)}, u32[]{:S(2)}) collective-permute-start(bf16[256,2048]{1,0:T(8,128)(2,1)} %bitcast.13), channel_id=1, source_target_pairs={{128,32},{480,96},{256,160},{96,224},{384,288},{224,352},{0,416},{... | collective-permute-start | bytes 3145736 | tf_op jit(solution)/shard_map/ppermute | solution.py:232
  4.4 30.9 %collective-permute-start.4 = (bf16[256,2048]{1,0:T(8,128)(2,1)}, bf16[256,2048]{1,0:T(8,128)(2,1)}, u32[]{:S(2)}, u32[]{:S(2)}) collective-permute-start(bf16[256,2048]{1,0:T(8,128)(2,1)} %bitcast.14), channel_id=1, source_target_pairs={{96,0},{64,32},{160,64},{128,96},{224,128},{192,160},{288,192},{25... | collective-permute-start | bytes 3145736 | tf_op jit(solution)/shard_map/ppermute | solution.py:231
  12.2 6.2 %collective-permute-start.2 = (bf16[240,2048]{1,0:T(8,128)(2,1)}, bf16[240,2048]{1,0:T(8,128)(2,1)S(1)}, u32[]{:S(2)}, u32[]{:S(2)}) collective-permute-start(bf16[240,2048]{1,0:T(8,128)(2,1)} %get-tuple-element.14), channel_id=1, source_target_pairs={{32,0},{0,32},{96,64},{64,96},{160,128},{128,160},{224,192},{192,2... | collective-permute-start | bytes 2949128 | tf_op jit(solution)/shard_map/ppermute | solution.py:264
  14.1 3.1 %collective-permute-start = (f32[1,384]{1,0:T(1,128)S(1)}, f32[1,384]{1,0:T(1,128)S(1)}, u32[]{:S(2)}, u32[]{:S(2)}) collective-permute-start(f32[1,384]{1,0:T(1,128)S(1)} %get-tuple-element.12), channel_id=1, source_target_pairs={{480,96},{96,224},{224,352},{352,480},{481,97},{97,225},{225,353},... | collective-permute-start | bytes 4616 | tf_op jit(solution)/shard_map/ppermute | solution.py:265
  14.8 3.5 %collective-permute-start.3 = (f32[24,2048]{1,0:T(8,128)S(1)}, f32[24,2048]{1,0:T(8,128)S(1)}, u32[]{:S(2)}, u32[]{:S(2)}) collective-permute-start(f32[24,2048]{1,0:T(8,128)S(1)} %get-tuple-element.15), channel_id=1, source_target_pairs={{32,0},{0,32},{96,64},{64,96},{160,128},{128,160},{224,192},{192,2... | collective-permute-start | bytes 589832 | tf_op jit(solution)/shard_map/ppermute | solution.py:266
  20.4 33.1 %all-to-all-start = ((bf16[64,104,128]{2,1,0:T(8,128)(2,1)}), bf16[64,104,128]{2,1,0:T(8,128)(2,1)S(1)}, u32[]{:S(2)}, u32[]{:S(2)}) async-start(bf16[64,104,128]{2,1,0:T(8,128)(2,1)} %last_products.1), calls=%async_computation | async-start | bytes 3407872 | tf_op jit(solution)/shard_map/all_to_all | solution.py:23
  38.7 1.1 copy-start.1
  53.5 28.8 %all-to-all-start.1 = ((bf16[64,96,128]{2,1,0:T(8,128)(2,1)}), bf16[64,96,128]{2,1,0:T(8,128)(2,1)S(1)}, u32[]{:S(2)}, u32[]{:S(2)}) async-start(bf16[64,96,128]{2,1,0:T(8,128)(2,1)} %copy-done.1), calls=%async_computation.1 | async-start | bytes 3145728 | tf_op jit(solution)/shard_map/all_to_all | solution.py:23
  62.3 0.8 copy-start

commit v11 on v10

--- a/solution.py
+++ b/solution.py
@@ -204,7 +204,7 @@
         add_up(labels, [part * PAIRS + LISTED, lister * PAIRS + 2 * LISTED], got, part, totals)
         return carry
 
-    lax.fori_loop(0, got.shape[0], one_part, 0, unroll=8)
+    lax.fori_loop(0, got.shape[0], one_part, 0, unroll=16)
     load.wait()
     out[...] = together((held,) + totals).reshape(out.shape).astype(out.dtype)
 

time: 119 us -> 119 us (level)
  no operation moved by 1% of the time
where the time goes in v11:
time: 119 us; the launch traced here: 118 us
  waiting for transfers between devices  39.9 us (34%)
  blocking collectives  33 us (28%)
  starting transfers between devices  28.3 us (24%)
  Pallas kernels  13.8 us (12%)
  local copies, waits for them, and re-layouts  2.11 us (2%)
    all_to_all x1, blocking collectives, exchanged(): return lax.all_to_all(block, axis, split_axis=0, concat_axis=0, tiled=True)  33 us
    all_to_all x2, waiting for transfers between devices, exchanged(): return lax.all_to_all(block, axis, split_axis=0, concat_axis=0, tiled=True)  32.8 us
    all_to_all x2, starting transfers between devices, exchanged(): return lax.all_to_all(block, axis, split_axis=0, concat_axis=0, tiled=True)  14.6 us
    ppermute x1, waiting for transfers between devices, body(): near_block = lax.ppermute(jacobian[0], 'tx', near)  6.18 us
    ppermute x1, starting transfers between devices, body(): far_block = lax.ppermute(jacobian[0], 'tx', far)  4.41 us
    ppermute x1, starting transfers between devices, body(): near_block = lax.ppermute(jacobian[0], 'tx', near)  4.32 us
    pallas_call x1, Pallas kernels, body(): pl.pallas_call(own_kernel, out_shape=(first, held, pltpu.VMEM((rows - TAI...  3.44 us
    pallas_call x1, Pallas kernels, body(): pl.pallas_call(near_kernel, out_shape=jax.ShapeDtypeStruct((parts, 2 * LI...  3.38 us
  transfers between devices with their start and end apart: 7, of which 4 were waited for; matrix products, arithmetic and copies ran while one was open for 0% of the time, Pallas kernels for 10%

profile of v11, /device:TPU:32, one launch (start us, length us, event | category | flops | bytes accessed | tf_op | source)
XLA Modules:
  0.0 118.2 jit_solution(2398090738872016691)
XLA Ops:
  0.0 4.4 %collective-permute-start.1 = (bf16[256,2048]{1,0:T(8,128)(2,1)}, bf16[256,2048]{1,0:T(8,128)(2,1)S(1)}, u32[]{:S(2)}, u32[]{:S(2)}) collective-permute-start(bf16[256,2048]{1,0:T(8,128)(2,1)} %bitcast.13), channel_id=1, source_target_pairs={{128,32},{480,96},{256,160},{96,224},{384,288},{224,352},{0,416},{... | collective-permute-start | bytes 3145736 | tf_op jit(solution)/shard_map/ppermute | solution.py:232
  4.4 4.3 %collective-permute-start.4 = (bf16[256,2048]{1,0:T(8,128)(2,1)}, bf16[256,2048]{1,0:T(8,128)(2,1)}, u32[]{:S(2)}, u32[]{:S(2)}) collective-permute-start(bf16[256,2048]{1,0:T(8,128)(2,1)} %bitcast.14), channel_id=1, source_target_pairs={{96,0},{64,32},{160,64},{128,96},{224,128},{192,160},{288,192},{25... | collective-permute-start | bytes 3145736 | tf_op jit(solution)/shard_map/ppermute | solution.py:231
  8.8 3.4 %own_products.1 = (bf16[64,104,128]{2,1,0:T(8,128)(2,1)}, bf16[256,2048]{1,0:T(8,128)(2,1)S(1)}, bf16[240,2048]{1,0:T(8,128)(2,1)}, f32[1,384]{1,0:T(1,128)S(1)}...) custom-call(s32[1]{0:T(128)} %bitcast.refs_0_, s32[1,1,24]{2,1,0:T(1,128)} %refs_1_.1, s32[1,1,24]{2,1,0:T(1,128)} %refs_2_.1, ...), custom_call_target="tpu_custom_call" | custom-call | tf_op jit(solution)/shard_map/own_products/pallas_call | solution.py:240
  12.2 1.9 %collective-permute-start.2 = (bf16[240,2048]{1,0:T(8,128)(2,1)}, bf16[240,2048]{1,0:T(8,128)(2,1)S(1)}, u32[]{:S(2)}, u32[]{:S(2)}) collective-permute-start(bf16[240,2048]{1,0:T(8,128)(2,1)} %get-tuple-element.14), channel_id=1, source_target_pairs={{32,0},{0,32},{96,64},{64,96},{160,128},{128,160},{224,192},{192,2... | collective-permute-start | bytes 2949128 | tf_op jit(solution)/shard_map/ppermute | solution.py:264
  14.1 0.7 collective-permute-start
  14.8 2.4 %collective-permute-start.3 = (f32[24,2048]{1,0:T(8,128)S(1)}, f32[24,2048]{1,0:T(8,128)S(1)}, u32[]{:S(2)}, u32[]{:S(2)}) collective-permute-start(f32[24,2048]{1,0:T(8,128)S(1)} %get-tuple-element.15), channel_id=1, source_target_pairs={{32,0},{0,32},{96,64},{64,96},{160,128},{128,160},{224,192},{192,2... | collective-permute-start | bytes 589832 | tf_op jit(solution)/shard_map/ppermute | solution.py:266
  17.2 0.0 collective-permute-done
  17.3 0.1 pad_add_fusion.lists
  17.3 0.9 collective-permute-done.3.refs_2_.tail
  18.3 0.1 reshape.21.lists
  18.4 0.0 collective-permute-done.2.refs_1_.top
  18.4 0.0 collective-permute-done.1.refs_0_
  18.4 2.0 %last_products.1 = bf16[64,104,128]{2,1,0:T(8,128)(2,1)} custom-call(s32[13]{0:T(128)S(1)} %pad_add_fusion.lists, f32[1,384]{1,0:T(1,128)S(1)} %get-tuple-element.20.metas, bf16[256,2048]{1,0:T(8,128)(2,1)S(1)} %get-tuple-element.13.own, bf16[256,2048]{1,0:T(8,128)(2,1)S(1)} %collective-permute-done.1.refs_0_, ...), custom_call_target="tpu_custom_call", output_to_operand_aliasing={{}: (6, {})} | custom-call | tf_op jit(solution)/shard_map/last_products/pallas_call | solution.py:276
  20.4 8.7 %all-to-all-start = ((bf16[64,104,128]{2,1,0:T(8,128)(2,1)}), bf16[64,104,128]{2,1,0:T(8,128)(2,1)S(1)}, u32[]{:S(2)}, u32[]{:S(2)}) async-start(bf16[64,104,128]{2,1,0:T(8,128)(2,1)} %last_products.1), calls=%async_computation | async-start | bytes 3407872 | tf_op jit(solution)/shard_map/all_to_all | solution.py:23
  29.2 6.2 %collective-permute-done.4.near = bf16[256,2048]{1,0:T(8,128)(2,1)} collective-permute-done((bf16[256,2048]{1,0:T(8,128)(2,1)}, bf16[256,2048]{1,0:T(8,128)(2,1)}, u32[]{:S(2)}, u32[]{:S(2)}) %collective-permute-start.4) | collective-permute-done | bytes 1048608 | tf_op jit(solution)/shard_map/ppermute | solution.py:231
  35.3 3.4 %near_products.1 = bf16[64,96,128]{2,1,0:T(8,128)(2,1)S(1)} custom-call(s32[24]{0:T(128)S(1)} %reshape.21.lists, f32[2,384]{1,0:T(2,128)S(1)} %pad_maximum_fusion.1.metas, bf16[1,256,2048]{2,1,0:T(8,128)(2,1)} %whole.1, bf16[240,2048]{1,0:T(8,128)(2,1)S(1)} %collective-permute-done.2.refs_1_.top, f32[24,2048]{1,0:T(8,128)S(1)} %collective-permute-done.3.refs_2_.tail, ...), custom_call_target="tpu_custom_call" | custom-call | flops 99999997952 | bytes 8388608 | tf_op jit(solution)/shard_map/near_products/pallas_call | solution.py:290
  38.7 0.0 copy-start.1
  38.7 1.1 copy-done.1
  39.9 13.6 %all-to-all-done.got = bf16[64,104,128]{2,1,0:T(8,128)(2,1)S(1)} async-done(((bf16[64,104,128]{2,1,0:T(8,128)(2,1)}), bf16[64,104,128]{2,1,0:T(8,128)(2,1)S(1)}, u32[]{:S(2)}, u32[]{:S(2)}) %all-to-all-start) | async-done | bytes 1703968 | tf_op jit(solution)/shard_map/all_to_all | solution.py:23
  53.5 5.8 %all-to-all-start.1 = ((bf16[64,96,128]{2,1,0:T(8,128)(2,1)}), bf16[64,96,128]{2,1,0:T(8,128)(2,1)S(1)}, u32[]{:S(2)}, u32[]{:S(2)}) async-start(bf16[64,96,128]{2,1,0:T(8,128)(2,1)} %copy-done.1), calls=%async_computation.1 | async-start | bytes 3145728 | tf_op jit(solution)/shard_map/all_to_all | solution.py:23
  59.3 0.1 fusion
  59.4 0.1 reshape.22.labels.numbers
  59.5 2.8 %first_sums.1.before = f32[128,8,128]{2,1,0:T(8,128)S(1)} custom-call(s32[1536]{0:T(1024)S(1)} %reshape.22.labels.numbers, bf16[64,104,128]{2,1,0:T(8,128)(2,1)S(1)} %all-to-all-done.got), custom_call_target="tpu_custom_call" | custom-call | tf_op jit(solution)/shard_map/first_sums/pallas_call | solution.py:303
  62.3 0.0 copy-start
  62.3 0.8 copy-done
  63.1 19.1 %all-to-all-done.1.got = bf16[64,96,128]{2,1,0:T(8,128)(2,1)S(1)} async-done(((bf16[64,96,128]{2,1,0:T(8,128)(2,1)}), bf16[64,96,128]{2,1,0:T(8,128)(2,1)S(1)}, u32[]{:S(2)}, u32[]{:S(2)}) %all-to-all-start.1) | async-done | bytes 1572896 | tf_op jit(solution)/shard_map/all_to_all | solution.py:23
  82.2 2.2 %near_sums.1 = bf16[1024,128]{1,0:T(8,128)(2,1)S(1)} custom-call(s32[1536]{0:T(1024)S(1)} %reshape.22.labels.numbers, bf16[64,96,128]{2,1,0:T(8,128)(2,1)S(1)} %all-to-all-done.1.got, f32[128,8,128]{2,1,0:T(8,128)} %copy-done), custom_call_target="tpu_custom_call" | custom-call | tf_op jit(solution)/shard_map/near_sums/pallas_call | solution.py:312
  84.4 33.0 %all_to_all.19 = bf16[16,64,128]{2,1,0:T(8,128)(2,1)S(1)} all-to-all(bf16[16,64,128]{2,1,0:T(8,128)(2,1)S(1)} %bitcast.11), channel_id=1, replica_groups=mesh['tx'=16,'mp_hi'=8,'mp_lo'=2,'rep'=2] {'mp_hi','mp_lo'}, dimensions={0} | all-to-all | bytes 524288 | tf_op jit(solution)/shard_map/all_to_all | solution.py:23
  117.5 0.6 pad_maximum_fusion
  (7 shorter events, 0.1 us)
Async XLA Ops:
  0.0 18.4 %collective-permute-start.1 = (bf16[256,2048]{1,0:T(8,128)(2,1)}, bf16[256,2048]{1,0:T(8,128)(2,1)S(1)}, u32[]{:S(2)}, u32[]{:S(2)}) collective-permute-start(bf16[256,2048]{1,0:T(8,128)(2,1)} %bitcast.13), channel_id=1, source_target_pairs={{128,32},{480,96},{256,160},{96,224},{384,288},{224,352},{0,416},{... | collective-permute-start | bytes 3145736 | tf_op jit(solution)/shard_map/ppermute | solution.py:232
  4.4 30.9 %collective-permute-start.4 = (bf16[256,2048]{1,0:T(8,128)(2,1)}, bf16[256,2048]{1,0:T(8,128)(2,1)}, u32[]{:S(2)}, u32[]{:S(2)}) collective-permute-start(bf16[256,2048]{1,0:T(8,128)(2,1)} %bitcast.14), channel_id=1, source_target_pairs={{96,0},{64,32},{160,64},{128,96},{224,128},{192,160},{288,192},{25... | collective-permute-start | bytes 3145736 | tf_op jit(solution)/shard_map/ppermute | solution.py:231
  12.2 6.2 %collective-permute-start.2 = (bf16[240,2048]{1,0:T(8,128)(2,1)}, bf16[240,2048]{1,0:T(8,128)(2,1)S(1)}, u32[]{:S(2)}, u32[]{:S(2)}) collective-permute-start(bf16[240,2048]{1,0:T(8,128)(2,1)} %get-tuple-element.14), channel_id=1, source_target_pairs={{32,0},{0,32},{96,64},{64,96},{160,128},{128,160},{224,192},{192,2... | collective-permute-start | bytes 2949128 | tf_op jit(solution)/shard_map/ppermute | solution.py:264
  14.1 3.1 %collective-permute-start = (f32[1,384]{1,0:T(1,128)S(1)}, f32[1,384]{1,0:T(1,128)S(1)}, u32[]{:S(2)}, u32[]{:S(2)}) collective-permute-start(f32[1,384]{1,0:T(1,128)S(1)} %get-tuple-element.12), channel_id=1, source_target_pairs={{480,96},{96,224},{224,352},{352,480},{481,97},{97,225},{225,353},... | collective-permute-start | bytes 4616 | tf_op jit(solution)/shard_map/ppermute | solution.py:265
  14.8 3.5 %collective-permute-start.3 = (f32[24,2048]{1,0:T(8,128)S(1)}, f32[24,2048]{1,0:T(8,128)S(1)}, u32[]{:S(2)}, u32[]{:S(2)}) collective-permute-start(f32[24,2048]{1,0:T(8,128)S(1)} %get-tuple-element.15), channel_id=1, source_target_pairs={{32,0},{0,32},{96,64},{64,96},{160,128},{128,160},{224,192},{192,2... | collective-permute-start | bytes 589832 | tf_op jit(solution)/shard_map/ppermute | solution.py:266
  20.4 33.1 %all-to-all-start = ((bf16[64,104,128]{2,1,0:T(8,128)(2,1)}), bf16[64,104,128]{2,1,0:T(8,128)(2,1)S(1)}, u32[]{:S(2)}, u32[]{:S(2)}) async-start(bf16[64,104,128]{2,1,0:T(8,128)(2,1)} %last_products.1), calls=%async_computation | async-start | bytes 3407872 | tf_op jit(solution)/shard_map/all_to_all | solution.py:23
  38.7 1.1 copy-start.1
  53.5 28.8 %all-to-all-start.1 = ((bf16[64,96,128]{2,1,0:T(8,128)(2,1)}), bf16[64,96,128]{2,1,0:T(8,128)(2,1)S(1)}, u32[]{:S(2)}, u32[]{:S(2)}) async-start(bf16[64,96,128]{2,1,0:T(8,128)(2,1)} %copy-done.1), calls=%async_computation.1 | async-start | bytes 3145728 | tf_op jit(solution)/shard_map/all_to_all | solution.py:23
  62.3 0.8 copy-start
